TPU v7x, 32 devices: a whole 2x2x4 slice. The times are simulated.
32 devices in a mesh: fsdp: 8 (over y, x, core), rep: 4 (over z).
Axes of the slice: x: 2, y: 2, z: 4, core: 2. Of those that a mesh axis runs over, the one named last changes fastest.
Arguments:
- images: bfloat16 [2, 32, 256, 768], P(None, ('fsdp', 'rep')), may hold values from -6 to 6
- cotangent: bfloat16 [2, 32, 256, 768], P(None, ('fsdp', 'rep')), may hold values from -6 to 6
- slot_flags: int32 [2, 32], P(None, ('fsdp', 'rep')), may hold values 0 or 1
- heads_weight: bfloat16 [2, 3, 768, 768], P(None, None, 'fsdp'), may hold values from -0.21875 to 0.21875
- heads_bias: bfloat16 [2, 2, 768], P(None, None, 'fsdp'), may hold values from -4 to 4
- merge_weight: bfloat16 [2, 768, 768], P(None, 'fsdp'), may hold values from -1.75 to 1.75
- merge_bias: bfloat16 [2, 768], P(None, 'fsdp'), may hold values from -4 to 4
- first_gain: bfloat16 [2, 768], P(None, 'fsdp'), may hold values from 0.5 to 1.5
- first_shift: bfloat16 [2, 768], P(None, 'fsdp'), may hold values from -4 to 4
- second_gain: bfloat16 [2, 768], P(None, 'fsdp'), may hold values from 0.5 to 1.5
- second_shift: bfloat16 [2, 768], P(None, 'fsdp'), may hold values from -4 to 4
- expand_weight: bfloat16 [2, 3072, 768], P(None, 'fsdp'), may hold values from -0.21875 to 0.21875
- expand_bias: bfloat16 [2, 3072], P(None, 'fsdp'), may hold values from -6 to 6
- reduce_weight: bfloat16 [2, 768, 3072], P(None, 'fsdp'), may hold values from -0.15625 to 0.15625
- reduce_bias: bfloat16 [2, 768], P(None, 'fsdp'), may hold values from -4 to 4
Outputs:
- outputs: bfloat16 [2, 32, 256, 768], P(None, ('fsdp', 'rep'))
- images_grad: bfloat16 [2, 32, 256, 768], P(None, ('fsdp', 'rep'))
- heads_weight_grad: float32 [2, 3, 768, 768], P(None, None, 'fsdp')
- heads_bias_grad: float32 [2, 2, 768], P(None, None, 'fsdp')
- merge_weight_grad: float32 [2, 768, 768], P(None, 'fsdp')
- merge_bias_grad: float32 [2, 768], P(None, 'fsdp')
- first_gain_grad: float32 [2, 768], P(None, 'fsdp')
- first_shift_grad: float32 [2, 768], P(None, 'fsdp')
- second_gain_grad: float32 [2, 768], P(None, 'fsdp')
- second_shift_grad: float32 [2, 768], P(None, 'fsdp')
- expand_weight_grad: float32 [2, 3072, 768], P(None, 'fsdp')
- expand_bias_grad: float32 [2, 3072], P(None, 'fsdp')
- reduce_weight_grad: float32 [2, 768, 3072], P(None, 'fsdp')
- reduce_bias_grad: float32 [2, 768], P(None, 'fsdp')
Inputs may be any that keep to these rules, and one draw needn't show every extreme that they name: `slot_flags`: 1 marks a slot that holds an image, 0 an empty slot.
All inputs are finite; a program needn't handle non-finite values. No bound on the sum of `slot_flags` on one device may be relied on, other than what follows from the above.
Results may differ from a plain program's by a relative error of at most 0.017.
Values may be sent and summed in bfloat16 or wider, within the bound.
No kernel may reach another device: no remote copies, remote signals or barrier semaphores. Data moves between devices by JAX's collectives and lax.ppermute only.
A program may use at most 256 MiB of HBM per device.

v0:
```python
import jax
import jax.numpy as jnp
from jax import lax
from jax.sharding import PartitionSpec as P

HEADS = 12
HEAD_DIM = 64


norm_eps = 1e-06


def layer_norm(token_rows, scale_row, offset_row):
    centre = token_rows - jnp.mean(token_rows, axis=-1, keepdims=True)
    spread = jnp.mean(centre * centre, axis=-1, keepdims=True)
    return centre * lax.rsqrt(spread + norm_eps) * scale_row + offset_row


def project(token_rows, weight):
    return lax.dot_general(
        token_rows, weight, (((1,), (1,)), ((), ())), preferred_element_type=jnp.float32
    )


def outer_sum(grad_rows, token_rows):
    return lax.dot_general(
        grad_rows, token_rows, (((0,), (0,)), ((), ())), preferred_element_type=jnp.float32
    )


def carry_back(grad_rows, weight):
    return jnp.dot(grad_rows, weight, preferred_element_type=jnp.float32)


def forward_layer(hidden, params):
    (
        heads_weight,
        heads_bias,
        merge_weight,
        merge_bias,
        first_gain,
        first_shift,
        second_gain,
        second_shift,
        expand_weight,
        expand_bias,
        reduce_weight,
        reduce_bias,
    ) = params
    seq_len, model_width = hidden.shape
    shaped = (seq_len, HEADS, HEAD_DIM)
    score_scale = HEAD_DIM ** (-0.5)
    normed = layer_norm(
        hidden, first_gain.astype(jnp.float32), first_shift.astype(jnp.float32)
    ).astype(jnp.bfloat16)
    queries = (project(normed, heads_weight[0]) + heads_bias[0].astype(jnp.float32)).astype(
        jnp.bfloat16
    )
    key_rows = project(normed, heads_weight[1]).astype(jnp.bfloat16)
    values = (project(normed, heads_weight[2]) + heads_bias[1].astype(jnp.float32)).astype(
        jnp.bfloat16
    )
    scores = (
        jnp.einsum(
            "qhd,khd->hqk",
            queries.reshape(shaped),
            key_rows.reshape(shaped),
            preferred_element_type=jnp.float32,
        )
        * score_scale
    )
    row_peak = jnp.max(scores, axis=-1, keepdims=True)
    exponent = jnp.exp(scores - row_peak)
    row_total = jnp.sum(exponent, axis=-1, keepdims=True)
    attend = exponent / row_total
    log_total = row_peak + jnp.log(row_total)
    mixed_rows = jnp.einsum(
        "hqk,khd->qhd",
        attend.astype(jnp.bfloat16),
        values.reshape(shaped),
        preferred_element_type=jnp.float32,
    )
    mixed_rows = mixed_rows.reshape(seq_len, model_width).astype(jnp.bfloat16)
    middle = hidden + (project(mixed_rows, merge_weight) + merge_bias.astype(jnp.float32))
    second = layer_norm(
        middle, second_gain.astype(jnp.float32), second_shift.astype(jnp.float32)
    ).astype(jnp.bfloat16)
    pre_act = project(second, expand_weight) + expand_bias.astype(jnp.float32)
    activated = jax.nn.gelu(pre_act, approximate=True).astype(jnp.bfloat16)
    result = middle + (project(activated, reduce_weight) + reduce_bias.astype(jnp.float32))
    saved = (
        hidden,
        normed,
        queries,
        key_rows,
        values,
        log_total,
        mixed_rows,
        middle,
        second,
        pre_act,
        activated,
    )
    return (result, saved)


def backward_layer(grad_out, params, saved):
    (
        heads_weight,
        heads_bias,
        merge_weight,
        merge_bias,
        first_gain,
        first_shift,
        second_gain,
        second_shift,
        expand_weight,
        expand_bias,
        reduce_weight,
        reduce_bias,
    ) = params
    (
        hidden,
        normed,
        queries,
        key_rows,
        values,
        log_total,
        mixed_rows,
        middle,
        second,
        pre_act,
        activated,
    ) = saved
    seq_len, model_width = hidden.shape
    shaped = (seq_len, HEADS, HEAD_DIM)
    score_scale = HEAD_DIM ** (-0.5)
    branch_low = grad_out.astype(jnp.bfloat16)
    reduce_weight_term = outer_sum(branch_low, activated)
    reduce_bias_term = jnp.sum(branch_low.astype(jnp.float32), axis=0)
    grad_act = carry_back(branch_low, reduce_weight)
    unused_value, gelu_back = jax.vjp(lambda point: jax.nn.gelu(point, approximate=True), pre_act)
    grad_pre = gelu_back(grad_act)[0].astype(jnp.bfloat16)
    expand_weight_term = outer_sum(grad_pre, second)
    expand_bias_term = jnp.sum(grad_pre.astype(jnp.float32), axis=0)
    grad_second = carry_back(grad_pre, expand_weight)
    unused_norm, second_back = jax.vjp(
        layer_norm, middle, second_gain.astype(jnp.float32), second_shift.astype(jnp.float32)
    )
    middle_part, second_gain_term, second_shift_term = second_back(grad_second)
    grad_middle = grad_out + middle_part
    attn_low = grad_middle.astype(jnp.bfloat16)
    merge_weight_term = outer_sum(attn_low, mixed_rows)
    merge_bias_term = jnp.sum(attn_low.astype(jnp.float32), axis=0)
    grad_mixed = carry_back(attn_low, merge_weight).astype(jnp.bfloat16).reshape(shaped)
    queries_heads = queries.reshape(shaped)
    keys_heads = key_rows.reshape(shaped)
    values_heads = values.reshape(shaped)
    scores = (
        jnp.einsum("qhd,khd->hqk", queries_heads, keys_heads, preferred_element_type=jnp.float32)
        * score_scale
    )
    attend = jnp.exp(scores - log_total)
    grad_values = jnp.einsum(
        "hqk,qhd->khd", attend.astype(jnp.bfloat16), grad_mixed, preferred_element_type=jnp.float32
    ).astype(jnp.bfloat16)
    grad_attend = jnp.einsum(
        "qhd,khd->hqk", grad_mixed, values_heads, preferred_element_type=jnp.float32
    )
    grad_scores = attend * (grad_attend - jnp.sum(grad_attend * attend, axis=-1, keepdims=True))
    grad_scores = grad_scores.astype(jnp.bfloat16)
    grad_queries = (
        jnp.einsum("hqk,khd->qhd", grad_scores, keys_heads, preferred_element_type=jnp.float32)
        * score_scale
    ).astype(jnp.bfloat16)
    grad_keys = (
        jnp.einsum("hqk,qhd->khd", grad_scores, queries_heads, preferred_element_type=jnp.float32)
        * score_scale
    ).astype(jnp.bfloat16)
    stacked_grads = jnp.stack(
        [
            grad_queries.reshape(seq_len, model_width),
            grad_keys.reshape(seq_len, model_width),
            grad_values.reshape(seq_len, model_width),
        ]
    )
    heads_weight_term = jnp.einsum(
        "jto,ti->joi", stacked_grads, normed, preferred_element_type=jnp.float32
    )
    grad_normed = jnp.einsum(
        "jto,joi->ti", stacked_grads, heads_weight, preferred_element_type=jnp.float32
    )
    heads_bias_term = jnp.stack(
        [
            jnp.sum(stacked_grads[0].astype(jnp.float32), axis=0),
            jnp.sum(stacked_grads[2].astype(jnp.float32), axis=0),
        ]
    )
    unused_first, first_back = jax.vjp(
        layer_norm, hidden, first_gain.astype(jnp.float32), first_shift.astype(jnp.float32)
    )
    hidden_part, first_gain_term, first_shift_term = first_back(grad_normed)
    grad_hidden = grad_middle + hidden_part
    terms = (
        heads_weight_term,
        heads_bias_term,
        merge_weight_term,
        merge_bias_term,
        first_gain_term,
        first_shift_term,
        second_gain_term,
        second_shift_term,
        expand_weight_term,
        expand_bias_term,
        reduce_weight_term,
        reduce_bias_term,
    )
    return (grad_hidden, terms)


def shards(
    images,
    cotangent,
    slot_flags,
    heads_weight,
    heads_bias,
    merge_weight,
    merge_bias,
    first_gain,
    first_shift,
    second_gain,
    second_shift,
    expand_weight,
    expand_bias,
    reduce_weight,
    reduce_bias,
):
    micro_count = images.shape[0]
    seq_len = images.shape[2]
    layers = heads_weight.shape[0]
    live_flags = slot_flags.astype(jnp.float32)
    states = [images[batch_at, 0].astype(jnp.float32) for batch_at in range(micro_count)]
    saved_all = []
    for layer_at in range(layers):
        saved_row = []
        for batch_at in range(micro_count):
            params = (
                lax.all_gather(heads_weight[layer_at], "fsdp", axis=1, tiled=True),
                lax.all_gather(heads_bias[layer_at], "fsdp", axis=1, tiled=True),
                lax.all_gather(merge_weight[layer_at], "fsdp", axis=0, tiled=True),
                lax.all_gather(merge_bias[layer_at], "fsdp", axis=0, tiled=True),
                lax.all_gather(first_gain[layer_at], "fsdp", axis=0, tiled=True),
                lax.all_gather(first_shift[layer_at], "fsdp", axis=0, tiled=True),
                lax.all_gather(second_gain[layer_at], "fsdp", axis=0, tiled=True),
                lax.all_gather(second_shift[layer_at], "fsdp", axis=0, tiled=True),
                lax.all_gather(expand_weight[layer_at], "fsdp", axis=0, tiled=True),
                lax.all_gather(expand_bias[layer_at], "fsdp", axis=0, tiled=True),
                lax.all_gather(reduce_weight[layer_at], "fsdp", axis=0, tiled=True),
                lax.all_gather(reduce_bias[layer_at], "fsdp", axis=0, tiled=True),
            )
            states[batch_at], saved = forward_layer(states[batch_at], params)
            saved_row.append(saved)
        saved_all.append(saved_row)
    outputs = jnp.stack(
        [live_flags[batch_at, 0] * states[batch_at] for batch_at in range(micro_count)]
    )[:, None].astype(jnp.bfloat16)
    grads_back = [
        cotangent[batch_at, 0].astype(jnp.float32) * live_flags[batch_at, 0]
        for batch_at in range(micro_count)
    ]
    collected = [None] * layers
    for layer_at in reversed(range(layers)):
        totals = None
        for batch_at in range(micro_count):
            params = (
                lax.all_gather(heads_weight[layer_at], "fsdp", axis=1, tiled=True),
                lax.all_gather(heads_bias[layer_at], "fsdp", axis=1, tiled=True),
                lax.all_gather(merge_weight[layer_at], "fsdp", axis=0, tiled=True),
                lax.all_gather(merge_bias[layer_at], "fsdp", axis=0, tiled=True),
                lax.all_gather(first_gain[layer_at], "fsdp", axis=0, tiled=True),
                lax.all_gather(first_shift[layer_at], "fsdp", axis=0, tiled=True),
                lax.all_gather(second_gain[layer_at], "fsdp", axis=0, tiled=True),
                lax.all_gather(second_shift[layer_at], "fsdp", axis=0, tiled=True),
                lax.all_gather(expand_weight[layer_at], "fsdp", axis=0, tiled=True),
                lax.all_gather(expand_bias[layer_at], "fsdp", axis=0, tiled=True),
                lax.all_gather(reduce_weight[layer_at], "fsdp", axis=0, tiled=True),
                lax.all_gather(reduce_bias[layer_at], "fsdp", axis=0, tiled=True),
            )
            grads_back[batch_at], terms = backward_layer(
                grads_back[batch_at], params, saved_all[layer_at][batch_at]
            )
            if totals is None:
                totals = terms
            else:
                totals = tuple((earlier + current for earlier, current in zip(totals, terms)))
        collected[layer_at] = totals
    images_grad = jnp.stack(grads_back)[:, None].astype(jnp.bfloat16)
    stacked = [
        jnp.stack([collected[layer_at][member] for layer_at in range(layers)])
        for member in range(12)
    ]
    shares = (
        lax.psum_scatter(
            stacked[0].astype(jnp.bfloat16), "fsdp", scatter_dimension=2, tiled=True
        ).astype(jnp.float32),
        lax.psum_scatter(
            stacked[1].astype(jnp.bfloat16), "fsdp", scatter_dimension=2, tiled=True
        ).astype(jnp.float32),
        lax.psum_scatter(
            stacked[2].astype(jnp.bfloat16), "fsdp", scatter_dimension=1, tiled=True
        ).astype(jnp.float32),
        lax.psum_scatter(
            stacked[3].astype(jnp.bfloat16), "fsdp", scatter_dimension=1, tiled=True
        ).astype(jnp.float32),
        lax.psum_scatter(
            stacked[4].astype(jnp.bfloat16), "fsdp", scatter_dimension=1, tiled=True
        ).astype(jnp.float32),
        lax.psum_scatter(
            stacked[5].astype(jnp.bfloat16), "fsdp", scatter_dimension=1, tiled=True
        ).astype(jnp.float32),
        lax.psum_scatter(
            stacked[6].astype(jnp.bfloat16), "fsdp", scatter_dimension=1, tiled=True
        ).astype(jnp.float32),
        lax.psum_scatter(
            stacked[7].astype(jnp.bfloat16), "fsdp", scatter_dimension=1, tiled=True
        ).astype(jnp.float32),
        lax.psum_scatter(
            stacked[8].astype(jnp.bfloat16), "fsdp", scatter_dimension=1, tiled=True
        ).astype(jnp.float32),
        lax.psum_scatter(
            stacked[9].astype(jnp.bfloat16), "fsdp", scatter_dimension=1, tiled=True
        ).astype(jnp.float32),
        lax.psum_scatter(
            stacked[10].astype(jnp.bfloat16), "fsdp", scatter_dimension=1, tiled=True
        ).astype(jnp.float32),
        lax.psum_scatter(
            stacked[11].astype(jnp.bfloat16), "fsdp", scatter_dimension=1, tiled=True
        ).astype(jnp.float32),
    )
    reduced = (
        lax.psum(shares[0].astype(jnp.bfloat16), "rep").astype(jnp.float32),
        lax.psum(shares[1].astype(jnp.bfloat16), "rep").astype(jnp.float32),
        lax.psum(shares[2].astype(jnp.bfloat16), "rep").astype(jnp.float32),
        lax.psum(shares[3].astype(jnp.bfloat16), "rep").astype(jnp.float32),
        lax.psum(shares[4].astype(jnp.bfloat16), "rep").astype(jnp.float32),
        lax.psum(shares[5].astype(jnp.bfloat16), "rep").astype(jnp.float32),
        lax.psum(shares[6].astype(jnp.bfloat16), "rep").astype(jnp.float32),
        lax.psum(shares[7].astype(jnp.bfloat16), "rep").astype(jnp.float32),
        lax.psum(shares[8].astype(jnp.bfloat16), "rep").astype(jnp.float32),
        lax.psum(shares[9].astype(jnp.bfloat16), "rep").astype(jnp.float32),
        lax.psum(shares[10].astype(jnp.bfloat16), "rep").astype(jnp.float32),
        lax.psum(shares[11].astype(jnp.bfloat16), "rep").astype(jnp.float32),
    )
    grad_scale = (micro_count * lax.axis_size("fsdp") * lax.axis_size("rep") * seq_len) ** (-0.5)
    finals = tuple((member_sum * grad_scale for member_sum in reduced))
    return (outputs, images_grad) + finals


def solution(mesh):
    placed = (
        P(None, ("fsdp", "rep"), None, None),
        P(None, ("fsdp", "rep"), None, None),
        P(None, ("fsdp", "rep")),
        P(None, None, "fsdp", None),
        P(None, None, "fsdp"),
        P(None, "fsdp", None),
        P(None, "fsdp"),
        P(None, "fsdp"),
        P(None, "fsdp"),
        P(None, "fsdp"),
        P(None, "fsdp"),
        P(None, "fsdp", None),
        P(None, "fsdp"),
        P(None, "fsdp", None),
        P(None, "fsdp"),
    )
    return jax.shard_map(
        shards,
        mesh=mesh,
        in_specs=placed,
        out_specs=(
            P(None, ("fsdp", "rep"), None, None),
            P(None, ("fsdp", "rep"), None, None),
            P(None, None, "fsdp", None),
            P(None, None, "fsdp"),
            P(None, "fsdp", None),
            P(None, "fsdp"),
            P(None, "fsdp"),
            P(None, "fsdp"),
            P(None, "fsdp"),
            P(None, "fsdp"),
            P(None, "fsdp", None),
            P(None, "fsdp"),
            P(None, "fsdp", None),
            P(None, "fsdp"),
        ),
        check_vma=False,
    )
```

profile of v0, /device:TPU:0, one launch (start us, length us, event | category | flops | bytes accessed | tf_op | source)
XLA Modules:
  0.0 1141.6 jit_solution(11297764659703963821)
XLA Ops:
  21.0 26.5 %all-reduce.12 = (bf16[768]{0:T(1024)(128)(2,1)S(1)}, bf16[768]{0:T(1024)(128)(2,1)S(1)}, bf16[768]{0:T(1024)(128)(2,1)S(1)}, bf16[768]{0:T(1024)(128)(2,1)S(1)}...) all-reduce(bf16[768]{0:T(1024)(128)(2,1)S(1)} %dynamic-update-slice, ...), channel_id=3, replica_groups=mesh['fsdp'=8,'rep'=4] {'fsdp'}, use_global_device_ids=true, to_apply=%add.1 | all-reduce | flops 9216 | bytes 36864
  53.4 7.5 all-gather.21
  61.5 9.3 all-gather.9
  71.7 8.4 all-gather.3
  84.8 10.5 all-gather.15
  95.3 5.3 fusion.266
  125.5 6.0 fusion.36
  131.6 26.2 %all-gather.39.cloned.1.call-done = bf16[1,768,3072]{2,1,0:T(8,128)(2,1)} async-done(((bf16[1,96,3072]{2,1,0:T(8,128)(2,1)}), bf16[1,768,3072]{2,1,0:T(8,128)(2,1)}) %all-gather.39.cloned.1.call-update) | async-done | bytes 4718608 | tf_op jit(solution)/shard_map/all_gather | solution.py:258
  157.7 5.7 fusion.345
  171.4 22.6 %all-gather.41.cloned.1.call-done = bf16[1,3,768,768]{3,2,1,0:T(8,128)(2,1)} async-done(((bf16[1,3,96,768]{3,2,1,0:T(8,128)(2,1)}), bf16[1,3,768,768]{3,2,1,0:T(8,128)(2,1)}) %all-gather.41.cloned.1.call-update) | async-done | bytes 3538960 | tf_op jit(solution)/shard_map/all_gather | solution.py:248
  235.3 26.0 %all-gather.45.cloned.1.call-done = bf16[1,3072,768]{2,1,0:T(8,128)(2,1)} async-done(((bf16[1,384,768]{2,1,0:T(8,128)(2,1)}), bf16[1,3072,768]{2,1,0:T(8,128)(2,1)}) %all-gather.45.cloned.1.call-update) | async-done | bytes 4718608 | tf_op jit(solution)/shard_map/all_gather | solution.py:256
  261.3 5.8 fusion.45
  270.3 32.4 %all-gather.47.cloned.1.call-done = bf16[1,768,3072]{2,1,0:T(8,128)(2,1)} async-done(((bf16[1,96,3072]{2,1,0:T(8,128)(2,1)}), bf16[1,768,3072]{2,1,0:T(8,128)(2,1)}) %all-gather.47.cloned.1.call-update) | async-done | bytes 4718608 | tf_op jit(solution)/shard_map/all_gather | solution.py:258
  302.7 8.1 convert_reduce_fusion.1
  449.9 7.1 fusion.35
  460.5 8.4 pad_maximum_fusion.1
  482.9 8.4 pad_maximum_fusion
  516.6 5.9 fusion.211
  522.5 11.1 reduce-scatter.29.cloned.1.call-done
  533.6 80.0 %reduce-scatter.35.cloned.1.call-done = bf16[2,96,3072]{2,1,0:T(8,128)(2,1)} async-done(((bf16[2,768,3072]{2,1,0:T(8,128)(2,1)}), bf16[2,96,3072]{2,1,0:T(8,128)(2,1)}) %reduce-scatter.35.cloned.1.call-update) | async-done | bytes 1179664 | tf_op jit(solution)/shard_map/reduce_scatter | solution.py:333
  613.6 79.9 %reduce-scatter.33.cloned.1.call-done = bf16[2,384,768]{2,1,0:T(8,128)(2,1)} async-done(((bf16[2,3072,768]{2,1,0:T(8,128)(2,1)}), bf16[2,384,768]{2,1,0:T(8,128)(2,1)}) %reduce-scatter.33.cloned.1.call-update) | async-done | bytes 1179664 | tf_op jit(solution)/shard_map/reduce_scatter | solution.py:327
  693.7 6.4 fusion.208
  702.9 27.2 %reduce-scatter.51.cloned.1.call-done = bf16[96,2]{1,0:T(8,128)(2,1)} async-done(((bf16[768,2]{1,0:T(8,128)(2,1)}), bf16[96,2]{1,0:T(8,128)(2,1)}) %reduce-scatter.51.cloned.1.call-update) | async-done | bytes 400
  730.9 35.9 %reduce-scatter.47.cloned.1.call-done = bf16[96,2]{1,0:T(8,128)(2,1)} async-done(((bf16[768,2]{1,0:T(8,128)(2,1)}), bf16[96,2]{1,0:T(8,128)(2,1)}) %reduce-scatter.47.cloned.1.call-update) | async-done | bytes 400
  767.6 35.6 %reduce-scatter.45.cloned.1.call-done = bf16[96,2]{1,0:T(8,128)(2,1)} async-done(((bf16[768,2]{1,0:T(8,128)(2,1)}), bf16[96,2]{1,0:T(8,128)(2,1)}) %reduce-scatter.45.cloned.1.call-update) | async-done | bytes 400
  804.0 35.9 %reduce-scatter.39.cloned.1.call-done = bf16[96,2]{1,0:T(8,128)(2,1)} async-done(((bf16[768,2]{1,0:T(8,128)(2,1)}), bf16[96,2]{1,0:T(8,128)(2,1)}) %reduce-scatter.39.cloned.1.call-update) | async-done | bytes 400
  840.7 35.6 %reduce-scatter.41.cloned.1.call-done = bf16[96,2]{1,0:T(8,128)(2,1)} async-done(((bf16[768,2]{1,0:T(8,128)(2,1)}), bf16[96,2]{1,0:T(8,128)(2,1)}) %reduce-scatter.41.cloned.1.call-update) | async-done | bytes 400
  877.1 35.9 %reduce-scatter.43.cloned.1.call-done = bf16[96,2]{1,0:T(8,128)(2,1)} async-done(((bf16[768,2]{1,0:T(8,128)(2,1)}), bf16[96,2]{1,0:T(8,128)(2,1)}) %reduce-scatter.43.cloned.1.call-update) | async-done | bytes 400
  913.8 36.3 %reduce-scatter.37.cloned.1.call-done = bf16[96,4]{1,0:T(8,128)(2,1)} async-done(((bf16[768,4]{1,0:T(8,128)(2,1)}), bf16[96,4]{1,0:T(8,128)(2,1)}) %reduce-scatter.37.cloned.1.call-update) | async-done | bytes 784
  951.0 38.0 %reduce-scatter.49.cloned.1.call-done = bf16[384,2]{1,0:T(8,128)(2,1)} async-done(((bf16[3072,2]{1,0:T(8,128)(2,1)}), bf16[384,2]{1,0:T(8,128)(2,1)}) %reduce-scatter.49.cloned.1.call-update) | async-done | bytes 1552
  990.0 12.0 %all-reduce.13 = (bf16[2,2,96]{2,1,0:T(2,128)(2,1)S(1)}, bf16[2,96]{1,0:T(2,128)(2,1)S(1)}, bf16[2,96]{1,0:T(2,128)(2,1)S(1)}, bf16[2,96]{1,0:T(2,128)(2,1)S(1)}...) all-reduce(bf16[2,2,96]{2,1,0:T(2,128)(2,1)S(1)} %copy.262, ...), channel_id=1, replica_groups=mesh['fsdp'=8,'rep'=4] {'rep'}, use_global_device_ids=true, to_apply=%region_55.0 | all-reduce | flops 2304 | bytes 9216 | tf_op jit(solution)/shard_map/psum | solution.py:342
  1006.6 120.1 %all-reduce.17.cloned.1.call-done = (bf16[2,3,96,768]{3,2,1,0:T(8,128)(2,1)}, bf16[2,96,768]{2,1,0:T(8,128)(2,1)}, bf16[2,384,768]{2,1,0:T(8,128)(2,1)}, bf16[2,96,3072]{2,1,0:T(8,128)(2,1)}) async-done(((bf16[2,3,96,768]{3,2,1,0:T(8,128)(2,1)}, bf16[2,96,768]{2,1,0:T(8,128)(2,1)}, bf16[2,384,768]{2,1,0:T(8,128)(2,1)}, bf16[2,96,3072]{2,1,0:T(8,128)(2,1)}), (bf16[2,3,96,768]{3,2,1,0:T(8,128)(2,1)}, ...) | async-done | bytes 3538960 | tf_op jit(solution)/shard_map/psum | solution.py:341
  (906 shorter events, 302.7 us)
Async XLA Ops:
  7.2 93.5 %all-gather.33.cloned.1.call-start = ((), (), s32[]{:S(2)}) async-start(), calls=%async_computation.16 | async-start | bytes 3981312 | tf_op jit(solution)/shard_map/all_gather | solution.py:248
  9.5 108.4 %all-gather.35.cloned.1.call-start = ((), (), s32[]{:S(2)}) async-start(), calls=%async_computation.17 | async-start | bytes 1327104 | tf_op jit(solution)/shard_map/all_gather | solution.py:250
  11.3 114.1 %all-gather.37.cloned.1.call-start = ((), (), s32[]{:S(2)}) async-start(), calls=%async_computation.18 | async-start | bytes 5308416 | tf_op jit(solution)/shard_map/all_gather | solution.py:256
  12.6 145.1 %all-gather.39.cloned.1.call-start = ((), (), s32[]{:S(2)}) async-start(), calls=%async_computation.19 | async-start | bytes 5308416 | tf_op jit(solution)/shard_map/all_gather | solution.py:258
  13.8 180.3 %all-gather.41.cloned.1.call-start = ((), (), s32[]{:S(2)}) async-start(), calls=%async_computation.20 | async-start | bytes 3981312 | tf_op jit(solution)/shard_map/all_gather | solution.py:248
  14.4 211.3 %all-gather.43.cloned.1.call-start = ((), (), s32[]{:S(2)}) async-start(), calls=%async_computation.21 | async-start | bytes 1327104 | tf_op jit(solution)/shard_map/all_gather | solution.py:250
  14.9 246.4 %all-gather.45.cloned.1.call-start = ((), (), s32[]{:S(2)}) async-start(), calls=%async_computation.22 | async-start | bytes 5308416 | tf_op jit(solution)/shard_map/all_gather | solution.py:256
  15.7 287.0 %all-gather.47.cloned.1.call-start = ((), (), s32[]{:S(2)}) async-start(), calls=%async_computation.23 | async-start | bytes 5308416 | tf_op jit(solution)/shard_map/all_gather | solution.py:258
  16.4 506.1 %reduce-scatter.31.cloned.1.call-start = ((), (), s32[]{:S(2)}) async-start(), calls=%async_computation.13 | async-start | bytes 2654208 | tf_op jit(solution)/shard_map/reduce_scatter | solution.py:309
  47.5 65.1 %copy-start.170 = (f32[768]{0:T(1024)}, f32[768]{0:T(1024)S(1)}, u32[]{:S(2)}) copy-start(f32[768]{0:T(1024)S(1)} %convert_element_type.701) | copy-start | bytes 9220
  47.7 60.0 %copy-start.158 = (f32[256]{0:T(256)}, f32[256]{0:T(256)S(1)}, u32[]{:S(2)}) copy-start(f32[256]{0:T(256)S(1)} %get-tuple-element.207) | copy-start | bytes 3076
  47.7 64.9 %copy-start.166 = (f32[256]{0:T(256)}, f32[256]{0:T(256)S(1)}, u32[]{:S(2)}) copy-start(f32[256]{0:T(256)S(1)} %get-tuple-element.208) | copy-start | bytes 3076
  48.6 64.0 %copy-start.210 = (f32[256]{0:T(256)}, f32[256]{0:T(256)S(1)}, u32[]{:S(2)}) copy-start(f32[256]{0:T(256)S(1)} %fusion.287) | copy-start | bytes 3076
  48.6 59.0 %copy-start.162 = (f32[256]{0:T(256)}, f32[256]{0:T(256)S(1)}, u32[]{:S(2)}) copy-start(f32[256]{0:T(256)S(1)} %fusion.291) | copy-start | bytes 3076
  48.6 64.0 %copy-start.132 = (f32[768]{0:T(1024)}, f32[768]{0:T(1024)S(1)}, u32[]{:S(2)}) copy-start(f32[768]{0:T(1024)S(1)} %convert_element_type.700) | copy-start | bytes 9220
  51.6 66.3 %copy-start.142 = (f32[768]{0:T(1024)}, f32[768]{0:T(1024)S(1)}, u32[]{:S(2)}) copy-start(f32[768]{0:T(1024)S(1)} %convert_element_type.702) | copy-start | bytes 9220
  232.9 89.2 %copy-start.189 = (f32[256]{0:T(256)}, f32[256]{0:T(256)S(1)}, u32[]{:S(2)}) copy-start(f32[256]{0:T(256)S(1)} %broadcast_multiply_fusion.4) | copy-start | bytes 3076
  234.0 88.1 %copy-start.237 = (f32[256]{0:T(256)}, f32[256]{0:T(256)S(1)}, u32[]{:S(2)}) copy-start(f32[256]{0:T(256)S(1)} %fusion.294) | copy-start | bytes 3076
  234.1 88.1 %copy-start.239 = (f32[256]{0:T(256)}, f32[256]{0:T(256)S(1)}, u32[]{:S(2)}) copy-start(f32[256]{0:T(256)S(1)} %fusion.290) | copy-start | bytes 3076
  421.7 112.0 %reduce-scatter.29.cloned.1.call-start = ((), (), s32[]{:S(2)}) async-start(), calls=%async_computation.12 | async-start | bytes 7962624 | tf_op jit(solution)/shard_map/reduce_scatter | solution.py:303
  442.7 170.9 %reduce-scatter.35.cloned.1.call-start = ((), (), s32[]{:S(2)}) async-start(), calls=%async_computation.15 | async-start | bytes 10616832 | tf_op jit(solution)/shard_map/reduce_scatter | solution.py:333
  469.0 224.5 %reduce-scatter.33.cloned.1.call-start = ((), (), s32[]{:S(2)}) async-start(), calls=%async_computation.14 | async-start | bytes 10616832 | tf_op jit(solution)/shard_map/reduce_scatter | solution.py:327
  491.3 238.7 %reduce-scatter.51.cloned.1.call-start = ((), (), s32[]{:S(2)}) async-start(), calls=%async_computation.31 | async-start | bytes 221184
  502.6 264.2 %reduce-scatter.47.cloned.1.call-start = ((), (), s32[]{:S(2)}) async-start(), calls=%async_computation.29 | async-start | bytes 221184
  503.6 299.5 %reduce-scatter.45.cloned.1.call-start = ((), (), s32[]{:S(2)}) async-start(), calls=%async_computation.28 | async-start | bytes 221184
  504.6 335.2 %reduce-scatter.39.cloned.1.call-start = ((), (), s32[]{:S(2)}) async-start(), calls=%async_computation.25 | async-start | bytes 221184
  508.3 367.9 %reduce-scatter.41.cloned.1.call-start = ((), (), s32[]{:S(2)}) async-start(), calls=%async_computation.26 | async-start | bytes 221184
  509.3 403.6 %reduce-scatter.43.cloned.1.call-start = ((), (), s32[]{:S(2)}) async-start(), calls=%async_computation.27 | async-start | bytes 221184
  510.9 439.2 %reduce-scatter.37.cloned.1.call-start = ((), (), s32[]{:S(2)}) async-start(), calls=%async_computation.24 | async-start | bytes 221184
  514.5 474.6 %reduce-scatter.49.cloned.1.call-start = ((), (), s32[]{:S(2)}) async-start(), calls=%async_computation.30 | async-start | bytes 884736
  516.5 610.2 %all-reduce.17.cloned.1.call-start = ((), (), s32[]{:S(2)}) async-start(), calls=%async_computation.32 | async-start | bytes 7077888 | tf_op jit(solution)/shard_map/psum | solution.py:341
  522.5 171.1 %copy-start.248 = (f32[768]{0:T(1024)S(1)}, f32[768]{0:T(1024)}, u32[]{:S(2)}) copy-start(f32[768]{0:T(1024)} %convert_element_type.711) | copy-start | bytes 9220
  (268 other events, 1291.7 us)
Sparse Core Ops, SparseCore 0:
  10.5 36.8 all-gather.32
  49.3 24.1 all-gather.34
  76.0 40.4 all-gather.36
  118.7 38.9 all-gather.38
  160.0 33.9 all-gather.40
  195.8 24.0 all-gather.42
  222.3 38.9 all-gather.44
  263.8 38.9 all-gather.46
  421.8 42.4 reduce-scatter.30
  468.1 65.5 reduce-scatter.28
  537.1 76.4 reduce-scatter.34
  617.0 76.4 reduce-scatter.32
  696.6 33.4 reduce-scatter.50
  733.2 33.5 reduce-scatter.46
  769.7 33.4 reduce-scatter.44
  806.3 33.4 reduce-scatter.38
  842.7 33.5 reduce-scatter.40
  879.5 33.4 reduce-scatter.42
  916.6 33.4 reduce-scatter.36
  954.0 35.0 reduce-scatter.48
  991.9 134.7 all-reduce.16
where the time goes:
time: 1150 us; the launch traced here: 1140 us
  waiting for transfers between devices  681 us (59%)
  matrix products  201 us (17%)
  local copies, waits for them, and re-layouts  82.3 us (7%)
  other arithmetic  81.9 us (7%)
  blocking collectives  74.2 us (6%)
  between operations  18.8 us (2%)
    unnamed x29, waiting for transfers between devices  283 us
    psum x1, waiting for transfers between devices, shards(): lax.psum(shares[0].astype(jnp.bfloat16), 'rep').astype(jnp.float32)  120 us
    reduce_scatter x1, waiting for transfers between devices, shards(): lax.psum_scatter(stacked[10].astype(jnp.bfloat16), 'fsdp', scatter_dimens...  80 us
    reduce_scatter x1, waiting for transfers between devices, shards(): lax.psum_scatter(stacked[8].astype(jnp.bfloat16), 'fsdp', scatter_dimensi...  79.9 us
    dot_general x24, matrix products, project(): lax.dot_general(token_rows, weight, (((1,), (1,)), ((), ())), preferred_e...  69.3 us
    all_gather x2, waiting for transfers between devices, shards(): lax.all_gather(reduce_weight[layer_at], 'fsdp', axis=0, tiled=True)  58.6 us
    dot_general x12, matrix products, outer_sum(): lax.dot_general(grad_rows, token_rows, (((0,), (0,)), ((), ())), preferre...  36.9 us
    dot_general x12, matrix products, carry_back(): return jnp.dot(grad_rows, weight, preferred_element_type=jnp.float32)  35.7 us
  transfers between devices with their start and end apart: 21, of which 16 were waited for; matrix products, arithmetic and copies ran while one was open for 20% of the time, Pallas kernels for 0%

commit v1 on v0

--- a/solution.py
+++ b/solution.py
@@ -1,6 +1,8 @@
 import jax
 import jax.numpy as jnp
 from jax import lax
+from jax.experimental import pallas as pl
+from jax.experimental.pallas import tpu as pltpu
 from jax.sharding import PartitionSpec as P
 
 HEADS = 12
@@ -218,7 +220,7 @@
     return (grad_hidden, terms)
 
 
-def shards(
+def plain_shards(
     images,
     cotangent,
     slot_flags,
@@ -356,7 +358,960 @@
     return (outputs, images_grad) + finals
 
 
+ROWS = 256
+WIDTH = 768
+FF_PARTS = 4
+f32 = jnp.float32
+bf16 = jnp.bfloat16
+VMEM_BYTES = 56 * 1024 * 1024
+
+
+def dot_nt(left, right):
+    return lax.dot_general(left, right, (((1,), (1,)), ((), ())), preferred_element_type=f32)
+
+
+def dot_nn(left, right):
+    return lax.dot_general(left, right, (((1,), (0,)), ((), ())), preferred_element_type=f32)
+
+
+def swap_core(value):
+    return lax.ppermute(value, "fsdp", [(at, at ^ 1) for at in range(8)])
+
+
+def swap_x(value):
+    return lax.ppermute(value, "fsdp", [(at, at ^ 2) for at in range(8)])
+
+
+def swap_y(value):
+    return lax.ppermute(value, "fsdp", [(at, at ^ 4) for at in range(8)])
+
+
+def gather_pack(own, cut):
+    along_x = swap_x(own)
+    along_y = swap_y(own)
+    across_low = swap_x(along_y[:cut])
+    across_high = swap_y(along_x[cut:])
+    even = (own, along_x, along_y, across_low, across_high)
+    return even + tuple(swap_core(piece) for piece in even)
+
+
+def piece_plan(cut, first, count):
+    plan = []
+    for odd in range(2):
+        for place, delta in ((0, 0), (1, 2), (2, 4)):
+            plan.append((5 * odd + place, first, count, delta ^ odd, 0))
+        low = min(max(cut - first, 0), count)
+        if low > 0:
+            plan.append((5 * odd + 3, first, low, 6 ^ odd, 0))
+        if low < count:
+            plan.append((5 * odd + 4, first + low - cut, count - low, 6 ^ odd, low))
+    return plan
+
+
+def block_copies(place, refs, plan, block, sems):
+    return [
+        pltpu.make_async_copy(
+            refs[array_at].at[pl.ds(row, count)],
+            block.at[place ^ delta, pl.ds(into, count)],
+            sems.at[at],
+        )
+        for at, (array_at, row, count, delta, into) in enumerate(plan)
+    ]
+
+
+def run_all(copies, what):
+    for copy in copies:
+        getattr(copy, what)()
+
+
+def in_any():
+    return pl.BlockSpec(memory_space=pl.ANY)
+
+
+def in_smem():
+    return pl.BlockSpec(memory_space=pltpu.SMEM)
+
+
+def params(steps=1):
+    return pltpu.CompilerParams(
+        dimension_semantics=("arbitrary",) * steps, vmem_limit_bytes=VMEM_BYTES
+    )
+
+
+def cost(flops, moved):
+    return pl.CostEstimate(flops=int(flops), bytes_accessed=int(moved), transcendentals=0)
+
+
+def rows_spec(width):
+    return pl.BlockSpec((ROWS, width), lambda image: (image, 0))
+
+
+def fixed(shape):
+    return pl.BlockSpec(shape, lambda image: (0,) * len(shape))
+
+
+def normalise(rows):
+    centre = rows - jnp.mean(rows, axis=-1, keepdims=True)
+    root = lax.rsqrt(jnp.mean(centre * centre, axis=-1, keepdims=True) + norm_eps)
+    return centre * root, root
+
+
+SM_HB0, SM_HB1, SM_MB, SM_G1, SM_S1, SM_G2, SM_S2, SM_RB = range(8)
+
+
+def attn_forward(place, hidden, small, pack, cut):
+    plans = [piece_plan(cut, 96 * at, 96) for at in range(4)]
+    copies_in_all = sum(len(plan) for plan in plans)
+
+    def kernel(place_ref, hidden_ref, small_ref, *rest):
+        packs = rest[:10]
+        middle_ref, normed_ref, qkv_ref, mixed_ref, blocks, sems = rest[10:]
+        place_now = place_ref[0]
+        image = pl.program_id(0)
+        copies = []
+        at = 0
+        for member, plan in enumerate(plans):
+            copies.append(
+                block_copies(
+                    place_now, packs, plan, blocks.at[member], sems.at[pl.ds(at, len(plan))]
+                )
+            )
+            at += len(plan)
+
+        @pl.when(image == 0)
+        def begin():
+            for group in copies:
+                run_all(group, "start")
+
+        rows = hidden_ref[...].astype(f32)
+        unit, root = normalise(rows)
+        normed = (unit * small_ref[SM_G1 : SM_G1 + 1] + small_ref[SM_S1 : SM_S1 + 1]).astype(bf16)
+        normed_ref[...] = normed
+
+        @pl.when(image == 0)
+        def arrive():
+            for group in copies:
+                run_all(group, "wait")
+
+        for member, bias in ((0, SM_HB0), (1, None), (2, SM_HB1)):
+            block = blocks[member].reshape(WIDTH, WIDTH)
+            made = dot_nt(normed, block)
+            if bias is not None:
+                made = made + small_ref[bias : bias + 1]
+            qkv_ref[:, WIDTH * member : WIDTH * (member + 1)] = made.astype(bf16)
+        lane = lax.broadcasted_iota(jnp.int32, (ROWS, 128), 1)
+        for pair in range(HEADS // 2):
+            q_pair = qkv_ref[:, 128 * pair : 128 * pair + 128]
+            k_pair = qkv_ref[:, WIDTH + 128 * pair : WIDTH + 128 * pair + 128]
+            v_pair = qkv_ref[:, 2 * WIDTH + 128 * pair : 2 * WIDTH + 128 * pair + 128]
+            parts = []
+            for half in range(2):
+                q_one = jnp.where((lane < 64) == (half == 0), q_pair, jnp.zeros_like(q_pair))
+                scores = dot_nt(q_one, k_pair) * (HEAD_DIM**-0.5)
+                peak = jnp.max(scores, axis=-1, keepdims=True)
+                powers = jnp.exp(scores - peak)
+                total = jnp.sum(powers, axis=-1, keepdims=True)
+                attend = (powers / total).astype(bf16)
+                parts.append(dot_nn(attend, v_pair))
+            mixed_ref[:, 128 * pair : 128 * pair + 128] = jnp.where(
+                lane < 64, parts[0], parts[1]
+            ).astype(bf16)
+        merged = dot_nt(mixed_ref[...], blocks[3].reshape(WIDTH, WIDTH))
+        middle_ref[...] = rows + (merged + small_ref[SM_MB : SM_MB + 1])
+
+    tokens = hidden.shape[0]
+    shape = jax.ShapeDtypeStruct
+    return pl.pallas_call(
+        kernel,
+        grid=(tokens // ROWS,),
+        in_specs=[in_smem(), rows_spec(WIDTH), fixed(small.shape)] + [in_any()] * 10,
+        out_specs=[rows_spec(WIDTH), rows_spec(WIDTH), rows_spec(3 * WIDTH), rows_spec(WIDTH)],
+        out_shape=[
+            shape((tokens, WIDTH), f32),
+            shape((tokens, WIDTH), bf16),
+            shape((tokens, 3 * WIDTH), bf16),
+            shape((tokens, WIDTH), bf16),
+        ],
+        scratch_shapes=[
+            pltpu.VMEM((4, 8, 96, WIDTH), bf16),
+            pltpu.SemaphoreType.DMA((copies_in_all,)),
+        ],
+        compiler_params=params(),
+        cost_estimate=cost(8 * tokens * WIDTH * WIDTH * 1.5, 12e6),
+        name="attn_forward",
+    )(place, hidden, small, *pack)
+
+
+def expand_forward(place, middle, small, expand_bias, pack, cut, first):
+    plan = piece_plan(cut, first, 384)
+
+    def kernel(place_ref, middle_ref, small_ref, bias_ref, *rest):
+        packs = rest[:10]
+        normed_ref, active_ref, slope_ref, block, sems = rest[10:]
+        image = pl.program_id(0)
+        copies = block_copies(place_ref[0], packs, plan, block, sems)
+
+        @pl.when(image == 0)
+        def begin():
+            run_all(copies, "start")
+
+        unit, root = normalise(middle_ref[...])
+        normed = (unit * small_ref[SM_G2 : SM_G2 + 1] + small_ref[SM_S2 : SM_S2 + 1]).astype(bf16)
+        normed_ref[...] = normed
+
+        @pl.when(image == 0)
+        def arrive():
+            run_all(copies, "wait")
+
+        for part in range(FF_PARTS):
+            weight = block[2 * part : 2 * part + 2].reshape(WIDTH, WIDTH)
+            point = dot_nt(normed, weight) + bias_ref[part : part + 1]
+            square = point * point
+            slant = jnp.tanh(0.7978845608028654 * point * (1.0 + 0.044715 * square))
+            upper = 0.5 + 0.5 * slant
+            columns = slice(WIDTH * part, WIDTH * (part + 1))
+            active_ref[:, columns] = (point * upper).astype(bf16)
+            bend = point * (0.7978845608028654 + (3 * 0.044715 * 0.7978845608028654) * square)
+            slope_ref[:, columns] = (upper + 0.5 * bend * (1.0 - slant * slant)).astype(bf16)
+
+    tokens = middle.shape[0]
+    hidden_units = FF_PARTS * WIDTH
+    shape = jax.ShapeDtypeStruct
+    return pl.pallas_call(
+        kernel,
+        grid=(tokens // ROWS,),
+        in_specs=[
+            in_smem(),
+            rows_spec(WIDTH),
+            fixed(small.shape),
+            fixed(expand_bias.shape),
+        ]
+        + [in_any()] * 10,
+        out_specs=[rows_spec(WIDTH), rows_spec(hidden_units), rows_spec(hidden_units)],
+        out_shape=[
+            shape((tokens, WIDTH), bf16),
+            shape((tokens, hidden_units), bf16),
+            shape((tokens, hidden_units), bf16),
+        ],
+        scratch_shapes=[
+            pltpu.VMEM((8, 384, WIDTH), bf16),
+            pltpu.SemaphoreType.DMA((len(plan),)),
+        ],
+        compiler_params=params(),
+        cost_estimate=cost(8 * tokens * WIDTH * WIDTH, 14e6),
+        name="expand_forward",
+    )(place, middle, small, expand_bias, *pack)
+
+
+def reduce_plans(cut, first):
+    return [piece_plan(cut, first + 96 * part, 96) for part in range(FF_PARTS)]
+
+
+def reduce_forward(place, live, middle, active, small, pack, cut, first, last):
+    plans = reduce_plans(cut, first)
+    copies_in_all = sum(len(plan) for plan in plans)
+
+    def kernel(place_ref, live_ref, middle_ref, active_ref, small_ref, *rest):
+        packs = rest[:10]
+        result_ref, blocks, sems = rest[10:]
+        image = pl.program_id(0)
+        copies = []
+        for part, plan in enumerate(plans):
+            at = sum(len(earlier) for earlier in plans[:part])
+            copies += block_copies(
+                place_ref[0], packs, plan, blocks.at[part], sems.at[pl.ds(at, len(plan))]
+            )
+
+        @pl.when(image == 0)
+        def arrive():
+            run_all(copies, "start")
+            run_all(copies, "wait")
+
+        total = middle_ref[...] + small_ref[SM_RB : SM_RB + 1]
+        for part in range(FF_PARTS):
+            total = total + dot_nt(
+                active_ref[:, WIDTH * part : WIDTH * (part + 1)],
+                blocks[part].reshape(WIDTH, WIDTH),
+            )
+        if last:
+            total = total * live_ref[image, 0].astype(f32)
+        result_ref[...] = total.astype(result_ref.dtype)
+
+    tokens = middle.shape[0]
+    return pl.pallas_call(
+        kernel,
+        grid=(tokens // ROWS,),
+        in_specs=[
+            in_smem(),
+            in_smem(),
+            rows_spec(WIDTH),
+            rows_spec(FF_PARTS * WIDTH),
+            fixed(small.shape),
+        ]
+        + [in_any()] * 10,
+        out_specs=rows_spec(WIDTH),
+        out_shape=jax.ShapeDtypeStruct((tokens, WIDTH), bf16 if last else f32),
+        scratch_shapes=[
+            pltpu.VMEM((FF_PARTS, 8, 96, WIDTH), bf16),
+            pltpu.SemaphoreType.DMA((copies_in_all,)),
+        ],
+        compiler_params=params(),
+        cost_estimate=cost(8 * tokens * WIDTH * WIDTH, 12e6),
+        name="reduce_forward",
+    )(place, live, middle, active, small, *pack)
+
+
+def split_owners(place_now, turned, mine_ref, theirs_ref, count, lead=()):
+    core = place_now & 1
+    chip = place_now >> 1
+    for owner in range(4):
+        mine_ref[lead + (owner ^ chip,)] = turned[2 * owner + core]
+        theirs_ref[lead + (owner ^ chip,)] = turned[2 * owner + 1 - core]
+
+
+def halves_spec(count):
+    return pl.BlockSpec((4, count, ROWS), lambda image: (0, 0, image))
+
+
+def start_grad(place, live, cotangent):
+    def kernel(place_ref, live_ref, cot_ref, grad_ref, mine_ref, theirs_ref, turned):
+        image = pl.program_id(0)
+        grad = cot_ref[...].astype(f32) * live_ref[image, 0].astype(f32)
+        grad_ref[...] = grad.astype(bf16)
+        turned[...] = grad.T.astype(bf16).reshape(8, 96, ROWS)
+        split_owners(place_ref[0], turned, mine_ref, theirs_ref, 96)
+
+    tokens = cotangent.shape[0]
+    shape = jax.ShapeDtypeStruct
+    return pl.pallas_call(
+        kernel,
+        grid=(tokens // ROWS,),
+        in_specs=[in_smem(), in_smem(), rows_spec(WIDTH)],
+        out_specs=[rows_spec(WIDTH), halves_spec(96), halves_spec(96)],
+        out_shape=[shape((tokens, WIDTH), bf16)] + [shape((4, 96, tokens), bf16)] * 2,
+        scratch_shapes=[pltpu.VMEM((8, 96, ROWS), bf16)],
+        compiler_params=params(),
+        cost_estimate=cost(1e6, 4e6),
+        name="start_grad",
+    )(place, live, cotangent)
+
+
+def ff_backward(place, grad, slope, middle, small, packs_and_plans):
+    (expand_pack, expand_cut, expand_first), (reduce_pack, reduce_cut, reduce_first) = (
+        packs_and_plans
+    )
+    expand_plan = piece_plan(expand_cut, expand_first, 384)
+    plans = reduce_plans(reduce_cut, reduce_first)
+    copies_in_all = sum(len(plan) for plan in plans)
+
+    def kernel(place_ref, grad_ref, slope_ref, middle_ref, small_ref, *rest):
+        expand_packs, reduce_packs = rest[:10], rest[10:20]
+        (
+            out_ref,
+            pre_mine,
+            pre_theirs,
+            attn_mine,
+            attn_theirs,
+            sums_ref,
+            expand_block,
+            reduce_blocks,
+            turned_pre,
+            turned_attn,
+            expand_sems,
+            reduce_sems,
+        ) = rest[20:]
+        place_now = place_ref[0]
+        image = pl.program_id(0)
+        reduce_copies = []
+        for part, plan in enumerate(plans):
+            at = sum(len(earlier) for earlier in plans[:part])
+            reduce_copies.append(
+                block_copies(
+                    place_now,
+                    reduce_packs,
+                    plan,
+                    reduce_blocks.at[part],
+                    reduce_sems.at[pl.ds(at, len(plan))],
+                )
+            )
+        expand_copies = block_copies(
+            place_now, expand_packs, expand_plan, expand_block, expand_sems
+        )
+
+        @pl.when(image == 0)
+        def begin():
+            for group in reduce_copies:
+                run_all(group, "start")
+            run_all(expand_copies, "start")
+            sums_ref[...] = jnp.zeros_like(sums_ref)
+
+        grad_rows = grad_ref[...].astype(f32)
+        low = grad_rows.astype(bf16)
+        sums_ref[0:1] += jnp.sum(low.astype(f32), axis=0, keepdims=True)
+        core = place_now & 1
+        chip = place_now >> 1
+        back = jnp.zeros((ROWS, WIDTH), f32)
+        for part in range(FF_PARTS):
+
+            @pl.when(image == 0)
+            def arrive():
+                run_all(reduce_copies[part], "wait")
+                if part == 0:
+                    run_all(expand_copies, "wait")
+
+            columns = slice(WIDTH * part, WIDTH * (part + 1))
+            up = dot_nn(low, reduce_blocks[part].reshape(WIDTH, WIDTH))
+            pre = up * slope_ref[:, columns].astype(f32)
+            pre_low = pre.astype(bf16)
+            sums_ref[4 + part : 5 + part] += jnp.sum(
+                pre_low.astype(f32), axis=0, keepdims=True
+            )
+            turned_pre[...] = pre_low.T.reshape(2, 384, ROWS)
+            pre_mine[part ^ chip] = turned_pre[core]
+            pre_theirs[part ^ chip] = turned_pre[1 - core]
+            back = back + dot_nn(
+                pre_low, expand_block[2 * part : 2 * part + 2].reshape(WIDTH, WIDTH)
+            )
+        unit, root = normalise(middle_ref[...])
+        sums_ref[1:2] += jnp.sum(back * unit, axis=0, keepdims=True)
+        sums_ref[2:3] += jnp.sum(back, axis=0, keepdims=True)
+        scaled = back * small_ref[SM_G2 : SM_G2 + 1]
+        result = grad_rows + root * (
+            scaled
+            - jnp.mean(scaled, axis=-1, keepdims=True)
+            - unit * jnp.mean(scaled * unit, axis=-1, keepdims=True)
+        )
+        out_ref[...] = result
+        result_low = result.astype(bf16)
+        sums_ref[3:4] += jnp.sum(result_low.astype(f32), axis=0, keepdims=True)
+        turned_attn[...] = result_low.T.reshape(8, 96, ROWS)
+        split_owners(place_now, turned_attn, attn_mine, attn_theirs, 96)
+
+    tokens = middle.shape[0]
+    shape = jax.ShapeDtypeStruct
+    return pl.pallas_call(
+        kernel,
+        grid=(tokens // ROWS,),
+        in_specs=[
+            in_smem(),
+            rows_spec(WIDTH),
+            rows_spec(FF_PARTS * WIDTH),
+            rows_spec(WIDTH),
+            fixed(small.shape),
+        ]
+        + [in_any()] * 20,
+        out_specs=[
+            rows_spec(WIDTH),
+            halves_spec(384),
+            halves_spec(384),
+            halves_spec(96),
+            halves_spec(96),
+            fixed((8, WIDTH)),
+        ],
+        out_shape=[shape((tokens, WIDTH), f32)]
+        + [shape((4, 384, tokens), bf16)] * 2
+        + [shape((4, 96, tokens), bf16)] * 2
+        + [shape((8, WIDTH), f32)],
+        scratch_shapes=[
+            pltpu.VMEM((8, 384, WIDTH), bf16),
+            pltpu.VMEM((FF_PARTS, 8, 96, WIDTH), bf16),
+            pltpu.VMEM((2, 384, ROWS), bf16),
+            pltpu.VMEM((8, 96, ROWS), bf16),
+            pltpu.SemaphoreType.DMA((len(expand_plan),)),
+            pltpu.SemaphoreType.DMA((copies_in_all,)),
+        ],
+        compiler_params=params(),
+        cost_estimate=cost(16 * tokens * WIDTH * WIDTH, 22e6),
+        name="ff_backward",
+    )(place, grad, slope, middle, small, *expand_pack, *reduce_pack)
+
+
+def attn_backward(place, grad, hidden, qkv, small, pack, cut, last):
+    plans = [piece_plan(cut, 96 * at, 96) for at in range(4)]
+    copies_in_all = sum(len(plan) for plan in plans)
+
+    def kernel(place_ref, grad_ref, hidden_ref, qkv_ref, small_ref, *rest):
+        packs = rest[:10]
+        if last:
+            out_ref, qkv_mine, qkv_theirs, sums_ref = rest[10:14]
+        else:
+            out_ref, qkv_mine, qkv_theirs, sums_ref, low_mine, low_theirs = rest[10:16]
+        blocks, turned, straight, sems = rest[-4:]
+        place_now = place_ref[0]
+        image = pl.program_id(0)
+        copies = []
+        at = 0
+        for member, plan in enumerate(plans):
+            copies.append(
+                block_copies(
+                    place_now, packs, plan, blocks.at[member], sems.at[pl.ds(at, len(plan))]
+                )
+            )
+            at += len(plan)
+
+        @pl.when(image == 0)
+        def begin():
+            for member in (3, 0, 1, 2):
+                run_all(copies[member], "start")
+            sums_ref[...] = jnp.zeros_like(sums_ref)
+
+        grad_rows = grad_ref[...]
+
+        @pl.when(image == 0)
+        def arrive():
+            for member in (3, 0, 1, 2):
+                run_all(copies[member], "wait")
+
+        mixed_back = dot_nn(grad_rows.astype(bf16), blocks[3].reshape(WIDTH, WIDTH)).astype(bf16)
+        lane = lax.broadcasted_iota(jnp.int32, (ROWS, 128), 1)
+        line = lax.broadcasted_iota(jnp.int32, (128, ROWS), 0)
+        for pair in range(HEADS // 2):
+            q_pair = qkv_ref[:, 128 * pair : 128 * pair + 128]
+            k_pair = qkv_ref[:, WIDTH + 128 * pair : WIDTH + 128 * pair + 128]
+            v_pair = qkv_ref[:, 2 * WIDTH + 128 * pair : 2 * WIDTH + 128 * pair + 128]
+            g_pair = mixed_back[:, 128 * pair : 128 * pair + 128]
+            q_turned = q_pair.T
+            k_turned = k_pair.T
+            g_turned = g_pair.T
+            made = []
+            for half in range(2):
+                here = (lane < 64) == (half == 0)
+                k_one = jnp.where(here, k_pair, jnp.zeros_like(k_pair))
+                v_one = jnp.where(here, v_pair, jnp.zeros_like(v_pair))
+                scores = dot_nt(k_one, q_pair) * (HEAD_DIM**-0.5)
+                peak = jnp.max(scores, axis=0, keepdims=True)
+                powers = jnp.exp(scores - peak)
+                attend = powers / jnp.sum(powers, axis=0, keepdims=True)
+                back = dot_nt(v_one, g_pair)
+                inner = jnp.sum(back * attend, axis=0, keepdims=True)
+                scores_back = (attend * (back - inner)).astype(bf16)
+                made.append(
+                    (
+                        dot_nn(k_turned, scores_back) * (HEAD_DIM**-0.5),
+                        dot_nt(q_turned, scores_back) * (HEAD_DIM**-0.5),
+                        dot_nt(g_turned, attend.astype(bf16)),
+                    )
+                )
+            for member in range(3):
+                both = jnp.where(line < 64, made[0][member], made[1][member]).astype(bf16)
+                turned[member, pl.ds(128 * pair, 128)] = both
+                straight[:, WIDTH * member + 128 * pair : WIDTH * member + 128 * pair + 128] = (
+                    both.T
+                )
+        core = place_now & 1
+        chip = place_now >> 1
+        back = jnp.zeros((ROWS, WIDTH), f32)
+        for member in range(3):
+            for owner in range(4):
+                for odd in range(2):
+                    rows = turned[
+                        member,
+                        pl.ds(pl.multiple_of(192 * owner + 96 * (core ^ odd), 96), 96),
+                    ]
+                    target = qkv_theirs if odd else qkv_mine
+                    target[member, owner ^ chip] = rows
+            straight_one = straight[:, WIDTH * member : WIDTH * (member + 1)]
+            back = back + dot_nn(straight_one, blocks[member].reshape(WIDTH, WIDTH))
+            if member != 1:
+                row = 0 if member == 0 else 1
+                sums_ref[row : row + 1] += jnp.sum(
+                    straight_one.astype(f32), axis=0, keepdims=True
+                )
+        unit, root = normalise(hidden_ref[...].astype(f32))
+        sums_ref[2:3] += jnp.sum(back * unit, axis=0, keepdims=True)
+        sums_ref[3:4] += jnp.sum(back, axis=0, keepdims=True)
+        scaled = back * small_ref[SM_G1 : SM_G1 + 1]
+        result = grad_rows + root * (
+            scaled
+            - jnp.mean(scaled, axis=-1, keepdims=True)
+            - unit * jnp.mean(scaled * unit, axis=-1, keepdims=True)
+        )
+        out_ref[...] = result.astype(out_ref.dtype)
+        if not last:
+            turned[0] = result.astype(bf16).T
+            for owner in range(4):
+                for odd in range(2):
+                    rows = turned[
+                        0, pl.ds(pl.multiple_of(192 * owner + 96 * (core ^ odd), 96), 96)
+                    ]
+                    target = low_theirs if odd else low_mine
+                    target[owner ^ chip] = rows
+
+    tokens = grad.shape[0]
+    shape = jax.ShapeDtypeStruct
+    heads_spec = pl.BlockSpec((3, 4, 96, ROWS), lambda image: (0, 0, 0, image))
+    out_specs = [rows_spec(WIDTH), heads_spec, heads_spec, fixed((8, WIDTH))]
+    out_shape = (
+        [shape((tokens, WIDTH), bf16 if last else f32)]
+        + [shape((3, 4, 96, tokens), bf16)] * 2
+        + [shape((8, WIDTH), f32)]
+    )
+    if not last:
+        out_specs += [halves_spec(96)] * 2
+        out_shape += [shape((4, 96, tokens), bf16)] * 2
+    return pl.pallas_call(
+        kernel,
+        grid=(tokens // ROWS,),
+        in_specs=[
+            in_smem(),
+            rows_spec(WIDTH),
+            rows_spec(WIDTH),
+            rows_spec(3 * WIDTH),
+            fixed(small.shape),
+        ]
+        + [in_any()] * 10,
+        out_specs=out_specs,
+        out_shape=out_shape,
+        scratch_shapes=[
+            pltpu.VMEM((4, 8, 96, WIDTH), bf16),
+            pltpu.VMEM((3, WIDTH, ROWS), bf16),
+            pltpu.VMEM((ROWS, 3 * WIDTH), bf16),
+            pltpu.SemaphoreType.DMA((copies_in_all,)),
+        ],
+        compiler_params=params(),
+        cost_estimate=cost(8 * tokens * WIDTH * WIDTH * 2.5, 16e6),
+        name="attn_backward",
+    )(place, grad, hidden, qkv, small, *pack)
+
+
+def spread(result, owner, rows, out_refs, half):
+    go_x, go_y, stay_x, stay_y = out_refs
+    low, high = result[:, :half].astype(bf16), result[:, half:].astype(bf16)
+    target, at = ((stay_x, 0), (go_x, 0), (stay_x, 1), (go_x, 1))[owner]
+    target[at, rows] = low
+    target, at = ((stay_y, 0), (stay_y, 1), (go_y, 0), (go_y, 1))[owner]
+    target[at, rows] = high
+
+
+def travel_shapes(rows_low, rows_high, half):
+    shape = jax.ShapeDtypeStruct
+    return [
+        shape((2, rows_low, half), bf16),
+        shape((2, rows_high, half), bf16),
+        shape((2, rows_low, half), bf16),
+        shape((2, rows_high, half), bf16),
+    ]
+
+
+def reduce_terms(grad_mine, grad_other, active_mine, active_other):
+    tokens, columns = active_mine.shape
+    half = columns // 2
+    chunk = min(half, WIDTH)
+
+    def kernel(grad_a, grad_b, low_a, low_b, high_a, high_b, go_x, go_y, stay_x, stay_y):
+        left_a = grad_a[...].reshape(384, tokens)
+        left_b = grad_b[...].reshape(384, tokens)
+        low = dot_nn(left_a, low_a[...]) + dot_nn(left_b, low_b[...])
+        low = low.astype(bf16).reshape(4, 96, chunk)
+        stay_x[0], go_x[0], stay_x[1], go_x[1] = low[0], low[1], low[2], low[3]
+        high = dot_nn(left_a, high_a[...]) + dot_nn(left_b, high_b[...])
+        high = high.astype(bf16).reshape(4, 96, chunk)
+        stay_y[0], stay_y[1], go_y[0], go_y[1] = high[0], high[1], high[2], high[3]
+
+    steps = half // chunk
+    grads_spec = pl.BlockSpec((4, 96, tokens), lambda at: (0, 0, 0))
+    low_spec = pl.BlockSpec((tokens, chunk), lambda at: (0, at))
+    high_spec = pl.BlockSpec((tokens, chunk), lambda at: (0, at + steps))
+    return pl.pallas_call(
+        kernel,
+        grid=(steps,),
+        in_specs=[grads_spec, grads_spec, low_spec, low_spec, high_spec, high_spec],
+        out_specs=[pl.BlockSpec((2, 96, chunk), lambda at: (0, 0, at))] * 4,
+        out_shape=travel_shapes(96, 96, half),
+        compiler_params=params(),
+        cost_estimate=cost(4 * 384 * tokens * columns, 12e6),
+        name="reduce_terms",
+    )(grad_mine, grad_other, active_mine, active_other, active_mine, active_other)
+
+
+def expand_terms(grad_mine, grad_other, normed_mine, normed_other):
+    tokens = normed_mine.shape[0]
+
+    def kernel(grad_a, grad_b, rows_a, rows_b, *out_refs):
+        for owner in range(4):
+            result = dot_nn(grad_a[owner], rows_a[...]) + dot_nn(grad_b[owner], rows_b[...])
+            spread(result, owner, slice(None), out_refs, WIDTH // 2)
+
+    return pl.pallas_call(
+        kernel,
+        out_shape=travel_shapes(384, 384, WIDTH // 2),
+        compiler_params=pltpu.CompilerParams(vmem_limit_bytes=VMEM_BYTES),
+        cost_estimate=cost(4 * 1536 * tokens * WIDTH, 9e6),
+        name="expand_terms",
+    )(grad_mine, grad_other, normed_mine, normed_other)
+
+
+def attn_terms(
+    qkv_mine,
+    qkv_other,
+    normed_mine,
+    normed_other,
+    attn_mine,
+    attn_other,
+    mixed_mine,
+    mixed_other,
+    small_terms,
+):
+    tokens = normed_mine.shape[0]
+
+    def kernel(
+        qkv_a, qkv_b, normed_a, normed_b, attn_a, attn_b, mixed_a, mixed_b, small_ref, *out_refs
+    ):
+        go_x, go_y, stay_x, stay_y = out_refs
+        for member in range(4):
+            if member < 3:
+                left_a, left_b, right_a, right_b = qkv_a[member], qkv_b[member], normed_a, normed_b
+            else:
+                left_a, left_b, right_a, right_b = attn_a[...], attn_b[...], mixed_a, mixed_b
+            result = dot_nn(left_a.reshape(384, tokens), right_a[...]) + dot_nn(
+                left_b.reshape(384, tokens), right_b[...]
+            )
+            for owner in range(4):
+                spread(
+                    result[96 * owner : 96 * owner + 96],
+                    owner,
+                    slice(96 * member, 96 * member + 96),
+                    out_refs,
+                    WIDTH // 2,
+                )
+        for owner in range(4):
+            target, at = ((stay_x, 0), (go_x, 0), (stay_x, 1), (go_x, 1))[owner]
+            target[at, 384:400] = small_ref[owner]
+
+    return pl.pallas_call(
+        kernel,
+        out_shape=travel_shapes(400, 384, WIDTH // 2),
+        compiler_params=pltpu.CompilerParams(vmem_limit_bytes=VMEM_BYTES),
+        cost_estimate=cost(4 * 1536 * tokens * WIDTH, 10e6),
+        name="attn_terms",
+    )(
+        qkv_mine,
+        qkv_other,
+        normed_mine,
+        normed_other,
+        attn_mine,
+        attn_other,
+        mixed_mine,
+        mixed_other,
+        small_terms,
+    )
+
+
+def by_difference(place_at, rows):
+    shape = rows.shape
+    for bit in range(3):
+        halves = rows.reshape((8 >> (bit + 1), 2, 1 << bit) + shape[1:])
+        rows = jnp.where((place_at >> bit) & 1 == 1, halves[:, ::-1], halves).reshape(shape)
+    return rows
+
+
+def add_low(*parts):
+    total = parts[0].astype(f32)
+    for part in parts[1:]:
+        total = total + part.astype(f32)
+    return total.astype(bf16)
+
+
+def sum_chips(go_x, go_y, stay_x, stay_y):
+    from_x, from_y = swap_x(go_x), swap_y(go_y)
+    low_on = swap_y(add_low(stay_x[1], from_x[1]))
+    high_on = swap_x(add_low(stay_y[1], from_y[1]))
+    return jnp.concatenate(
+        [add_low(stay_x[0], from_x[0], low_on), add_low(stay_y[0], from_y[0], high_on)]
+    )
+
+
+def sum_replicas(part):
+    inward = add_low(part, lax.ppermute(part, "rep", [(0, 1), (3, 2)]))
+    total = add_low(inward, lax.ppermute(inward, "rep", [(1, 2), (2, 1)]))
+    outward = lax.ppermute(total, "rep", [(1, 0), (2, 3)])
+    rep_at = lax.axis_index("rep")
+    return jnp.where((rep_at == 0) | (rep_at == 3), outward, total).astype(f32)
+
+
+def shards(
+    images,
+    cotangent,
+    slot_flags,
+    heads_weight,
+    heads_bias,
+    merge_weight,
+    merge_bias,
+    first_gain,
+    first_shift,
+    second_gain,
+    second_shift,
+    expand_weight,
+    expand_bias,
+    reduce_weight,
+    reduce_bias,
+):
+    micro_count, unused_slots, seq_len, width = images.shape
+    layers = heads_weight.shape[0]
+    tokens = micro_count * seq_len
+    place_at = lax.axis_index("fsdp").astype(jnp.int32)
+    place = place_at[None]
+
+    def small_rows(layer):
+        rows = jnp.concatenate(
+            [
+                heads_bias[layer],
+                merge_bias[layer][None],
+                first_gain[layer][None],
+                first_shift[layer][None],
+                second_gain[layer][None],
+                second_shift[layer][None],
+                reduce_bias[layer][None],
+                expand_bias[layer].reshape(4, 96),
+            ]
+        )
+        return jnp.pad(rows, ((0, 4), (0, width - 96)))
+
+    def reduce_rows(layer):
+        return [reduce_weight[layer][:, width * part : width * (part + 1)] for part in range(4)]
+
+    attn_cut, ff_cut = 192, 384
+    attn_packs, ff_packs = [], []
+    for layer in range(layers):
+        own = jnp.concatenate(
+            [
+                heads_weight[layer].reshape(288, width),
+                merge_weight[layer],
+                small_rows(layer),
+            ]
+        )
+        attn_packs.append(gather_pack(own, attn_cut))
+        own = jnp.concatenate([expand_weight[layer]] + reduce_rows(layer))
+        ff_packs.append(gather_pack(own, ff_cut))
+
+    smalls, expand_biases = [], []
+    for pack in attn_packs:
+        own, along_x, along_y, unused, across, own_c, x_c, y_c, unused_c, across_c = pack
+        rows = [
+            own[384:396, :96],
+            own_c[384:396, :96],
+            along_x[384:396, :96],
+            x_c[384:396, :96],
+            along_y[384:396, :96],
+            y_c[384:396, :96],
+            across[192:204, :96],
+            across_c[192:204, :96],
+        ]
+        ordered = by_difference(place_at, jnp.stack(rows).astype(f32))
+        smalls.append(ordered[:, :8].transpose(1, 0, 2).reshape(8, width))
+        expand_biases.append(ordered[:, 8:].reshape(4, width))
+
+    hidden = images.reshape(tokens, width)
+    saved = []
+    grad, low_mine, low_theirs = start_grad(place, slot_flags, cotangent.reshape(tokens, width))
+    for layer in range(layers):
+        last = layer == layers - 1
+        small = smalls[layer]
+        middle, normed, qkv, mixed = attn_forward(
+            place, hidden, small, attn_packs[layer], attn_cut
+        )
+        second, active, slope = expand_forward(
+            place, middle, small, expand_biases[layer], ff_packs[layer], ff_cut, 0
+        )
+        following = reduce_forward(
+            place, slot_flags, middle, active, small, ff_packs[layer], ff_cut, 384, last
+        )
+        others = tuple(swap_core(rows) for rows in (normed, mixed, second, active))
+        saved.append((hidden, normed, qkv, mixed, middle, second, active, slope, others))
+        hidden = following
+    outputs = hidden.reshape(images.shape)
+
+    sums = [None] * layers
+    for layer in reversed(range(layers)):
+        last = layer == 0
+        small = smalls[layer]
+        before, normed, qkv, mixed, middle, second, active, slope, others = saved[layer]
+        normed_other, mixed_other, second_other, active_other = others
+        reduce_sum = sum_replicas(
+            sum_chips(*reduce_terms(low_mine, swap_core(low_theirs), active, active_other))
+        )
+        grad, pre_mine, pre_theirs, attn_mine, attn_theirs, ff_sums = ff_backward(
+            place,
+            grad,
+            slope,
+            middle,
+            small,
+            ((ff_packs[layer], ff_cut, 0), (ff_packs[layer], ff_cut, 384)),
+        )
+        expand_sum = sum_replicas(
+            sum_chips(*expand_terms(pre_mine, swap_core(pre_theirs), second, second_other))
+        )
+        made = attn_backward(place, grad, before, qkv, small, attn_packs[layer], attn_cut, last)
+        grad, qkv_mine, qkv_theirs, attn_sums = made[:4]
+        if not last:
+            low_mine, low_theirs = made[4:]
+        vectors = jnp.concatenate(
+            [
+                attn_sums[0:2],
+                ff_sums[3:4],
+                attn_sums[2:4],
+                ff_sums[1:3],
+                ff_sums[0:1],
+            ]
+        )
+        terms = jnp.concatenate(
+            [
+                vectors.reshape(8, 8, 96).transpose(1, 0, 2),
+                ff_sums[4:8].reshape(8, 4, 96),
+            ],
+            axis=1,
+        )
+        terms = by_difference(place_at, terms).reshape(4, 2, 12, 96)
+        terms = terms[:, 0] + swap_core(terms[:, 1])
+        terms = jnp.pad(terms, ((0, 0), (0, 4), (0, width // 2 - 96))).astype(bf16)
+        attn_sum = sum_replicas(
+            sum_chips(
+                *attn_terms(
+                    qkv_mine,
+                    swap_core(qkv_theirs),
+                    normed,
+                    normed_other,
+                    attn_mine,
+                    swap_core(attn_theirs),
+                    mixed,
+                    mixed_other,
+                    terms,
+                )
+            )
+        )
+        sums[layer] = (reduce_sum, expand_sum, attn_sum)
+    images_grad = grad.reshape(images.shape)
+
+    grad_scale = (
+        micro_count * images.shape[1] * lax.axis_size("fsdp") * lax.axis_size("rep") * seq_len
+    ) ** (-0.5)
+    finals = []
+    for reduce_sum, expand_sum, attn_sum in sums:
+        low, high = attn_sum[:400] * grad_scale, attn_sum[400:] * grad_scale
+        whole = jnp.concatenate([low[:384], high], axis=1)
+        vectors = low[384:396, :96]
+        finals.append(
+            (
+                whole[:288].reshape(3, 96, width),
+                vectors[SM_HB0 : SM_HB1 + 1],
+                whole[288:],
+                vectors[SM_MB],
+                vectors[SM_G1],
+                vectors[SM_S1],
+                vectors[SM_G2],
+                vectors[SM_S2],
+                jnp.concatenate([expand_sum[:384], expand_sum[384:]], axis=1) * grad_scale,
+                vectors[8:12].reshape(384),
+                jnp.concatenate([reduce_sum[:96], reduce_sum[96:]], axis=1) * grad_scale,
+                vectors[SM_RB],
+            )
+        )
+    stacked = tuple(jnp.stack(member) for member in zip(*finals))
+    return (outputs, images_grad) + stacked
+
+
 def solution(mesh):
+    body = shards if (mesh.shape["fsdp"], mesh.shape["rep"]) == (8, 4) else plain_shards
     placed = (
         P(None, ("fsdp", "rep"), None, None),
         P(None, ("fsdp", "rep"), None, None),
@@ -375,7 +1330,7 @@
         P(None, "fsdp"),
     )
     return jax.shard_map(
-        shards,
+        body,
         mesh=mesh,
         in_specs=placed,
         out_specs=(

time: 1150 us -> 596 us (0.52)
  waiting for transfers between devices: 681 us -> 247 us
  matrix products: 201 us -> 0 us
  Pallas kernels: 0 us -> 178 us
  starting transfers between devices: 1.86 us -> 84.2 us
  blocking collectives: 74.2 us -> 0 us
  other arithmetic: 81.9 us -> 33 us
  local copies, waits for them, and re-layouts: 82.3 us -> 39.9 us
  between operations: 18.8 us -> 2.95 us
    unnamed x29 -> x0, waiting for transfers between devices: 283 us -> none
    ppermute x0 -> x96, waiting for transfers between devices: none -> 247 us  [the longest x20 91.3 us: swap_x(): return lax.ppermute(value, 'fsdp', [(at, at ^ 2) for at in range(8)])]
    dot_general x80 -> x0, matrix products: 201 us -> none  [the longest x24 69.3 us: project(): lax.dot_general(token_rows, weight, (((1,), (1,)), ((), ())), preferred_e...]
    pallas_call x0 -> x17, Pallas kernels: none -> 178 us  [the longest x2 41.7 us: attn_backward(): pl.pallas_call(kernel, grid=(tokens // ROWS,), in_specs=[in_smem(), rows_...]
    reduce_scatter x4 -> x0, waiting for transfers between devices: 171 us -> none  [the longest x1 80 us: shards(): lax.psum_scatter(stacked[10].astype(jnp.bfloat16), 'fsdp', scatter_dimens...]
    psum x1 -> x0, waiting for transfers between devices: 120 us -> none  [shards(): lax.psum(shares[0].astype(jnp.bfloat16), 'rep').astype(jnp.float32)]
    all_gather x8 -> x0, waiting for transfers between devices: 107 us -> none  [the longest x2 58.6 us: shards(): lax.all_gather(reduce_weight[layer_at], 'fsdp', axis=0, tiled=True)]
    ppermute x0 -> x96, starting transfers between devices: none -> 84.2 us  [the longest x20 25.2 us: swap_y(): return lax.ppermute(value, 'fsdp', [(at, at ^ 4) for at in range(8)])]
  transfers between devices with their start and end apart: 21 -> 96, of which waited for: 16 -> 38; matrix products, arithmetic and copies ran while one was open for 20% -> 11% of each run, Pallas kernels for 0% -> 30%
where the time goes in v1:
time: 596 us; the launch traced here: 585 us
  waiting for transfers between devices  247 us (41%)
  Pallas kernels  178 us (30%)
  starting transfers between devices  84.2 us (14%)
  local copies, waits for them, and re-layouts  39.9 us (7%)
  other arithmetic  33 us (6%)
    ppermute x20, waiting for transfers between devices, swap_x(): return lax.ppermute(value, 'fsdp', [(at, at ^ 2) for at in range(8)])  91.3 us
    ppermute x20, waiting for transfers between devices, swap_y(): return lax.ppermute(value, 'fsdp', [(at, at ^ 4) for at in range(8)])  56.6 us
    ppermute x6, waiting for transfers between devices, sum_replicas(): outward = lax.ppermute(total, 'rep', [(1, 0), (2, 3)])  54.8 us
    pallas_call x2, Pallas kernels, attn_backward(): pl.pallas_call(kernel, grid=(tokens // ROWS,), in_specs=[in_smem(), rows_...  41.7 us
    ppermute x6, waiting for transfers between devices, sum_replicas(): inward = add_low(part, lax.ppermute(part, 'rep', [(0, 1), (3, 2)]))  40.5 us
    pallas_call x2, Pallas kernels, ff_backward(): pl.pallas_call(kernel, grid=(tokens // ROWS,), in_specs=[in_smem(), rows_...  32.4 us
    ppermute x20, starting transfers between devices, swap_y(): return lax.ppermute(value, 'fsdp', [(at, at ^ 4) for at in range(8)])  25.2 us
    ppermute x20, starting transfers between devices, swap_x(): return lax.ppermute(value, 'fsdp', [(at, at ^ 2) for at in range(8)])  24.7 us
  transfers between devices with their start and end apart: 96, of which 38 were waited for; matrix products, arithmetic and copies ran while one was open for 11% of the time, Pallas kernels for 30%

profile of v1, /device:TPU:0, one launch (start us, length us, event | category | flops | bytes accessed | tf_op | source)
XLA Modules:
  0.0 585.2 jit_solution(17104566602316922991)
XLA Ops:
  25.5 11.1 %collective-permute-done.19.rest_1_ = bf16[400,768]{1,0:T(8,128)(2,1)S(1)} collective-permute-done((bf16[400,768]{1,0:T(8,128)(2,1)}, bf16[400,768]{1,0:T(8,128)(2,1)S(1)}, u32[]{:S(2)}, u32[]{:S(2)}) %collective-permute-start.19) | collective-permute-done | bytes 614432 | tf_op jit(solution)/shard_map/ppermute | solution.py:382
  48.7 15.1 %collective-permute-done.10.rest_2_.rest_12_ = bf16[768,768]{1,0:T(8,128)(2,1)S(1)} collective-permute-done((bf16[768,768]{1,0:T(8,128)(2,1)}, bf16[768,768]{1,0:T(8,128)(2,1)S(1)}, u32[]{:S(2)}, u32[]{:S(2)}) %collective-permute-start.10) | collective-permute-done | bytes 1179680 | tf_op jit(solution)/shard_map/ppermute | solution.py:386
  66.6 22.5 %collective-permute-done.28.rest_2_.rest_12_ = bf16[768,768]{1,0:T(8,128)(2,1)S(1)} collective-permute-done((bf16[768,768]{1,0:T(8,128)(2,1)}, bf16[768,768]{1,0:T(8,128)(2,1)S(1)}, u32[]{:S(2)}, u32[]{:S(2)}) %collective-permute-start.28) | collective-permute-done | bytes 1179680 | tf_op jit(solution)/shard_map/ppermute | solution.py:386
  110.1 11.6 %collective-permute-done.11.rest_3_.rest_13_ = bf16[384,768]{1,0:T(8,128)(2,1)} collective-permute-done((bf16[384,768]{1,0:T(8,128)(2,1)S(1)}, bf16[384,768]{1,0:T(8,128)(2,1)}, u32[]{:S(2)}, u32[]{:S(2)}) %collective-permute-start.11) | collective-permute-done | bytes 589856 | tf_op jit(solution)/shard_map/ppermute | solution.py:382
  123.4 10.1 %collective-permute-done.29.rest_3_.rest_13_ = bf16[384,768]{1,0:T(8,128)(2,1)S(1)} collective-permute-done((bf16[384,768]{1,0:T(8,128)(2,1)S(1)}, bf16[384,768]{1,0:T(8,128)(2,1)S(1)}, u32[]{:S(2)}, u32[]{:S(2)}) %collective-permute-start.29) | collective-permute-done | bytes 589856 | tf_op jit(solution)/shard_map/ppermute | solution.py:382
  144.3 11.9 %attn_forward.2 = (f32[512,768]{1,0:T(8,128)}, bf16[512,768]{1,0:T(8,128)(2,1)}, bf16[512,2304]{1,0:T(8,128)(2,1)}, bf16[512,768]{1,0:T(8,128)(2,1)}) custom-call(s32[1]{0:T(128)} %bitcast.place_ref, bf16[512,768]{1,0:T(8,128)(2,1)} %bitcast.255, f32[8,768]{1,0:T(8,128)} %reshape.302.small_ref, bf16[400,768]{1,0:T(8,128)(2,1)} %fusion.4.rest_0_, ...), custom_call_target="tpu_custom_call" | custom-call | flops 3623878656 | bytes 12000000 | tf_op jit(solution)/shard_map/attn_forward/pallas_call | solution.py:524
  156.9 11.1 %expand_forward.2 = (bf16[512,768]{1,0:T(8,128)(2,1)}, bf16[512,3072]{1,0:T(8,128)(2,1)}, bf16[512,3072]{1,0:T(8,128)(2,1)}) custom-call(s32[1]{0:T(128)} %bitcast.place_ref, f32[512,768]{1,0:T(8,128)} %get-tuple-element.77.middle_ref, f32[8,768]{1,0:T(8,128)} %reshape.302.small_ref, f32[4,768]{1,0:T(4,128)} %reshape.303.bias_ref, ...), custom_call_target="tpu_custom_call" | custom-call | flops 2415919104 | bytes 14000000 | tf_op jit(solution)/shard_map/expand_forward/pallas_call | solution.py:580
  167.9 8.2 %reduce_forward.2.hidden_ref = f32[512,768]{1,0:T(8,128)} custom-call(s32[1]{0:T(128)} %bitcast.place_ref, s32[2,1]{1,0:T(2,128)} %copy.53.live_ref, f32[512,768]{1,0:T(8,128)} %get-tuple-element.77.middle_ref, bf16[512,3072]{1,0:T(8,128)(2,1)} %get-tuple-element.78.active_ref.low_a.high_a, f32[8,768]{1,0:T(8,128)} %reshape.302.small_ref, ...), custom_call_target="tpu_custom_call" | custom-call | flops 2415919104 | bytes 12000000 | tf_op jit(solution)/shard_map/reduce_forward/pallas_call | solution.py:641
  176.1 12.2 %attn_forward.3 = (f32[512,768]{1,0:T(8,128)}, bf16[512,768]{1,0:T(8,128)(2,1)}, bf16[512,2304]{1,0:T(8,128)(2,1)}, bf16[512,768]{1,0:T(8,128)(2,1)}) custom-call(s32[1]{0:T(128)} %bitcast.place_ref, f32[512,768]{1,0:T(8,128)} %reduce_forward.2.hidden_ref, f32[8,768]{1,0:T(8,128)} %reshape.305.small_ref, bf16[400,768]{1,0:T(8,128)(2,1)} %fusion.5.rest_0_, ...), custom_call_target="tpu_custom_call" | custom-call | flops 3623878656 | bytes 12000000 | tf_op jit(solution)/shard_map/attn_forward/pallas_call | solution.py:524
  190.3 11.1 %expand_forward.3 = (bf16[512,768]{1,0:T(8,128)(2,1)}, bf16[512,3072]{1,0:T(8,128)(2,1)}, bf16[512,3072]{1,0:T(8,128)(2,1)}) custom-call(s32[1]{0:T(128)} %bitcast.place_ref, f32[512,768]{1,0:T(8,128)} %get-tuple-element.79.middle_ref, f32[8,768]{1,0:T(8,128)} %reshape.305.small_ref, f32[4,768]{1,0:T(4,128)} %reshape.306.bias_ref, ...), custom_call_target="tpu_custom_call" | custom-call | flops 2415919104 | bytes 14000000 | tf_op jit(solution)/shard_map/expand_forward/pallas_call | solution.py:580
  201.4 16.1 %ff_backward.2 = (f32[512,768]{1,0:T(8,128)}, bf16[4,384,512]{2,1,0:T(8,128)(2,1)}, bf16[4,384,512]{2,1,0:T(8,128)(2,1)}, bf16[4,96,512]{2,1,0:T(8,128)(2,1)}, b...) custom-call(s32[1]{0:T(128)} %bitcast.place_ref, bf16[512,768]{1,0:T(8,128)(2,1)} %get-tuple-element.81.grad_ref, ...), custom_call_target="tpu_custom_call" | custom-call | flops 4831838208 | bytes 22000000 | tf_op jit(solution)/shard_map/ff_backward/pallas_call | solution.py:792
  219.8 21.1 %attn_backward.2 = (f32[512,768]{1,0:T(8,128)}, bf16[3,4,96,512]{3,2,1,0:T(8,128)(2,1)}, bf16[3,4,96,512]{3,2,1,0:T(8,128)(2,1)}, f32[8,768]{1,0:T(8,128)}, bf16...) custom-call(s32[1]{0:T(128)} %bitcast.place_ref, f32[512,768]{1,0:T(8,128)} %get-tuple-element.83.grad_ref, ...), custom_call_target="tpu_custom_call" | custom-call | flops 6039797760 | bytes 16000000 | tf_op jit(solution)/shard_map/attn_backward/pallas_call | solution.py:952
  241.0 16.3 %ff_backward.3 = (f32[512,768]{1,0:T(8,128)}, bf16[4,384,512]{2,1,0:T(8,128)(2,1)}, bf16[4,384,512]{2,1,0:T(8,128)(2,1)}, bf16[4,96,512]{2,1,0:T(8,128)(2,1)}, b...) custom-call(s32[1]{0:T(128)} %bitcast.place_ref, f32[512,768]{1,0:T(8,128)} %get-tuple-element.85.grad_ref, ...), custom_call_target="tpu_custom_call" | custom-call | flops 4831838208 | bytes 22000000 | tf_op jit(solution)/shard_map/ff_backward/pallas_call | solution.py:792
  260.9 20.6 %attn_backward.3 = (bf16[512,768]{1,0:T(8,128)(2,1)}, bf16[3,4,96,512]{3,2,1,0:T(8,128)(2,1)}, bf16[3,4,96,512]{3,2,1,0:T(8,128)(2,1)}, f32[8,768]{1,0:T(8,128)}) custom-call(s32[1]{0:T(128)} %bitcast.place_ref, f32[512,768]{1,0:T(8,128)} %get-tuple-element.87.grad_ref, bf16[512,768]{1,0:T(8,128)(2,1)} %bitcast.256, ...), custom_call_target="tpu_custom_call" | custom-call | flops 6039797760 | bytes 16000000 | tf_op jit(solution)/shard_map/attn_backward/pallas_call | solution.py:952
  286.6 8.3 %reduce_forward.3 = bf16[512,768]{1,0:T(8,128)(2,1)} custom-call(s32[1]{0:T(128)} %bitcast.place_ref, s32[2,1]{1,0:T(2,128)} %copy.53.live_ref, f32[512,768]{1,0:T(8,128)} %get-tuple-element.79.middle_ref, bf16[512,3072]{1,0:T(8,128)(2,1)} %get-tuple-element.80.active_ref.low_a.high_a, f32[8,768]{1,0:T(8,128)} %reshape.305.small_ref, ...), custom_call_target="tpu_custom_call" | custom-call | flops 2415919104 | bytes 12000000 | tf_op jit(solution)/shard_map/reduce_forward/pallas_call | solution.py:641
  296.8 6.8 %attn_terms.3 = (bf16[2,400,384]{2,1,0:T(8,128)(2,1)}, bf16[2,384,384]{2,1,0:T(8,128)(2,1)}, bf16[2,400,384]{2,1,0:T(8,128)(2,1)}, bf16[2,384,384]{2,1,0:T(8,128)(2,1)}) custom-call(bf16[3,4,96,512]{3,2,1,0:T(8,128)(2,1)} %get-tuple-element.102.qkv_a, bf16[3,4,96,512]{3,2,1,0:T(8,128)(2,1)} %collective-permute-done.48.qkv_b, ...), custom_call_target="tpu_custom_call" | custom-call | flops 2415919104 | bytes 10000000 | tf_op jit(solution)/shard_map/attn_terms/pallas_call | solution.py:1081
  305.1 7.0 %attn_terms.2 = (bf16[2,400,384]{2,1,0:T(8,128)(2,1)}, bf16[2,384,384]{2,1,0:T(8,128)(2,1)}, bf16[2,400,384]{2,1,0:T(8,128)(2,1)}, bf16[2,384,384]{2,1,0:T(8,128)(2,1)}) custom-call(bf16[3,4,96,512]{3,2,1,0:T(8,128)(2,1)} %get-tuple-element.90.qkv_a, bf16[3,4,96,512]{3,2,1,0:T(8,128)(2,1)} %collective-permute-done.36.qkv_b, ...), custom_call_target="tpu_custom_call" | custom-call | flops 2415919104 | bytes 10000000 | tf_op jit(solution)/shard_map/attn_terms/pallas_call | solution.py:1081
  313.0 6.3 %expand_terms.3 = (bf16[2,384,384]{2,1,0:T(8,128)(2,1)}, bf16[2,384,384]{2,1,0:T(8,128)(2,1)}, bf16[2,384,384]{2,1,0:T(8,128)(2,1)}, bf16[2,384,384]{2,1,0:T(8,128)(2,1)}) custom-call(bf16[4,384,512]{2,1,0:T(8,128)(2,1)} %get-tuple-element.121.grad_a, bf16[4,384,512]{2,1,0:T(8,128)(2,1)} %collective-permute-done.69.grad_b, ...), custom_call_target="tpu_custom_call" | custom-call | flops 2415919104 | bytes 9000000 | tf_op jit(solution)/shard_map/expand_terms/pallas_call | solution.py:1035
  320.9 6.2 %expand_terms.2 = (bf16[2,384,384]{2,1,0:T(8,128)(2,1)}, bf16[2,384,384]{2,1,0:T(8,128)(2,1)}, bf16[2,384,384]{2,1,0:T(8,128)(2,1)}, bf16[2,384,384]{2,1,0:T(8,128)(2,1)}) custom-call(bf16[4,384,512]{2,1,0:T(8,128)(2,1)} %get-tuple-element.114.grad_a, bf16[4,384,512]{2,1,0:T(8,128)(2,1)} %collective-permute-done.60.grad_b, ...), custom_call_target="tpu_custom_call" | custom-call | flops 2415919104 | bytes 9000000 | tf_op jit(solution)/shard_map/expand_terms/pallas_call | solution.py:1035
  337.9 11.6 %collective-permute-done.41 = bf16[2,400,384]{2,1,0:T(8,128)(2,1)S(1)} collective-permute-done((bf16[2,400,384]{2,1,0:T(8,128)(2,1)}, bf16[2,400,384]{2,1,0:T(8,128)(2,1)S(1)}, u32[]{:S(2)}, u32[]{:S(2)}) %collective-permute-start.41) | collective-permute-done | bytes 614432 | tf_op jit(solution)/shard_map/ppermute | solution.py:382
  365.8 7.1 %collective-permute-done.42 = bf16[400,384]{1,0:T(8,128)(2,1)S(1)} collective-permute-done((bf16[400,384]{1,0:T(8,128)(2,1)S(1)}, bf16[400,384]{1,0:T(8,128)(2,1)S(1)}, u32[]{:S(2)}, u32[]{:S(2)}) %collective-permute-start.42) | collective-permute-done | bytes 307232 | tf_op jit(solution)/shard_map/ppermute | solution.py:386
  410.3 10.4 %collective-permute-done.45 = bf16[784,384]{1,0:T(8,128)(2,1)S(1)} collective-permute-done((bf16[784,384]{1,0:T(8,128)(2,1)S(1)}, bf16[784,384]{1,0:T(8,128)(2,1)S(1)}, u32[]{:S(2)}, u32[]{:S(2)}) %collective-permute-start.45) | collective-permute-done | bytes 602144 | tf_op jit(solution)/shard_map/ppermute | solution.py:1125
  420.9 12.5 %collective-permute-done.75 = bf16[768,384]{1,0:T(8,128)(2,1)S(1)} collective-permute-done((bf16[768,384]{1,0:T(8,128)(2,1)S(1)}, bf16[768,384]{1,0:T(8,128)(2,1)S(1)}, u32[]{:S(2)}, u32[]{:S(2)}) %collective-permute-start.75) | collective-permute-done | bytes 589856 | tf_op jit(solution)/shard_map/ppermute | solution.py:1125
  433.5 9.3 %collective-permute-done.66 = bf16[768,384]{1,0:T(8,128)(2,1)S(1)} collective-permute-done((bf16[768,384]{1,0:T(8,128)(2,1)S(1)}, bf16[768,384]{1,0:T(8,128)(2,1)S(1)}, u32[]{:S(2)}, u32[]{:S(2)}) %collective-permute-start.66) | collective-permute-done | bytes 589856 | tf_op jit(solution)/shard_map/ppermute | solution.py:1125
  447.5 6.2 %reduce_terms.3 = (bf16[2,96,1536]{2,1,0:T(8,128)(2,1)}, bf16[2,96,1536]{2,1,0:T(8,128)(2,1)}, bf16[2,96,1536]{2,1,0:T(8,128)(2,1)}, bf16[2,96,1536]{2,1,0:T(8,128)(2,1)}) custom-call(bf16[4,96,512]{2,1,0:T(8,128)(2,1)} %get-tuple-element.134.grad_a, bf16[4,96,512]{2,1,0:T(8,128)(2,1)} %copy-done.44, ...), custom_call_target="tpu_custom_call" | custom-call | flops 2415919104 | bytes 12000000 | tf_op jit(solution)/shard_map/reduce_terms/pallas_call | solution.py:1015
  455.4 6.1 %reduce_terms.2 = (bf16[2,96,1536]{2,1,0:T(8,128)(2,1)}, bf16[2,96,1536]{2,1,0:T(8,128)(2,1)}, bf16[2,96,1536]{2,1,0:T(8,128)(2,1)}, bf16[2,96,1536]{2,1,0:T(8,128)(2,1)}) custom-call(bf16[4,96,512]{2,1,0:T(8,128)(2,1)} %get-tuple-element.128.grad_a, bf16[4,96,512]{2,1,0:T(8,128)(2,1)} %collective-permute-done.78.grad_b, ...), custom_call_target="tpu_custom_call" | custom-call | flops 2415919104 | bytes 12000000 | tf_op jit(solution)/shard_map/reduce_terms/pallas_call | solution.py:1015
  472.4 5.5 collective-permute-done.89
  482.1 5.5 collective-permute-done.80
  489.8 23.7 %collective-permute-done.59 = bf16[784,384]{1,0:T(8,128)(2,1)S(1)} collective-permute-done((bf16[784,384]{1,0:T(8,128)(2,1)S(1)}, bf16[784,384]{1,0:T(8,128)(2,1)S(1)}, u32[]{:S(2)}, u32[]{:S(2)}) %collective-permute-start.59) | collective-permute-done | bytes 602144 | tf_op jit(solution)/shard_map/ppermute | solution.py:1127
  514.6 11.8 %collective-permute-done.47 = bf16[784,384]{1,0:T(8,128)(2,1)S(1)} collective-permute-done((bf16[784,384]{1,0:T(8,128)(2,1)S(1)}, bf16[784,384]{1,0:T(8,128)(2,1)S(1)}, u32[]{:S(2)}, u32[]{:S(2)}) %collective-permute-start.47) | collective-permute-done | bytes 602144 | tf_op jit(solution)/shard_map/ppermute | solution.py:1127
  563.4 13.1 %collective-permute-done.95 = bf16[192,1536]{1,0:T(8,128)(2,1)S(1)} collective-permute-done((bf16[192,1536]{1,0:T(8,128)(2,1)S(1)}, bf16[192,1536]{1,0:T(8,128)(2,1)S(1)}, u32[]{:S(2)}, u32[]{:S(2)}) %collective-permute-start.95) | collective-permute-done | bytes 589856 | tf_op jit(solution)/shard_map/ppermute | solution.py:1127
  576.7 6.1 %collective-permute-done.86 = bf16[192,1536]{1,0:T(8,128)(2,1)S(1)} collective-permute-done((bf16[192,1536]{1,0:T(8,128)(2,1)S(1)}, bf16[192,1536]{1,0:T(8,128)(2,1)S(1)}, u32[]{:S(2)}, u32[]{:S(2)}) %collective-permute-start.86) | collective-permute-done | bytes 589856 | tf_op jit(solution)/shard_map/ppermute | solution.py:1127
  (555 shorter events, 219.9 us)
Async XLA Ops:
  11.5 27.0 %collective-permute-start.21 = (bf16[400,768]{1,0:T(8,128)(2,1)}, bf16[400,768]{1,0:T(8,128)(2,1)S(1)}, u32[]{:S(2)}, u32[]{:S(2)}) collective-permute-start(bf16[400,768]{1,0:T(8,128)(2,1)} %fusion.5.rest_0_), channel_id=1, source_target_pairs={{0,16},{4,20},{8,24},{12,28},{16,0},{20,4},{24,8},{28,12},{1,17},{... | collective-permute-start | bytes 1843208 | tf_op jit(solution)/shard_map/ppermute | solution.py:386
  17.4 46.4 %collective-permute-start.10 = (bf16[768,768]{1,0:T(8,128)(2,1)}, bf16[768,768]{1,0:T(8,128)(2,1)S(1)}, u32[]{:S(2)}, u32[]{:S(2)}) collective-permute-start(bf16[768,768]{1,0:T(8,128)(2,1)} %slice_dynamic-update-slice_fusion.4.rest_0_.rest_10_), channel_id=1, source_target_pairs={{0,16},{4,20},{8,24},{12,28},{16,0},{20,4},{24,8},{28,12},{1,17},{... | collective-permute-start | bytes 3538952 | tf_op jit(solution)/shard_map/ppermute | solution.py:386
  23.5 40.4 %collective-permute-start.9 = (bf16[768,768]{1,0:T(8,128)(2,1)}, bf16[768,768]{1,0:T(8,128)(2,1)}, u32[]{:S(2)}, u32[]{:S(2)}) collective-permute-start(bf16[768,768]{1,0:T(8,128)(2,1)} %slice_dynamic-update-slice_fusion.4.rest_0_.rest_10_), channel_id=1, source_target_pairs={{0,8},{4,12},{8,0},{12,4},{16,24},{20,28},{24,16},{28,20},{1,9},{5... | collective-permute-start | bytes 3538952 | tf_op jit(solution)/shard_map/ppermute | solution.py:382
  36.6 52.6 %collective-permute-start.27 = (bf16[768,768]{1,0:T(8,128)(2,1)}, bf16[768,768]{1,0:T(8,128)(2,1)S(1)}, u32[]{:S(2)}, u32[]{:S(2)}) collective-permute-start(bf16[768,768]{1,0:T(8,128)(2,1)} %slice_dynamic-update-slice_fusion.rest_0_.rest_10_), channel_id=1, source_target_pairs={{0,8},{4,12},{8,0},{12,4},{16,24},{20,28},{24,16},{28,20},{1,9},{5... | collective-permute-start | bytes 3538952 | tf_op jit(solution)/shard_map/ppermute | solution.py:382
  39.4 49.7 %collective-permute-start.28 = (bf16[768,768]{1,0:T(8,128)(2,1)}, bf16[768,768]{1,0:T(8,128)(2,1)S(1)}, u32[]{:S(2)}, u32[]{:S(2)}) collective-permute-start(bf16[768,768]{1,0:T(8,128)(2,1)} %slice_dynamic-update-slice_fusion.rest_0_.rest_10_), channel_id=1, source_target_pairs={{0,16},{4,20},{8,24},{12,28},{16,0},{20,4},{24,8},{28,12},{1,17},{... | collective-permute-start | bytes 3538952 | tf_op jit(solution)/shard_map/ppermute | solution.py:386
  47.3 44.0 %collective-permute-start.2 = (bf16[400,768]{1,0:T(8,128)(2,1)}, bf16[400,768]{1,0:T(8,128)(2,1)S(1)}, u32[]{:S(2)}, u32[]{:S(2)}) collective-permute-start(bf16[400,768]{1,0:T(8,128)(2,1)} %collective-permute-done.1.rest_1_), channel_id=1, source_target_pairs={{0,4},{4,0},{8,12},{12,8},{16,20},{20,16},{24,28},{28,24},{1,5},{5... | collective-permute-start | bytes 1843208 | tf_op jit(solution)/shard_map/ppermute | solution.py:378
  63.8 28.3 %collective-permute-start.20 = (bf16[400,768]{1,0:T(8,128)(2,1)S(1)}, bf16[400,768]{1,0:T(8,128)(2,1)S(1)}, u32[]{:S(2)}, u32[]{:S(2)}) collective-permute-start(bf16[400,768]{1,0:T(8,128)(2,1)S(1)} %copy-done.47), channel_id=1, source_target_pairs={{0,4},{4,0},{8,12},{12,8},{16,20},{20,16},{24,28},{28,24},{1,5},{5... | collective-permute-start | bytes 1843208 | tf_op jit(solution)/shard_map/ppermute | solution.py:378
  63.9 39.2 %collective-permute-start.5 = (bf16[208,768]{1,0:T(8,128)(2,1)S(1)}, bf16[208,768]{1,0:T(8,128)(2,1)S(1)}, u32[]{:S(2)}, u32[]{:S(2)}) collective-permute-start(bf16[208,768]{1,0:T(8,128)(2,1)S(1)} %slice.655), channel_id=1, source_target_pairs={{0,16},{4,20},{8,24},{12,28},{16,0},{20,4},{24,8},{28,12},{1,17},{... | collective-permute-start | bytes 958472 | tf_op jit(solution)/shard_map/ppermute | solution.py:386
  106.2 29.4 %collective-permute-start.14 = (bf16[768,768]{1,0:T(8,128)(2,1)}, bf16[768,768]{1,0:T(8,128)(2,1)S(1)}, u32[]{:S(2)}, u32[]{:S(2)}) collective-permute-start(bf16[768,768]{1,0:T(8,128)(2,1)} %collective-permute-done.9.rest_1_.rest_11_), channel_id=1, source_target_pairs={{0,4},{4,0},{8,12},{12,8},{16,20},{20,16},{24,28},{28,24},{1,5},{5... | collective-permute-start | bytes 3538952 | tf_op jit(solution)/shard_map/ppermute | solution.py:378
  107.0 29.2 %collective-permute-start.15 = (bf16[768,768]{1,0:T(8,128)(2,1)S(1)}, bf16[768,768]{1,0:T(8,128)(2,1)S(1)}, u32[]{:S(2)}, u32[]{:S(2)}) collective-permute-start(bf16[768,768]{1,0:T(8,128)(2,1)S(1)} %collective-permute-done.10.rest_2_.rest_12_), channel_id=1, source_target_pairs={{0,4},{4,0},{8,12},{12,8},{16,20},{20,16},{24,28},{28,24},{1,5},{5... | collective-permute-start | bytes 3538952 | tf_op jit(solution)/shard_map/ppermute | solution.py:378
  123.3 32.9 %collective-permute-start.16 = (bf16[384,768]{1,0:T(8,128)(2,1)}, bf16[384,768]{1,0:T(8,128)(2,1)}, u32[]{:S(2)}, u32[]{:S(2)}) collective-permute-start(bf16[384,768]{1,0:T(8,128)(2,1)} %collective-permute-done.11.rest_3_.rest_13_), channel_id=1, source_target_pairs={{0,4},{4,0},{8,12},{12,8},{16,20},{20,16},{24,28},{28,24},{1,5},{5... | collective-permute-start | bytes 1769480 | tf_op jit(solution)/shard_map/ppermute | solution.py:378
  135.6 52.7 %collective-permute-start.31 = (bf16[768,768]{1,0:T(8,128)(2,1)}, bf16[768,768]{1,0:T(8,128)(2,1)}, u32[]{:S(2)}, u32[]{:S(2)}) collective-permute-start(bf16[768,768]{1,0:T(8,128)(2,1)} %slice_dynamic-update-slice_fusion.rest_0_.rest_10_), channel_id=1, source_target_pairs={{0,4},{4,0},{8,12},{12,8},{16,20},{20,16},{24,28},{28,24},{1,5},{5... | collective-permute-start | bytes 3538952 | tf_op jit(solution)/shard_map/ppermute | solution.py:378
  135.6 53.2 %collective-permute-start.32 = (bf16[768,768]{1,0:T(8,128)(2,1)S(1)}, bf16[768,768]{1,0:T(8,128)(2,1)}, u32[]{:S(2)}, u32[]{:S(2)}) collective-permute-start(bf16[768,768]{1,0:T(8,128)(2,1)S(1)} %collective-permute-done.27.rest_1_.rest_11_), channel_id=1, source_target_pairs={{0,4},{4,0},{8,12},{12,8},{16,20},{20,16},{24,28},{28,24},{1,5},{5... | collective-permute-start | bytes 3538952 | tf_op jit(solution)/shard_map/ppermute | solution.py:378
  136.2 52.7 %collective-permute-start.33 = (bf16[768,768]{1,0:T(8,128)(2,1)S(1)}, bf16[768,768]{1,0:T(8,128)(2,1)S(1)}, u32[]{:S(2)}, u32[]{:S(2)}) collective-permute-start(bf16[768,768]{1,0:T(8,128)(2,1)S(1)} %collective-permute-done.28.rest_2_.rest_12_), channel_id=1, source_target_pairs={{0,4},{4,0},{8,12},{12,8},{16,20},{20,16},{24,28},{28,24},{1,5},{5... | collective-permute-start | bytes 3538952 | tf_op jit(solution)/shard_map/ppermute | solution.py:378
  156.3 32.6 %collective-permute-start.34 = (bf16[384,768]{1,0:T(8,128)(2,1)S(1)}, bf16[384,768]{1,0:T(8,128)(2,1)S(1)}, u32[]{:S(2)}, u32[]{:S(2)}) collective-permute-start(bf16[384,768]{1,0:T(8,128)(2,1)S(1)} %copy-done.10), channel_id=1, source_target_pairs={{0,4},{4,0},{8,12},{12,8},{16,20},{20,16},{24,28},{28,24},{1,5},{5... | collective-permute-start | bytes 1769480 | tf_op jit(solution)/shard_map/ppermute | solution.py:378
  156.8 32.1 %collective-permute-start.35 = (bf16[384,768]{1,0:T(8,128)(2,1)S(1)}, bf16[384,768]{1,0:T(8,128)(2,1)S(1)}, u32[]{:S(2)}, u32[]{:S(2)}) collective-permute-start(bf16[384,768]{1,0:T(8,128)(2,1)S(1)} %copy-done.12), channel_id=1, source_target_pairs={{0,4},{4,0},{8,12},{12,8},{16,20},{20,16},{24,28},{28,24},{1,5},{5... | collective-permute-start | bytes 1769480 | tf_op jit(solution)/shard_map/ppermute | solution.py:378
  188.3 94.4 %collective-permute-start.37 = (bf16[512,768]{1,0:T(8,128)(2,1)}, bf16[512,768]{1,0:T(8,128)(2,1)}, u32[]{:S(2)}, u32[]{:S(2)}) collective-permute-start(bf16[512,768]{1,0:T(8,128)(2,1)} %get-tuple-element.92.normed_a), channel_id=1, source_target_pairs={{0,4},{4,0},{8,12},{12,8},{16,20},{20,16},{24,28},{28,24},{1,5},{5... | collective-permute-start | bytes 2359304 | tf_op jit(solution)/shard_map/ppermute | solution.py:378
  188.8 94.0 %collective-permute-start.39 = (bf16[512,768]{1,0:T(8,128)(2,1)}, bf16[512,768]{1,0:T(8,128)(2,1)}, u32[]{:S(2)}, u32[]{:S(2)}) collective-permute-start(bf16[512,768]{1,0:T(8,128)(2,1)} %get-tuple-element.95.mixed_a), channel_id=1, source_target_pairs={{0,4},{4,0},{8,12},{12,8},{16,20},{20,16},{24,28},{28,24},{1,5},{5... | collective-permute-start | bytes 2359304 | tf_op jit(solution)/shard_map/ppermute | solution.py:378
  259.5 35.8 %collective-permute-start.48 = (bf16[3,4,96,512]{3,2,1,0:T(8,128)(2,1)}, bf16[3,4,96,512]{3,2,1,0:T(8,128)(2,1)}, u32[]{:S(2)}, u32[]{:S(2)}) collective-permute-start(bf16[3,4,96,512]{3,2,1,0:T(8,128)(2,1)} %get-tuple-element.103), channel_id=1, source_target_pairs={{0,4},{4,0},{8,12},{12,8},{16,20},{20,16},{24,28},{28,24},{1,5},{5... | collective-permute-start | bytes 3538952 | tf_op jit(solution)/shard_map/ppermute | solution.py:378
  285.3 26.9 %collective-permute-start.69 = (bf16[4,384,512]{2,1,0:T(8,128)(2,1)S(1)}, bf16[4,384,512]{2,1,0:T(8,128)(2,1)}, u32[]{:S(2)}, u32[]{:S(2)}) collective-permute-start(bf16[4,384,512]{2,1,0:T(8,128)(2,1)S(1)} %copy-done.78), channel_id=1, source_target_pairs={{0,4},{4,0},{8,12},{12,8},{16,20},{20,16},{24,28},{28,24},{1,5},{5... | collective-permute-start | bytes 4718600 | tf_op jit(solution)/shard_map/ppermute | solution.py:378
  286.4 33.0 %collective-permute-start.60 = (bf16[4,384,512]{2,1,0:T(8,128)(2,1)S(1)}, bf16[4,384,512]{2,1,0:T(8,128)(2,1)}, u32[]{:S(2)}, u32[]{:S(2)}) collective-permute-start(bf16[4,384,512]{2,1,0:T(8,128)(2,1)S(1)} %copy-done.79), channel_id=1, source_target_pairs={{0,4},{4,0},{8,12},{12,8},{16,20},{20,16},{24,28},{28,24},{1,5},{5... | collective-permute-start | bytes 4718600 | tf_op jit(solution)/shard_map/ppermute | solution.py:378
  312.1 134.7 %collective-permute-start.88 = (bf16[512,3072]{1,0:T(8,128)(2,1)S(1)}, bf16[512,3072]{1,0:T(8,128)(2,1)}, u32[]{:S(2)}, u32[]{:S(2)}) collective-permute-start(bf16[512,3072]{1,0:T(8,128)(2,1)S(1)} %copy-done.1), channel_id=1, source_target_pairs={{0,4},{4,0},{8,12},{12,8},{16,20},{20,16},{24,28},{28,24},{1,5},{5... | collective-permute-start | bytes 9437192 | tf_op jit(solution)/shard_map/ppermute | solution.py:378
  319.3 135.1 %collective-permute-start.79 = (bf16[512,3072]{1,0:T(8,128)(2,1)S(1)}, bf16[512,3072]{1,0:T(8,128)(2,1)}, u32[]{:S(2)}, u32[]{:S(2)}) collective-permute-start(bf16[512,3072]{1,0:T(8,128)(2,1)S(1)} %copy-done), channel_id=1, source_target_pairs={{0,4},{4,0},{8,12},{12,8},{16,20},{20,16},{24,28},{28,24},{1,5},{5... | collective-permute-start | bytes 9437192 | tf_op jit(solution)/shard_map/ppermute | solution.py:378
  332.2 42.1 %collective-permute-start.73 = (bf16[2,384,384]{2,1,0:T(8,128)(2,1)}, bf16[2,384,384]{2,1,0:T(8,128)(2,1)S(1)}, u32[]{:S(2)}, u32[]{:S(2)}) collective-permute-start(bf16[2,384,384]{2,1,0:T(8,128)(2,1)} %get-tuple-element.127), channel_id=1, source_target_pairs={{0,16},{4,20},{8,24},{12,28},{16,0},{20,4},{24,8},{28,12},{1,17},{... | collective-permute-start | bytes 1769480 | tf_op jit(solution)/shard_map/ppermute | solution.py:386
  377.9 30.7 %collective-permute-start.57 = (bf16[784,384]{1,0:T(8,128)(2,1)S(1)}, bf16[784,384]{1,0:T(8,128)(2,1)S(1)}, u32[]{:S(2)}, u32[]{:S(2)}) collective-permute-start(bf16[784,384]{1,0:T(8,128)(2,1)S(1)} %pad_maximum_fusion.4), channel_id=1, source_target_pairs={{0,1},{3,2},{4,5},{7,6},{8,9},{11,10},{12,13},{15,14},{16,17},{19,... | collective-permute-start | bytes 1806344 | tf_op jit(solution)/shard_map/ppermute | solution.py:1125
  406.9 26.5 %collective-permute-start.75 = (bf16[768,384]{1,0:T(8,128)(2,1)S(1)}, bf16[768,384]{1,0:T(8,128)(2,1)S(1)}, u32[]{:S(2)}, u32[]{:S(2)}) collective-permute-start(bf16[768,384]{1,0:T(8,128)(2,1)S(1)} %pad_maximum_fusion.7), channel_id=1, source_target_pairs={{0,1},{3,2},{4,5},{7,6},{8,9},{11,10},{12,13},{15,14},{16,17},{19,... | collective-permute-start | bytes 1769480 | tf_op jit(solution)/shard_map/ppermute | solution.py:1125
  408.7 34.1 %collective-permute-start.66 = (bf16[768,384]{1,0:T(8,128)(2,1)S(1)}, bf16[768,384]{1,0:T(8,128)(2,1)S(1)}, u32[]{:S(2)}, u32[]{:S(2)}) collective-permute-start(bf16[768,384]{1,0:T(8,128)(2,1)S(1)} %pad_maximum_fusion.6), channel_id=1, source_target_pairs={{0,1},{3,2},{4,5},{7,6},{8,9},{11,10},{12,13},{15,14},{16,17},{19,... | collective-permute-start | bytes 1769480 | tf_op jit(solution)/shard_map/ppermute | solution.py:1125
  467.5 46.0 %collective-permute-start.59 = (bf16[784,384]{1,0:T(8,128)(2,1)S(1)}, bf16[784,384]{1,0:T(8,128)(2,1)S(1)}, u32[]{:S(2)}, u32[]{:S(2)}) collective-permute-start(bf16[784,384]{1,0:T(8,128)(2,1)S(1)} %add_convert_fusion), channel_id=1, source_target_pairs={{1,0},{2,3},{5,4},{6,7},{9,8},{10,11},{13,12},{14,15},{17,16},{18,... | collective-permute-start | bytes 1806344 | tf_op jit(solution)/shard_map/ppermute | solution.py:1127
  470.3 56.1 %collective-permute-start.47 = (bf16[784,384]{1,0:T(8,128)(2,1)S(1)}, bf16[784,384]{1,0:T(8,128)(2,1)S(1)}, u32[]{:S(2)}, u32[]{:S(2)}) collective-permute-start(bf16[784,384]{1,0:T(8,128)(2,1)S(1)} %add_convert_fusion.2), channel_id=1, source_target_pairs={{1,0},{2,3},{5,4},{6,7},{9,8},{10,11},{13,12},{14,15},{17,16},{18,... | collective-permute-start | bytes 1806344 | tf_op jit(solution)/shard_map/ppermute | solution.py:1127
  477.9 68.3 %collective-permute-start.77 = (bf16[768,384]{1,0:T(8,128)(2,1)S(1)}, bf16[768,384]{1,0:T(8,128)(2,1)}, u32[]{:S(2)}, u32[]{:S(2)}) collective-permute-start(bf16[768,384]{1,0:T(8,128)(2,1)S(1)} %add_convert_fusion.8), channel_id=1, source_target_pairs={{1,0},{2,3},{5,4},{6,7},{9,8},{10,11},{13,12},{14,15},{17,16},{18,... | collective-permute-start | bytes 1769480 | tf_op jit(solution)/shard_map/ppermute | solution.py:1127
  480.0 67.6 %collective-permute-start.68 = (bf16[768,384]{1,0:T(8,128)(2,1)S(1)}, bf16[768,384]{1,0:T(8,128)(2,1)}, u32[]{:S(2)}, u32[]{:S(2)}) collective-permute-start(bf16[768,384]{1,0:T(8,128)(2,1)S(1)} %add_convert_fusion.10), channel_id=1, source_target_pairs={{1,0},{2,3},{5,4},{6,7},{9,8},{10,11},{13,12},{14,15},{17,16},{18,... | collective-permute-start | bytes 1769480 | tf_op jit(solution)/shard_map/ppermute | solution.py:1127
  487.6 50.2 %collective-permute-start.92 = (bf16[96,1536]{1,0:T(8,128)(2,1)}, bf16[96,1536]{1,0:T(8,128)(2,1)}, u32[]{:S(2)}, u32[]{:S(2)}) collective-permute-start(bf16[96,1536]{1,0:T(8,128)(2,1)} %fusion.29), channel_id=1, source_target_pairs={{0,8},{4,12},{8,0},{12,4},{16,24},{20,28},{24,16},{28,20},{1,9},{5... | collective-permute-start | bytes 884744 | tf_op jit(solution)/shard_map/ppermute | solution.py:382
  (159 other events, 2018.0 us)

commit v2 on v1

--- a/solution.py
+++ b/solution.py
@@ -364,6 +364,7 @@
 f32 = jnp.float32
 bf16 = jnp.bfloat16
 VMEM_BYTES = 56 * 1024 * 1024
+SMALL_VMEM_BYTES = 24 * 1024 * 1024
 
 
 def dot_nt(left, right):
@@ -386,37 +387,36 @@
     return lax.ppermute(value, "fsdp", [(at, at ^ 4) for at in range(8)])
 
 
-def gather_pack(own, cut):
-    along_x = swap_x(own)
-    along_y = swap_y(own)
-    across_low = swap_x(along_y[:cut])
-    across_high = swap_y(along_x[cut:])
-    even = (own, along_x, along_y, across_low, across_high)
-    return even + tuple(swap_core(piece) for piece in even)
-
-
-def piece_plan(cut, first, count):
-    plan = []
-    for odd in range(2):
-        for place, delta in ((0, 0), (1, 2), (2, 4)):
-            plan.append((5 * odd + place, first, count, delta ^ odd, 0))
-        low = min(max(cut - first, 0), count)
-        if low > 0:
-            plan.append((5 * odd + 3, first, low, 6 ^ odd, 0))
-        if low < count:
-            plan.append((5 * odd + 4, first + low - cut, count - low, 6 ^ odd, low))
-    return plan
-
-
-def block_copies(place, refs, plan, block, sems):
+PIECES = 10
+
+
+def regions_of(rows, cut, x_row, y_row):
     return [
-        pltpu.make_async_copy(
-            refs[array_at].at[pl.ds(row, count)],
-            block.at[place ^ delta, pl.ds(into, count)],
-            sems.at[at],
+        region
+        for odd in range(2)
+        for region in (
+            (5 * odd, odd, 0, rows, 0),
+            (5 * odd + 1, 2 ^ odd, 0, rows, x_row),
+            (5 * odd + 2, 4 ^ odd, 0, rows, y_row),
+            (5 * odd + 3, 6 ^ odd, 0, cut, 0),
+            (5 * odd + 4, 6 ^ odd, cut, rows, 0),
         )
-        for at, (array_at, row, count, delta, into) in enumerate(plan)
     ]
+
+
+def block_copies(place, refs, regions, first, count, block, sems):
+    copies = []
+    for array_at, delta, low, high, start in regions:
+        begin, end = max(low, first), min(high, first + count)
+        if begin < end:
+            copies.append(
+                pltpu.make_async_copy(
+                    refs[array_at].at[pl.ds(start + begin - low, end - begin)],
+                    block.at[place ^ delta, pl.ds(begin - first, end - begin)],
+                    sems.at[len(copies)],
+                )
+            )
+    return copies
 
 
 def run_all(copies, what):
@@ -438,8 +438,8 @@
     )
 
 
-def cost(flops, moved):
-    return pl.CostEstimate(flops=int(flops), bytes_accessed=int(moved), transcendentals=0)
+def cost(micros):
+    return pl.CostEstimate(flops=int(micros * 1.1e9), bytes_accessed=1 << 10, transcendentals=0)
 
 
 def rows_spec(width):
@@ -456,27 +456,248 @@
     return centre * root, root
 
 
+def own_copies(sources, target, sems, kind, layer):
+    if kind == "attn":
+        heads, merge = sources[:2]
+        pairs = [(heads.at[layer, at], target.at[pl.ds(96 * at, 96)]) for at in range(3)]
+        pairs.append((merge.at[layer], target.at[pl.ds(288, 96)]))
+    else:
+        expand, reduce = sources[2:]
+        pairs = [(expand.at[layer], target.at[pl.ds(0, 384)])]
+        for part in range(FF_PARTS):
+            pairs.append(
+                (
+                    reduce.at[layer, :, pl.ds(WIDTH * part, WIDTH)],
+                    target.at[pl.ds(384 + 96 * part, 96)],
+                )
+            )
+    return [pltpu.make_async_copy(*pair, sems.at[at]) for at, pair in enumerate(pairs)]
+
+
+def own_packs(wanted, matrices, vectors):
+    count = len(wanted)
+
+    def kernel(*refs):
+        sources, vector_refs = refs[:4], refs[4:12]
+        outs = refs[12 : 12 + count]
+        rows, low_rows, sems, vector_sems = refs[12 + count :]
+        copies = []
+        for at, (kind, layer) in enumerate(wanted):
+            copies += own_copies(sources, outs[at], sems.at[at], kind, layer)
+        run_all(copies, "start")
+        vector_copies = []
+        for at, (kind, layer) in enumerate(wanted):
+            if kind == "attn":
+                rows[...] = jnp.zeros_like(rows)
+                rows[0:2, 0:96] = vector_refs[0][layer].astype(f32)
+                for row in range(2, 8):
+                    values = vector_refs[row - 1][...].astype(f32)
+                    rows[row : row + 1, 0:96] = values[layer : layer + 1]
+                rows[8:9, 0:384] = vector_refs[7][...].astype(f32)[layer : layer + 1]
+                low_rows[at] = rows[...].astype(bf16)
+                vector_copies.append(
+                    pltpu.make_async_copy(
+                        low_rows.at[at], outs[at].at[pl.ds(384, 16)], vector_sems.at[at]
+                    )
+                )
+        run_all(vector_copies, "start")
+        run_all(copies + vector_copies, "wait")
+
+    return pl.pallas_call(
+        kernel,
+        in_specs=[in_any()] * 4 + [pl.BlockSpec(memory_space=pltpu.VMEM)] * 8,
+        out_specs=[in_any()] * count,
+        out_shape=[
+            jax.ShapeDtypeStruct((400 if kind == "attn" else 768, WIDTH), bf16)
+            for kind, layer in wanted
+        ],
+        scratch_shapes=[
+            pltpu.VMEM((16, WIDTH), f32),
+            pltpu.VMEM((count, 16, WIDTH), bf16),
+            pltpu.SemaphoreType.DMA((count, 5)),
+            pltpu.SemaphoreType.DMA((count,)),
+        ],
+        compiler_params=pltpu.CompilerParams(vmem_limit_bytes=SMALL_VMEM_BYTES),
+        cost_estimate=cost(0.01),
+        name="own_packs",
+    )(*matrices, *vectors)
+
+
+def join_rows(pieces_of):
+    flat = [piece for pieces in pieces_of for piece in pieces]
+    heights = [sum(rows for unused, unused_first, rows in pieces) for pieces in pieces_of]
+
+    def kernel(*refs):
+        ins, outs, sems = refs[: len(flat)], refs[len(flat) : -1], refs[-1]
+        copies = []
+        for out, pieces in zip(outs, pieces_of):
+            into = 0
+            for unused, first, rows in pieces:
+                at = len(copies)
+                copies.append(
+                    pltpu.make_async_copy(
+                        ins[at].at[pl.ds(first, rows)], out.at[pl.ds(into, rows)], sems.at[at]
+                    )
+                )
+                into += rows
+        run_all(copies, "start")
+        run_all(copies, "wait")
+
+    return pl.pallas_call(
+        kernel,
+        in_specs=[in_any()] * len(flat),
+        out_specs=[in_any()] * len(heights),
+        out_shape=[jax.ShapeDtypeStruct((rows, WIDTH), bf16) for rows in heights],
+        scratch_shapes=[pltpu.SemaphoreType.DMA((len(flat),))],
+        compiler_params=pltpu.CompilerParams(vmem_limit_bytes=SMALL_VMEM_BYTES),
+        cost_estimate=cost(0.01),
+        name="join_rows",
+    )(*[array for array, unused, unused_rows in flat])
+
+
+def gathered_vectors(place, pack):
+    arrays, regions = pack
+    used = {}
+    for array_at, delta, low, high, start in regions:
+        if low <= 384 and 400 <= high:
+            used[delta] = (arrays[array_at], start + 384 - low)
+    deltas = sorted(used)
+
+    def kernel(place_ref, *refs):
+        ins, small_ref, expand_ref, rows, sems = refs[:8], refs[8], refs[9], refs[10], refs[11]
+        copies = [
+            pltpu.make_async_copy(
+                ins[at].at[pl.ds(used[delta][1], 16)], rows.at[at], sems.at[at]
+            )
+            for at, delta in enumerate(deltas)
+        ]
+        run_all(copies, "start")
+        here = place_ref[0]
+        row = lax.broadcasted_iota(jnp.int32, (1024, WIDTH), 0)
+        column = lax.broadcasted_iota(jnp.int32, (1024, WIDTH), 1)
+        at = row & 127
+        wanted = 96 * ((row >> 7) ^ here) + at
+        chosen = jnp.where((column == wanted) & (at < 96), 1.0, 0.0).astype(bf16)
+        run_all(copies, "wait")
+        flat = jnp.concatenate([rows[at, 0:8, 0:128].astype(f32) for at in range(8)], axis=1)
+        small_ref[...] = dot_nn(flat.astype(bf16), chosen)
+        for at, delta in enumerate(deltas):
+            owner = here ^ delta
+            line = rows[at].astype(f32)[8:9, 0:384]
+
+            @pl.when((owner & 1) == 0)
+            def left():
+                expand_ref[owner >> 1, :, 0:384] = line
+
+            @pl.when((owner & 1) == 1)
+            def right():
+                expand_ref[owner >> 1, :, 384:768] = line
+
+    shape = jax.ShapeDtypeStruct
+    return pl.pallas_call(
+        kernel,
+        in_specs=[in_smem()] + [in_any()] * 8,
+        out_specs=[pl.BlockSpec(memory_space=pltpu.VMEM)] * 2,
+        out_shape=[shape((8, WIDTH), f32), shape((4, 1, WIDTH), f32)],
+        scratch_shapes=[pltpu.VMEM((8, 16, WIDTH), bf16), pltpu.SemaphoreType.DMA((8,))],
+        compiler_params=pltpu.CompilerParams(vmem_limit_bytes=SMALL_VMEM_BYTES),
+        cost_estimate=cost(0.01),
+        name="gathered_vectors",
+    )(place, *[used[delta][0] for delta in deltas])
+
+
+def elementwise(name, body, ins, out_shapes):
+    def kernel(*refs):
+        body(refs[: len(ins)], refs[len(ins) :])
+
+    return pl.pallas_call(
+        kernel,
+        in_specs=[pl.BlockSpec(memory_space=pltpu.VMEM)] * len(ins),
+        out_specs=[pl.BlockSpec(memory_space=pltpu.VMEM)] * len(out_shapes),
+        out_shape=[jax.ShapeDtypeStruct(shape, bf16) for shape in out_shapes],
+        compiler_params=pltpu.CompilerParams(vmem_limit_bytes=SMALL_VMEM_BYTES),
+        cost_estimate=cost(0.01),
+        name=name,
+    )(*ins)
+
+
+def add_low(*parts):
+    total = parts[0].astype(f32)
+    for part in parts[1:]:
+        total = total + part.astype(f32)
+    return total.astype(bf16)
+
+
+def first_steps(travel):
+    go_x, go_y, stay_x, stay_y = travel
+    return swap_x(go_x), swap_y(go_y), stay_x, stay_y
+
+
+def second_steps(state):
+    def body(ins, outs):
+        from_x, from_y, stay_x, stay_y = ins
+        outs[0][...] = add_low(stay_x[1], from_x[1])
+        outs[1][...] = add_low(stay_y[1], from_y[1])
+        outs[2][...] = add_low(stay_x[0], from_x[0])
+        outs[3][...] = add_low(stay_y[0], from_y[0])
+
+    low, high = state[0].shape[1:], state[1].shape[1:]
+    low_on, high_on, kept_low, kept_high = elementwise(
+        "second_steps", body, state, [low, high, low, high]
+    )
+    return swap_y(low_on), swap_x(high_on), kept_low, kept_high
+
+
+def ends(state):
+    from_y, from_x, kept_low, kept_high = state
+    low, high = kept_low.shape[0], kept_high.shape[0]
+
+    def body(ins, outs):
+        outs[0][0:low] = add_low(ins[2][...], ins[0][...])
+        outs[0][low : low + high] = add_low(ins[3][...], ins[1][...])
+
+    return elementwise("ends", body, state, [(low + high, WIDTH // 2)])[0]
+
+
+def to_middle(part):
+    return part, lax.ppermute(part, "rep", [(0, 1), (3, 2)])
+
+
+def plus(parts):
+    def body(ins, outs):
+        outs[0][...] = add_low(ins[0][...], ins[1][...])
+
+    return elementwise("plus", body, parts, [parts[0].shape])[0]
+
+
+def across_middle(parts):
+    inward = plus(parts)
+    return inward, lax.ppermute(inward, "rep", [(1, 2), (2, 1)])
+
+
+def to_ends(parts):
+    total = plus(parts)
+    return total, lax.ppermute(total, "rep", [(1, 0), (2, 3)])
+
+
 SM_HB0, SM_HB1, SM_MB, SM_G1, SM_S1, SM_G2, SM_S2, SM_RB = range(8)
 
 
-def attn_forward(place, hidden, small, pack, cut):
-    plans = [piece_plan(cut, 96 * at, 96) for at in range(4)]
-    copies_in_all = sum(len(plan) for plan in plans)
+def heads_copies(place_now, packs, regions, blocks, sems):
+    return [
+        block_copies(place_now, packs, regions, 96 * at, 96, blocks.at[at], sems.at[at])
+        for at in range(4)
+    ]
+
+
+def attn_forward(place, hidden, small, pack):
 
     def kernel(place_ref, hidden_ref, small_ref, *rest):
-        packs = rest[:10]
-        middle_ref, normed_ref, qkv_ref, mixed_ref, blocks, sems = rest[10:]
+        packs = rest[:PIECES]
+        middle_ref, normed_ref, qkv_ref, mixed_ref, blocks, sems = rest[PIECES:]
         place_now = place_ref[0]
         image = pl.program_id(0)
-        copies = []
-        at = 0
-        for member, plan in enumerate(plans):
-            copies.append(
-                block_copies(
-                    place_now, packs, plan, blocks.at[member], sems.at[pl.ds(at, len(plan))]
-                )
-            )
-            at += len(plan)
+        copies = heads_copies(place_now, packs, pack[1], blocks, sems)
 
         @pl.when(image == 0)
         def begin():
@@ -524,7 +745,7 @@
     return pl.pallas_call(
         kernel,
         grid=(tokens // ROWS,),
-        in_specs=[in_smem(), rows_spec(WIDTH), fixed(small.shape)] + [in_any()] * 10,
+        in_specs=[in_smem(), rows_spec(WIDTH), fixed(small.shape)] + [in_any()] * PIECES,
         out_specs=[rows_spec(WIDTH), rows_spec(WIDTH), rows_spec(3 * WIDTH), rows_spec(WIDTH)],
         out_shape=[
             shape((tokens, WIDTH), f32),
@@ -534,22 +755,21 @@
         ],
         scratch_shapes=[
             pltpu.VMEM((4, 8, 96, WIDTH), bf16),
-            pltpu.SemaphoreType.DMA((copies_in_all,)),
+            pltpu.SemaphoreType.DMA((4, PIECES)),
         ],
         compiler_params=params(),
-        cost_estimate=cost(8 * tokens * WIDTH * WIDTH * 1.5, 12e6),
+        cost_estimate=cost(0.01),
         name="attn_forward",
-    )(place, hidden, small, *pack)
-
-
-def expand_forward(place, middle, small, expand_bias, pack, cut, first):
-    plan = piece_plan(cut, first, 384)
+    )(place, hidden, small, *pack[0])
+
+
+def expand_forward(place, middle, small, expand_bias, pack, first):
 
     def kernel(place_ref, middle_ref, small_ref, bias_ref, *rest):
-        packs = rest[:10]
-        normed_ref, active_ref, slope_ref, block, sems = rest[10:]
+        packs = rest[:PIECES]
+        normed_ref, active_ref, slope_ref, block, sems = rest[PIECES:]
         image = pl.program_id(0)
-        copies = block_copies(place_ref[0], packs, plan, block, sems)
+        copies = block_copies(place_ref[0], packs, pack[1], first, 384, block, sems)
 
         @pl.when(image == 0)
         def begin():
@@ -565,7 +785,7 @@
 
         for part in range(FF_PARTS):
             weight = block[2 * part : 2 * part + 2].reshape(WIDTH, WIDTH)
-            point = dot_nt(normed, weight) + bias_ref[part : part + 1]
+            point = dot_nt(normed, weight) + bias_ref[part]
             square = point * point
             slant = jnp.tanh(0.7978845608028654 * point * (1.0 + 0.044715 * square))
             upper = 0.5 + 0.5 * slant
@@ -586,7 +806,7 @@
             fixed(small.shape),
             fixed(expand_bias.shape),
         ]
-        + [in_any()] * 10,
+        + [in_any()] * PIECES,
         out_specs=[rows_spec(WIDTH), rows_spec(hidden_units), rows_spec(hidden_units)],
         out_shape=[
             shape((tokens, WIDTH), bf16),
@@ -595,40 +815,43 @@
         ],
         scratch_shapes=[
             pltpu.VMEM((8, 384, WIDTH), bf16),
-            pltpu.SemaphoreType.DMA((len(plan),)),
+            pltpu.SemaphoreType.DMA((PIECES,)),
         ],
         compiler_params=params(),
-        cost_estimate=cost(8 * tokens * WIDTH * WIDTH, 14e6),
+        cost_estimate=cost(0.01),
         name="expand_forward",
-    )(place, middle, small, expand_bias, *pack)
-
-
-def reduce_plans(cut, first):
-    return [piece_plan(cut, first + 96 * part, 96) for part in range(FF_PARTS)]
-
-
-def reduce_forward(place, live, middle, active, small, pack, cut, first, last):
-    plans = reduce_plans(cut, first)
-    copies_in_all = sum(len(plan) for plan in plans)
+    )(place, middle, small, expand_bias, *pack[0])
+
+
+def reduce_copies(place_now, packs, regions, first, blocks, sems):
+    return [
+        block_copies(
+            place_now, packs, regions, first + 96 * part, 96, blocks.at[part], sems.at[part]
+        )
+        for part in range(FF_PARTS)
+    ]
+
+
+def reduce_forward(place, live, middle, active, small, pack, first, last):
 
     def kernel(place_ref, live_ref, middle_ref, active_ref, small_ref, *rest):
-        packs = rest[:10]
-        result_ref, blocks, sems = rest[10:]
+        packs = rest[:PIECES]
+        result_ref, blocks, sems = rest[PIECES:]
         image = pl.program_id(0)
-        copies = []
-        for part, plan in enumerate(plans):
-            at = sum(len(earlier) for earlier in plans[:part])
-            copies += block_copies(
-                place_ref[0], packs, plan, blocks.at[part], sems.at[pl.ds(at, len(plan))]
-            )
+        copies = reduce_copies(place_ref[0], packs, pack[1], first, blocks, sems)
 
         @pl.when(image == 0)
-        def arrive():
-            run_all(copies, "start")
-            run_all(copies, "wait")
+        def begin():
+            for group in copies:
+                run_all(group, "start")
 
         total = middle_ref[...] + small_ref[SM_RB : SM_RB + 1]
         for part in range(FF_PARTS):
+
+            @pl.when(image == 0)
+            def arrive():
+                run_all(copies[part], "wait")
+
             total = total + dot_nt(
                 active_ref[:, WIDTH * part : WIDTH * (part + 1)],
                 blocks[part].reshape(WIDTH, WIDTH),
@@ -648,17 +871,17 @@
             rows_spec(FF_PARTS * WIDTH),
             fixed(small.shape),
         ]
-        + [in_any()] * 10,
+        + [in_any()] * PIECES,
         out_specs=rows_spec(WIDTH),
         out_shape=jax.ShapeDtypeStruct((tokens, WIDTH), bf16 if last else f32),
         scratch_shapes=[
             pltpu.VMEM((FF_PARTS, 8, 96, WIDTH), bf16),
-            pltpu.SemaphoreType.DMA((copies_in_all,)),
+            pltpu.SemaphoreType.DMA((4, PIECES)),
         ],
         compiler_params=params(),
-        cost_estimate=cost(8 * tokens * WIDTH * WIDTH, 12e6),
+        cost_estimate=cost(0.01),
         name="reduce_forward",
-    )(place, live, middle, active, small, *pack)
+    )(place, live, middle, active, small, *pack[0])
 
 
 def split_owners(place_now, turned, mine_ref, theirs_ref, count, lead=()):
@@ -691,21 +914,14 @@
         out_shape=[shape((tokens, WIDTH), bf16)] + [shape((4, 96, tokens), bf16)] * 2,
         scratch_shapes=[pltpu.VMEM((8, 96, ROWS), bf16)],
         compiler_params=params(),
-        cost_estimate=cost(1e6, 4e6),
+        cost_estimate=cost(0.01),
         name="start_grad",
     )(place, live, cotangent)
 
 
-def ff_backward(place, grad, slope, middle, small, packs_and_plans):
-    (expand_pack, expand_cut, expand_first), (reduce_pack, reduce_cut, reduce_first) = (
-        packs_and_plans
-    )
-    expand_plan = piece_plan(expand_cut, expand_first, 384)
-    plans = reduce_plans(reduce_cut, reduce_first)
-    copies_in_all = sum(len(plan) for plan in plans)
-
+def ff_backward(place, grad, slope, middle, small, pack):
     def kernel(place_ref, grad_ref, slope_ref, middle_ref, small_ref, *rest):
-        expand_packs, reduce_packs = rest[:10], rest[10:20]
+        packs = rest[:PIECES]
         (
             out_ref,
             pre_mine,
@@ -719,35 +935,24 @@
             turned_attn,
             expand_sems,
             reduce_sems,
-        ) = rest[20:]
+        ) = rest[PIECES:]
         place_now = place_ref[0]
         image = pl.program_id(0)
-        reduce_copies = []
-        for part, plan in enumerate(plans):
-            at = sum(len(earlier) for earlier in plans[:part])
-            reduce_copies.append(
-                block_copies(
-                    place_now,
-                    reduce_packs,
-                    plan,
-                    reduce_blocks.at[part],
-                    reduce_sems.at[pl.ds(at, len(plan))],
-                )
-            )
+        copies = reduce_copies(place_now, packs, pack[1], 384, reduce_blocks, reduce_sems)
         expand_copies = block_copies(
-            place_now, expand_packs, expand_plan, expand_block, expand_sems
+            place_now, packs, pack[1], 0, 384, expand_block, expand_sems
         )
 
         @pl.when(image == 0)
         def begin():
-            for group in reduce_copies:
+            for group in copies:
                 run_all(group, "start")
             run_all(expand_copies, "start")
             sums_ref[...] = jnp.zeros_like(sums_ref)
 
         grad_rows = grad_ref[...].astype(f32)
         low = grad_rows.astype(bf16)
-        sums_ref[0:1] += jnp.sum(low.astype(f32), axis=0, keepdims=True)
+        sums_ref[2:3] += jnp.sum(low.astype(f32), axis=0, keepdims=True)
         core = place_now & 1
         chip = place_now >> 1
         back = jnp.zeros((ROWS, WIDTH), f32)
@@ -755,7 +960,7 @@
 
             @pl.when(image == 0)
             def arrive():
-                run_all(reduce_copies[part], "wait")
+                run_all(copies[part], "wait")
                 if part == 0:
                     run_all(expand_copies, "wait")
 
@@ -773,8 +978,8 @@
                 pre_low, expand_block[2 * part : 2 * part + 2].reshape(WIDTH, WIDTH)
             )
         unit, root = normalise(middle_ref[...])
-        sums_ref[1:2] += jnp.sum(back * unit, axis=0, keepdims=True)
-        sums_ref[2:3] += jnp.sum(back, axis=0, keepdims=True)
+        sums_ref[0:1] += jnp.sum(back * unit, axis=0, keepdims=True)
+        sums_ref[1:2] += jnp.sum(back, axis=0, keepdims=True)
         scaled = back * small_ref[SM_G2 : SM_G2 + 1]
         result = grad_rows + root * (
             scaled
@@ -799,7 +1004,7 @@
             rows_spec(WIDTH),
             fixed(small.shape),
         ]
-        + [in_any()] * 20,
+        + [in_any()] * PIECES,
         out_specs=[
             rows_spec(WIDTH),
             halves_spec(384),
@@ -817,37 +1022,34 @@
             pltpu.VMEM((FF_PARTS, 8, 96, WIDTH), bf16),
             pltpu.VMEM((2, 384, ROWS), bf16),
             pltpu.VMEM((8, 96, ROWS), bf16),
-            pltpu.SemaphoreType.DMA((len(expand_plan),)),
-            pltpu.SemaphoreType.DMA((copies_in_all,)),
+            pltpu.SemaphoreType.DMA((PIECES,)),
+            pltpu.SemaphoreType.DMA((4, PIECES)),
         ],
         compiler_params=params(),
-        cost_estimate=cost(16 * tokens * WIDTH * WIDTH, 22e6),
+        cost_estimate=cost(0.01),
         name="ff_backward",
-    )(place, grad, slope, middle, small, *expand_pack, *reduce_pack)
-
-
-def attn_backward(place, grad, hidden, qkv, small, pack, cut, last):
-    plans = [piece_plan(cut, 96 * at, 96) for at in range(4)]
-    copies_in_all = sum(len(plan) for plan in plans)
-
-    def kernel(place_ref, grad_ref, hidden_ref, qkv_ref, small_ref, *rest):
-        packs = rest[:10]
+    )(place, grad, slope, middle, small, *pack[0])
+
+
+def attn_backward(place, grad, hidden, qkv, small, ff_sums, pack, last):
+    def kernel(place_ref, grad_ref, hidden_ref, qkv_ref, small_ref, ff_sums_ref, *rest):
+        packs = rest[:PIECES]
         if last:
-            out_ref, qkv_mine, qkv_theirs, sums_ref = rest[10:14]
+            out_ref, qkv_mine, qkv_theirs, vec_mine, vec_theirs = rest[PIECES : PIECES + 5]
         else:
-            out_ref, qkv_mine, qkv_theirs, sums_ref, low_mine, low_theirs = rest[10:16]
-        blocks, turned, straight, sems = rest[-4:]
+            (
+                out_ref,
+                qkv_mine,
+                qkv_theirs,
+                vec_mine,
+                vec_theirs,
+                low_mine,
+                low_theirs,
+            ) = rest[PIECES : PIECES + 7]
+        blocks, turned, straight, sums_ref, sems = rest[-5:]
         place_now = place_ref[0]
         image = pl.program_id(0)
-        copies = []
-        at = 0
-        for member, plan in enumerate(plans):
-            copies.append(
-                block_copies(
-                    place_now, packs, plan, blocks.at[member], sems.at[pl.ds(at, len(plan))]
-                )
-            )
-            at += len(plan)
+        copies = heads_copies(place_now, packs, pack[1], blocks, sems)
 
         @pl.when(image == 0)
         def begin():
@@ -918,8 +1120,34 @@
                     straight_one.astype(f32), axis=0, keepdims=True
                 )
         unit, root = normalise(hidden_ref[...].astype(f32))
-        sums_ref[2:3] += jnp.sum(back * unit, axis=0, keepdims=True)
-        sums_ref[3:4] += jnp.sum(back, axis=0, keepdims=True)
+        sums_ref[3:4] += jnp.sum(back * unit, axis=0, keepdims=True)
+        sums_ref[4:5] += jnp.sum(back, axis=0, keepdims=True)
+
+        @pl.when(image == pl.num_programs(0) - 1)
+        def vectors():
+            sums_ref[2:3] = ff_sums_ref[3:4]
+            sums_ref[5:8] = ff_sums_ref[0:3]
+            row = lax.broadcasted_iota(jnp.int32, (WIDTH, 1024), 0)
+            column = lax.broadcasted_iota(jnp.int32, (WIDTH, 1024), 1)
+            at = column & 127
+            wanted = 96 * ((column >> 7) ^ place_now) + at
+            chosen = jnp.where((row == wanted) & (at < 96), 1.0, 0.0)
+            cut = jnp.dot(
+                sums_ref[...],
+                chosen,
+                preferred_element_type=f32,
+                precision=lax.Precision.HIGHEST,
+            )
+            for delta in range(8):
+                owner = place_now ^ delta
+                target = vec_theirs if delta & 1 else vec_mine
+                target[delta >> 1] = jnp.zeros((16, WIDTH // 2), f32)
+                target[delta >> 1, 0:8, 0:128] = cut[:, 128 * delta : 128 * delta + 128]
+                line = ff_sums_ref[pl.ds(4 + (owner >> 1), 1)]
+                target[delta >> 1, 8:9] = jnp.where(
+                    (owner & 1) == 0, line[:, : WIDTH // 2], line[:, WIDTH // 2 :]
+                )
+
         scaled = back * small_ref[SM_G1 : SM_G1 + 1]
         result = grad_rows + root * (
             scaled
@@ -940,11 +1168,12 @@
     tokens = grad.shape[0]
     shape = jax.ShapeDtypeStruct
     heads_spec = pl.BlockSpec((3, 4, 96, ROWS), lambda image: (0, 0, 0, image))
-    out_specs = [rows_spec(WIDTH), heads_spec, heads_spec, fixed((8, WIDTH))]
+    vector_shape = (4, 16, WIDTH // 2)
+    out_specs = [rows_spec(WIDTH), heads_spec, heads_spec, fixed(vector_shape), fixed(vector_shape)]
     out_shape = (
         [shape((tokens, WIDTH), bf16 if last else f32)]
         + [shape((3, 4, 96, tokens), bf16)] * 2
-        + [shape((8, WIDTH), f32)]
+        + [shape(vector_shape, f32)] * 2
     )
     if not last:
         out_specs += [halves_spec(96)] * 2
@@ -958,24 +1187,27 @@
             rows_spec(WIDTH),
             rows_spec(3 * WIDTH),
             fixed(small.shape),
+            fixed(ff_sums.shape),
         ]
-        + [in_any()] * 10,
+        + [in_any()] * PIECES,
         out_specs=out_specs,
         out_shape=out_shape,
         scratch_shapes=[
             pltpu.VMEM((4, 8, 96, WIDTH), bf16),
             pltpu.VMEM((3, WIDTH, ROWS), bf16),
             pltpu.VMEM((ROWS, 3 * WIDTH), bf16),
-            pltpu.SemaphoreType.DMA((copies_in_all,)),
+            pltpu.VMEM((8, WIDTH), f32),
+            pltpu.SemaphoreType.DMA((4, PIECES)),
         ],
         compiler_params=params(),
-        cost_estimate=cost(8 * tokens * WIDTH * WIDTH * 2.5, 16e6),
+        cost_estimate=cost(0.01),
         name="attn_backward",
-    )(place, grad, hidden, qkv, small, *pack)
-
-
-def spread(result, owner, rows, out_refs, half):
+    )(place, grad, hidden, qkv, small, ff_sums, *pack[0])
+
+
+def spread(result, owner, rows, out_refs):
     go_x, go_y, stay_x, stay_y = out_refs
+    half = WIDTH // 2
     low, high = result[:, :half].astype(bf16), result[:, half:].astype(bf16)
     target, at = ((stay_x, 0), (go_x, 0), (stay_x, 1), (go_x, 1))[owner]
     target[at, rows] = low
@@ -983,150 +1215,101 @@
     target[at, rows] = high
 
 
-def travel_shapes(rows_low, rows_high, half):
+def travel_shapes(rows_low, rows_high):
     shape = jax.ShapeDtypeStruct
-    return [
-        shape((2, rows_low, half), bf16),
-        shape((2, rows_high, half), bf16),
-        shape((2, rows_low, half), bf16),
-        shape((2, rows_high, half), bf16),
-    ]
-
-
-def reduce_terms(grad_mine, grad_other, active_mine, active_other):
-    tokens, columns = active_mine.shape
-    half = columns // 2
-    chunk = min(half, WIDTH)
-
-    def kernel(grad_a, grad_b, low_a, low_b, high_a, high_b, go_x, go_y, stay_x, stay_y):
-        left_a = grad_a[...].reshape(384, tokens)
-        left_b = grad_b[...].reshape(384, tokens)
-        low = dot_nn(left_a, low_a[...]) + dot_nn(left_b, low_b[...])
-        low = low.astype(bf16).reshape(4, 96, chunk)
-        stay_x[0], go_x[0], stay_x[1], go_x[1] = low[0], low[1], low[2], low[3]
-        high = dot_nn(left_a, high_a[...]) + dot_nn(left_b, high_b[...])
-        high = high.astype(bf16).reshape(4, 96, chunk)
-        stay_y[0], stay_y[1], go_y[0], go_y[1] = high[0], high[1], high[2], high[3]
-
-    steps = half // chunk
-    grads_spec = pl.BlockSpec((4, 96, tokens), lambda at: (0, 0, 0))
-    low_spec = pl.BlockSpec((tokens, chunk), lambda at: (0, at))
-    high_spec = pl.BlockSpec((tokens, chunk), lambda at: (0, at + steps))
+    half = WIDTH // 2
+    return [shape((2, rows, half), bf16) for rows in (rows_low, rows_high, rows_low, rows_high)]
+
+
+def owner_terms(reduce=None, expand=None, merge=None, heads=None, small_terms=None):
+    given, in_specs, sections = [], [], []
+    rows = 0
+    tokens = (reduce or expand or heads)[1][0].shape[0]
+    whole = pl.BlockSpec((tokens, WIDTH), lambda at: (0, 0))
+    four = pl.BlockSpec((4, 96, tokens), lambda at: (0, 0, 0))
+    for name, pair, left, right, taken in (
+        ("reduce", reduce, four, pl.BlockSpec((tokens, WIDTH), lambda at: (0, at)), 384),
+        ("expand", expand, pl.BlockSpec((1, 384, tokens), lambda at: (at, 0, 0)), whole, 384),
+        ("merge", merge, four, whole, 96),
+        (
+            "heads",
+            heads,
+            pl.BlockSpec((1, 4, 96, tokens), lambda at: (jnp.minimum(at, 2), 0, 0, 0)),
+            whole,
+            288,
+        ),
+    ):
+        if pair is not None:
+            given += [*pair[0], *pair[1]]
+            in_specs += [left, left, right, right]
+            sections.append((name, rows))
+            rows += taken
+    extra = 0
+    if small_terms is not None:
+        given += small_terms
+        in_specs += [pl.BlockSpec(small_terms[0].shape, lambda at: (0, 0, 0))] * 2
+        extra = 16
+
+    def kernel(*refs):
+        ins, out_refs = refs[: len(given)], refs[len(given) :]
+        go_x, go_y, stay_x, stay_y = out_refs
+        part = pl.program_id(0)
+
+        def multiply(place, first):
+            left_a, left_b, right_a, right_b = ins[4 * place : 4 * place + 4]
+            result = dot_nn(left_a[...].reshape(384, tokens), right_a[...]) + dot_nn(
+                left_b[...].reshape(384, tokens), right_b[...]
+            )
+            if first is None:
+                return result
+            for owner in range(4):
+                spread(
+                    result[96 * owner : 96 * owner + 96], owner, pl.ds(first, 96), out_refs
+                )
+
+        for place, (name, first) in enumerate(sections):
+            if name == "reduce":
+                multiply(place, pl.multiple_of(first + 96 * part, 96))
+            elif name == "heads":
+
+                @pl.when(part < 3)
+                def one_head_block():
+                    multiply(place, pl.multiple_of(first + 96 * part, 96))
+
+            elif name == "merge":
+
+                @pl.when(part == 3)
+                def merge_block():
+                    multiply(place, first)
+
+            else:
+                result = multiply(place, None)
+                for owner in range(4):
+
+                    @pl.when(part == owner)
+                    def keep():
+                        spread(result, owner, slice(first, first + 384), out_refs)
+
+        if small_terms is not None:
+
+            @pl.when(part == 3)
+            def vectors():
+                for owner in range(4):
+                    target, at = ((stay_x, 0), (go_x, 0), (stay_x, 1), (go_x, 1))[owner]
+                    target[at, rows : rows + 16] = (ins[-2][owner] + ins[-1][owner]).astype(bf16)
+
+    half = WIDTH // 2
+    heights = (rows + extra, rows, rows + extra, rows)
     return pl.pallas_call(
         kernel,
-        grid=(steps,),
-        in_specs=[grads_spec, grads_spec, low_spec, low_spec, high_spec, high_spec],
-        out_specs=[pl.BlockSpec((2, 96, chunk), lambda at: (0, 0, at))] * 4,
-        out_shape=travel_shapes(96, 96, half),
+        grid=(4,),
+        in_specs=in_specs,
+        out_specs=[pl.BlockSpec((2, height, half), lambda at: (0, 0, 0)) for height in heights],
+        out_shape=[jax.ShapeDtypeStruct((2, height, half), bf16) for height in heights],
         compiler_params=params(),
-        cost_estimate=cost(4 * 384 * tokens * columns, 12e6),
-        name="reduce_terms",
-    )(grad_mine, grad_other, active_mine, active_other, active_mine, active_other)
-
-
-def expand_terms(grad_mine, grad_other, normed_mine, normed_other):
-    tokens = normed_mine.shape[0]
-
-    def kernel(grad_a, grad_b, rows_a, rows_b, *out_refs):
-        for owner in range(4):
-            result = dot_nn(grad_a[owner], rows_a[...]) + dot_nn(grad_b[owner], rows_b[...])
-            spread(result, owner, slice(None), out_refs, WIDTH // 2)
-
-    return pl.pallas_call(
-        kernel,
-        out_shape=travel_shapes(384, 384, WIDTH // 2),
-        compiler_params=pltpu.CompilerParams(vmem_limit_bytes=VMEM_BYTES),
-        cost_estimate=cost(4 * 1536 * tokens * WIDTH, 9e6),
-        name="expand_terms",
-    )(grad_mine, grad_other, normed_mine, normed_other)
-
-
-def attn_terms(
-    qkv_mine,
-    qkv_other,
-    normed_mine,
-    normed_other,
-    attn_mine,
-    attn_other,
-    mixed_mine,
-    mixed_other,
-    small_terms,
-):
-    tokens = normed_mine.shape[0]
-
-    def kernel(
-        qkv_a, qkv_b, normed_a, normed_b, attn_a, attn_b, mixed_a, mixed_b, small_ref, *out_refs
-    ):
-        go_x, go_y, stay_x, stay_y = out_refs
-        for member in range(4):
-            if member < 3:
-                left_a, left_b, right_a, right_b = qkv_a[member], qkv_b[member], normed_a, normed_b
-            else:
-                left_a, left_b, right_a, right_b = attn_a[...], attn_b[...], mixed_a, mixed_b
-            result = dot_nn(left_a.reshape(384, tokens), right_a[...]) + dot_nn(
-                left_b.reshape(384, tokens), right_b[...]
-            )
-            for owner in range(4):
-                spread(
-                    result[96 * owner : 96 * owner + 96],
-                    owner,
-                    slice(96 * member, 96 * member + 96),
-                    out_refs,
-                    WIDTH // 2,
-                )
-        for owner in range(4):
-            target, at = ((stay_x, 0), (go_x, 0), (stay_x, 1), (go_x, 1))[owner]
-            target[at, 384:400] = small_ref[owner]
-
-    return pl.pallas_call(
-        kernel,
-        out_shape=travel_shapes(400, 384, WIDTH // 2),
-        compiler_params=pltpu.CompilerParams(vmem_limit_bytes=VMEM_BYTES),
-        cost_estimate=cost(4 * 1536 * tokens * WIDTH, 10e6),
-        name="attn_terms",
-    )(
-        qkv_mine,
-        qkv_other,
-        normed_mine,
-        normed_other,
-        attn_mine,
-        attn_other,
-        mixed_mine,
-        mixed_other,
-        small_terms,
-    )
-
-
-def by_difference(place_at, rows):
-    shape = rows.shape
-    for bit in range(3):
-        halves = rows.reshape((8 >> (bit + 1), 2, 1 << bit) + shape[1:])
-        rows = jnp.where((place_at >> bit) & 1 == 1, halves[:, ::-1], halves).reshape(shape)
-    return rows
-
-
-def add_low(*parts):
-    total = parts[0].astype(f32)
-    for part in parts[1:]:
-        total = total + part.astype(f32)
-    return total.astype(bf16)
-
-
-def sum_chips(go_x, go_y, stay_x, stay_y):
-    from_x, from_y = swap_x(go_x), swap_y(go_y)
-    low_on = swap_y(add_low(stay_x[1], from_x[1]))
-    high_on = swap_x(add_low(stay_y[1], from_y[1]))
-    return jnp.concatenate(
-        [add_low(stay_x[0], from_x[0], low_on), add_low(stay_y[0], from_y[0], high_on)]
-    )
-
-
-def sum_replicas(part):
-    inward = add_low(part, lax.ppermute(part, "rep", [(0, 1), (3, 2)]))
-    total = add_low(inward, lax.ppermute(inward, "rep", [(1, 2), (2, 1)]))
-    outward = lax.ppermute(total, "rep", [(1, 0), (2, 3)])
-    rep_at = lax.axis_index("rep")
-    return jnp.where((rep_at == 0) | (rep_at == 3), outward, total).astype(f32)
+        cost_estimate=cost(0.01),
+        name="owner_terms",
+    )(*given)
 
 
 def shards(
@@ -1152,160 +1335,256 @@
     place_at = lax.axis_index("fsdp").astype(jnp.int32)
     place = place_at[None]
 
-    def small_rows(layer):
-        rows = jnp.concatenate(
-            [
-                heads_bias[layer],
-                merge_bias[layer][None],
-                first_gain[layer][None],
-                first_shift[layer][None],
-                second_gain[layer][None],
-                second_shift[layer][None],
-                reduce_bias[layer][None],
-                expand_bias[layer].reshape(4, 96),
-            ]
+    matrices = (heads_weight, merge_weight, expand_weight, reduce_weight)
+    vectors = (
+        heads_bias,
+        merge_bias,
+        first_gain,
+        first_shift,
+        second_gain,
+        second_shift,
+        reduce_bias,
+        expand_bias,
+    )
+    kinds = [(kind, layer) for layer in range(layers) for kind in ("attn", "ff")]
+    rows_of = [400 if kind == "attn" else 768 for kind, layer in kinds]
+    cut_of = [192 if kind == "attn" else 384 for kind, layer in kinds]
+    x_rows = [0] + cut_of
+    y_rows = [0] + [rows - cut for rows, cut in zip(rows_of, cut_of)]
+    count = len(kinds)
+
+    def send_round(at, own_now, x_before, y_before):
+        if at == 0:
+            return swap_x(own_now), swap_y(own_now)
+        rows, cut = rows_of[at - 1], cut_of[at - 1]
+        to_x = [(y_before, y_rows[at - 1], cut)]
+        to_y = [(x_before, x_rows[at - 1] + cut, rows - cut)]
+        if at < count:
+            to_x.append((own_now, 0, rows_of[at]))
+            to_y.append((own_now, 0, rows_of[at]))
+        to_x, to_y = join_rows([to_x, to_y])
+        return swap_x(to_x), swap_y(to_y)
+
+    def pack_of(at, own_pair, came):
+        (x_0, y_0, cx_0, cy_0), (x_1, y_1, cx_1, cy_1) = came[at], came[at + 1]
+        return (
+            (own_pair[0], x_0, y_0, x_1, y_1, own_pair[1], cx_0, cy_0, cx_1, cy_1),
+            regions_of(rows_of[at], cut_of[at], x_rows[at], y_rows[at]),
         )
-        return jnp.pad(rows, ((0, 4), (0, width - 96)))
-
-    def reduce_rows(layer):
-        return [reduce_weight[layer][:, width * part : width * (part + 1)] for part in range(4)]
-
-    attn_cut, ff_cut = 192, 384
-    attn_packs, ff_packs = [], []
-    for layer in range(layers):
-        own = jnp.concatenate(
-            [
-                heads_weight[layer].reshape(288, width),
-                merge_weight[layer],
-                small_rows(layer),
-            ]
-        )
-        attn_packs.append(gather_pack(own, attn_cut))
-        own = jnp.concatenate([expand_weight[layer]] + reduce_rows(layer))
-        ff_packs.append(gather_pack(own, ff_cut))
-
-    smalls, expand_biases = [], []
-    for pack in attn_packs:
-        own, along_x, along_y, unused, across, own_c, x_c, y_c, unused_c, across_c = pack
-        rows = [
-            own[384:396, :96],
-            own_c[384:396, :96],
-            along_x[384:396, :96],
-            x_c[384:396, :96],
-            along_y[384:396, :96],
-            y_c[384:396, :96],
-            across[192:204, :96],
-            across_c[192:204, :96],
-        ]
-        ordered = by_difference(place_at, jnp.stack(rows).astype(f32))
-        smalls.append(ordered[:, :8].transpose(1, 0, 2).reshape(8, width))
-        expand_biases.append(ordered[:, 8:].reshape(4, width))
+
+    def both(values):
+        return tuple(swap_core(value) for value in values)
 
     hidden = images.reshape(tokens, width)
-    saved = []
+    seal = lax.optimization_barrier
+
+    came = []
+    own = own_packs(kinds[:1], matrices, vectors)
+    new = send_round(0, own[0], None, None)
+    own += own_packs(kinds[1:], matrices, vectors)
+    own_other = both(own)
     grad, low_mine, low_theirs = start_grad(place, slot_flags, cotangent.reshape(tokens, width))
-    for layer in range(layers):
-        last = layer == layers - 1
-        small = smalls[layer]
-        middle, normed, qkv, mixed = attn_forward(
-            place, hidden, small, attn_packs[layer], attn_cut
-        )
-        second, active, slope = expand_forward(
-            place, middle, small, expand_biases[layer], ff_packs[layer], ff_cut, 0
-        )
-        following = reduce_forward(
-            place, slot_flags, middle, active, small, ff_packs[layer], ff_cut, 384, last
-        )
-        others = tuple(swap_core(rows) for rows in (normed, mixed, second, active))
-        saved.append((hidden, normed, qkv, mixed, middle, second, active, slope, others))
-        hidden = following
-    outputs = hidden.reshape(images.shape)
-
-    sums = [None] * layers
-    for layer in reversed(range(layers)):
-        last = layer == 0
-        small = smalls[layer]
-        before, normed, qkv, mixed, middle, second, active, slope, others = saved[layer]
-        normed_other, mixed_other, second_other, active_other = others
-        reduce_sum = sum_replicas(
-            sum_chips(*reduce_terms(low_mine, swap_core(low_theirs), active, active_other))
-        )
-        grad, pre_mine, pre_theirs, attn_mine, attn_theirs, ff_sums = ff_backward(
-            place,
-            grad,
-            slope,
-            middle,
-            small,
-            ((ff_packs[layer], ff_cut, 0), (ff_packs[layer], ff_cut, 384)),
-        )
-        expand_sum = sum_replicas(
-            sum_chips(*expand_terms(pre_mine, swap_core(pre_theirs), second, second_other))
-        )
-        made = attn_backward(place, grad, before, qkv, small, attn_packs[layer], attn_cut, last)
-        grad, qkv_mine, qkv_theirs, attn_sums = made[:4]
-        if not last:
-            low_mine, low_theirs = made[4:]
-        vectors = jnp.concatenate(
-            [
-                attn_sums[0:2],
-                ff_sums[3:4],
-                attn_sums[2:4],
-                ff_sums[1:3],
-                ff_sums[0:1],
-            ]
-        )
-        terms = jnp.concatenate(
-            [
-                vectors.reshape(8, 8, 96).transpose(1, 0, 2),
-                ff_sums[4:8].reshape(8, 4, 96),
-            ],
-            axis=1,
-        )
-        terms = by_difference(place_at, terms).reshape(4, 2, 12, 96)
-        terms = terms[:, 0] + swap_core(terms[:, 1])
-        terms = jnp.pad(terms, ((0, 0), (0, 4), (0, width // 2 - 96))).astype(bf16)
-        attn_sum = sum_replicas(
-            sum_chips(
-                *attn_terms(
-                    qkv_mine,
-                    swap_core(qkv_theirs),
-                    normed,
-                    normed_other,
-                    attn_mine,
-                    swap_core(attn_theirs),
-                    mixed,
-                    mixed_other,
-                    terms,
-                )
-            )
-        )
-        sums[layer] = (reduce_sum, expand_sum, attn_sum)
-    images_grad = grad.reshape(images.shape)
+    own, own_other, new, grad, low_mine, low_theirs = seal(
+        (own, own_other, new, grad, low_mine, low_theirs)
+    )
+
+    got, new = new, send_round(1, own[1], *new)
+    came.append(got + both(got))
+    low = (low_mine, swap_core(low_theirs))
+    own, own_other, came, new, low, grad = seal((own, own_other, came, new, low, grad))
+
+    got, new = new, send_round(2, own[2], *new)
+    came.append(got + both(got))
+    pack_a0 = pack_of(0, (own[0], own_other[0]), came)
+    small_0, expand_rows_0 = gathered_vectors(place, pack_a0)
+    middle_0, normed_0, qkv_0, mixed_0 = attn_forward(place, hidden, small_0, pack_a0)
+    own, came, new, small_0, expand_rows_0, middle_0, normed_0, qkv_0, mixed_0 = seal(
+        (own, came, new, small_0, expand_rows_0, middle_0, normed_0, qkv_0, mixed_0)
+    )
+
+    got, new = new, send_round(3, own[3], *new)
+    came.append(got + both(got))
+    pack_f0 = pack_of(1, (own[1], own_other[1]), came)
+    second_0, active_0, slope_0 = expand_forward(
+        place, middle_0, small_0, expand_rows_0, pack_f0, 0
+    )
+    hidden_1 = reduce_forward(
+        place, slot_flags, middle_0, active_0, small_0, pack_f0, 384, False
+    )
+    others_a0 = both((normed_0, mixed_0))
+    own, came, new, second_0, active_0, slope_0, hidden_1, others_a0 = seal(
+        (own, came, new, second_0, active_0, slope_0, hidden_1, others_a0)
+    )
+
+    got, new = new, send_round(4, None, *new)
+    came.append(got + both(got))
+    pack_a1 = pack_of(2, (own[2], own_other[2]), came)
+    small_1, expand_rows_1 = gathered_vectors(place, pack_a1)
+    middle_1, normed_1, qkv_1, mixed_1 = attn_forward(place, hidden_1, small_1, pack_a1)
+    second_other_0 = swap_core(second_0)
+    came, new, small_1, expand_rows_1, middle_1, normed_1, qkv_1, mixed_1, second_other_0 = seal(
+        (came, new, small_1, expand_rows_1, middle_1, normed_1, qkv_1, mixed_1, second_other_0)
+    )
+
+    came.append(new + both(new))
+    pack_f1 = pack_of(3, (own[3], own_other[3]), came)
+    second_1, active_1, slope_1 = expand_forward(
+        place, middle_1, small_1, expand_rows_1, pack_f1, 0
+    )
+    others_a1 = both((normed_1, mixed_1))
+    active_other_0 = swap_core(active_0)
+    second_1, active_1, slope_1, others_a1, active_other_0, came = seal(
+        (second_1, active_1, slope_1, others_a1, active_other_0, came)
+    )
+    pack_f1 = pack_of(3, (own[3], own_other[3]), came)
+
+    grad, pre_mine, pre_theirs, attn_mine, attn_theirs, ff_sums = ff_backward(
+        place, grad, slope_1, middle_1, small_1, pack_f1
+    )
+    others_f1 = both((second_1, active_1))
+    grad, pre_mine, pre_theirs, attn_mine, attn_theirs, ff_sums, others_f1 = seal(
+        (grad, pre_mine, pre_theirs, attn_mine, attn_theirs, ff_sums, others_f1)
+    )
+
+    travel_r1 = owner_terms(reduce=(low, (active_1, others_f1[1])))
+    pre_other, attn_other = both((pre_theirs, attn_theirs))
+    travel_r1, pre_other, attn_other, grad = seal((travel_r1, pre_other, attn_other, grad))
+
+    state_r1 = first_steps(travel_r1)
+    travel_em1 = owner_terms(
+        expand=((pre_mine, pre_other), (second_1, others_f1[0])),
+        merge=((attn_mine, attn_other), (mixed_1, others_a1[1])),
+    )
+    state_r1, travel_em1, grad = seal((state_r1, travel_em1, grad))
+
+    state_r1 = second_steps(state_r1)
+    state_em1 = first_steps(travel_em1)
+    grad, qkv_mine, qkv_theirs, vec_mine, vec_theirs, low_mine, low_theirs = attn_backward(
+        place, grad, hidden_1, qkv_1, small_1, ff_sums, pack_a1, False
+    )
+    made = (grad, qkv_mine, qkv_theirs, vec_mine, vec_theirs, low_mine, low_theirs)
+    state_r1, state_em1, made = seal((state_r1, state_em1, made))
+    grad, qkv_mine, qkv_theirs, vec_mine, vec_theirs, low_mine, low_theirs = made
+
+    sum_r1 = to_middle(ends(state_r1))
+    state_em1 = second_steps(state_em1)
+    low_other, qkv_other, vec_other = both((low_theirs, qkv_theirs, vec_theirs))
+    travel_hr = owner_terms(
+        reduce=((low_mine, low_other), (active_0, active_other_0)),
+        heads=((qkv_mine, qkv_other), (normed_1, others_a1[0])),
+        small_terms=(vec_mine, vec_other),
+    )
+    sum_r1, state_em1, travel_hr, grad = seal((sum_r1, state_em1, travel_hr, grad))
+
+    state_hr = first_steps(travel_hr)
+    sum_em1 = to_middle(ends(state_em1))
+    sum_r1 = across_middle(sum_r1)
+    grad, pre_mine, pre_theirs, attn_mine, attn_theirs, ff_sums = ff_backward(
+        place, grad, slope_0, middle_0, small_0, pack_f0
+    )
+    made = (grad, pre_mine, pre_theirs, attn_mine, attn_theirs, ff_sums)
+    state_hr, sum_em1, sum_r1, made = seal((state_hr, sum_em1, sum_r1, made))
+    grad, pre_mine, pre_theirs, attn_mine, attn_theirs, ff_sums = made
+
+    state_hr = second_steps(state_hr)
+    sum_em1 = across_middle(sum_em1)
+    pre_other, attn_other = both((pre_theirs, attn_theirs))
+    travel_em0 = owner_terms(
+        expand=((pre_mine, pre_other), (second_0, second_other_0)),
+        merge=((attn_mine, attn_other), (mixed_0, others_a0[1])),
+    )
+    state_hr, sum_em1, travel_em0, grad = seal((state_hr, sum_em1, travel_em0, grad))
+
+    state_em0 = first_steps(travel_em0)
+    sum_hr = to_middle(ends(state_hr))
+    final_r1, final_em1 = to_ends(sum_r1), to_ends(sum_em1)
+    images_grad, qkv_mine, qkv_theirs, vec_mine, vec_theirs = attn_backward(
+        place, grad, hidden, qkv_0, small_0, ff_sums, pack_a0, True
+    )
+    made = (images_grad, qkv_mine, qkv_theirs, vec_mine, vec_theirs)
+    state_em0, sum_hr, final_r1, final_em1, made = seal(
+        (state_em0, sum_hr, final_r1, final_em1, made)
+    )
+    images_grad, qkv_mine, qkv_theirs, vec_mine, vec_theirs = made
+
+    state_em0 = second_steps(state_em0)
+    sum_hr = across_middle(sum_hr)
+    qkv_other, vec_other = both((qkv_theirs, vec_theirs))
+    travel_h0 = owner_terms(
+        heads=((qkv_mine, qkv_other), (normed_0, others_a0[0])), small_terms=(vec_mine, vec_other)
+    )
+    state_em0, sum_hr, travel_h0 = seal((state_em0, sum_hr, travel_h0))
+
+    state_h0 = first_steps(travel_h0)
+    sum_em0 = to_middle(ends(state_em0))
+    final_hr = to_ends(sum_hr)
+    middle_last, active_last, travel_h0 = seal((middle_1, active_1, travel_h0))
+    outputs = reduce_forward(
+        place, slot_flags, middle_last, active_last, small_1, pack_f1, 384, True
+    ).reshape(images.shape)
+    state_h0, outputs = seal((state_h0, outputs))
+
+    state_h0 = second_steps(state_h0)
+    sum_em0 = across_middle(sum_em0)
+    state_h0 = seal(state_h0)
+    sum_h0 = to_middle(ends(state_h0))
+    sum_h0, sum_em0 = seal((sum_h0, sum_em0))
+    sum_h0 = across_middle(sum_h0)
+    final_em0 = to_ends(sum_em0)
+    final_h0 = to_ends(sum_h0)
+    rep_at = lax.axis_index("rep")
+    at_end = (rep_at == 0) | (rep_at == lax.axis_size("rep") - 1)
+    final_r1, final_em1, final_hr, final_em0, final_h0 = (
+        jnp.where(at_end, outward, total)
+        for total, outward in (final_r1, final_em1, final_hr, final_em0, final_h0)
+    )
+    images_grad = images_grad.reshape(images.shape)
 
     grad_scale = (
         micro_count * images.shape[1] * lax.axis_size("fsdp") * lax.axis_size("rep") * seq_len
     ) ** (-0.5)
-    finals = []
-    for reduce_sum, expand_sum, attn_sum in sums:
-        low, high = attn_sum[:400] * grad_scale, attn_sum[400:] * grad_scale
-        whole = jnp.concatenate([low[:384], high], axis=1)
-        vectors = low[384:396, :96]
-        finals.append(
-            (
-                whole[:288].reshape(3, 96, width),
-                vectors[SM_HB0 : SM_HB1 + 1],
-                whole[288:],
-                vectors[SM_MB],
-                vectors[SM_G1],
-                vectors[SM_S1],
-                vectors[SM_G2],
-                vectors[SM_S2],
-                jnp.concatenate([expand_sum[:384], expand_sum[384:]], axis=1) * grad_scale,
-                vectors[8:12].reshape(384),
-                jnp.concatenate([reduce_sum[:96], reduce_sum[96:]], axis=1) * grad_scale,
-                vectors[SM_RB],
-            )
+
+    def halves(low_half, high_half):
+        return jnp.concatenate([low_half, high_half], axis=1).astype(f32) * grad_scale
+
+    def as_reduce(rows):
+        return rows.reshape(4, 96, width).transpose(1, 0, 2).reshape(96, 4 * width)
+
+    def layer_grads(reduce_sum, em_sum, heads_sum, vectors):
+        vectors = vectors.astype(f32) * grad_scale
+        short = vectors[:, :96]
+        return (
+            heads_sum.reshape(3, 96, width),
+            short[SM_HB0 : SM_HB1 + 1],
+            em_sum[384:480],
+            short[SM_MB],
+            short[SM_G1],
+            short[SM_S1],
+            short[SM_G2],
+            short[SM_S2],
+            em_sum[:384],
+            vectors[8],
+            as_reduce(reduce_sum),
+            short[SM_RB],
         )
+
+    hr_low, hr_high = final_hr[:688], final_hr[688:]
+    hr_sum = halves(hr_low[:672], hr_high)
+    h0_low, h0_high = final_h0[:304], final_h0[304:]
+    finals = [
+        layer_grads(
+            hr_sum[:384],
+            halves(final_em0[:480], final_em0[480:]),
+            halves(h0_low[:288], h0_high),
+            h0_low[288:],
+        ),
+        layer_grads(
+            halves(final_r1[:384], final_r1[384:]),
+            halves(final_em1[:480], final_em1[480:]),
+            hr_sum[384:],
+            hr_low[672:],
+        ),
+    ]
     stacked = tuple(jnp.stack(member) for member in zip(*finals))
     return (outputs, images_grad) + stacked
 

time: 596 us -> 468 us (0.79); the launches traced: 585 us -> 464 us
  waiting for transfers between devices: 247 us -> 126 us
  Pallas kernels: 178 us -> 205 us
  other arithmetic: 33 us -> 16.5 us
    ppermute x18 -> x15, waiting for transfers between devices: 95.3 us -> 30.4 us  [the longest x5 24.4 us: to_ends(): return (total, lax.ppermute(total, 'rep', [(1, 0), (2, 3)]))]
    ppermute x20 -> x15, waiting for transfers between devices: 56.6 us -> 18.1 us  [swap_y(): return lax.ppermute(value, 'fsdp', [(at, at ^ 4) for at in range(8)])]
    ppermute x20 -> x15, waiting for transfers between devices: 91.3 us -> 57.3 us  [swap_x(): return lax.ppermute(value, 'fsdp', [(at, at ^ 2) for at in range(8)])]
    pallas_call x6 -> x33, Pallas kernels: 38.6 us -> 58.6 us  [the longest x5 40.1 us: owner_terms(): pl.pallas_call(kernel, grid=(4,), in_specs=in_specs, out_specs=[pl.BlockS...]
    convert_element_type x44 -> x0, other arithmetic: 19.5 us -> none  [the longest x36 16.8 us: add_low(): return total.astype(bf16)]
    ppermute x38 -> x32, waiting for transfers between devices: 4.13 us -> 19.9 us  [swap_core(): return lax.ppermute(value, 'fsdp', [(at, at ^ 1) for at in range(8)])]
    unnamed x214 -> x161, local copies, waits for them, and re-layouts: 13.5 us -> 27.6 us
    ppermute x18 -> x15, starting transfers between devices: 26.8 us -> 40.5 us  [the longest x5 29.1 us: to_middle(): return (part, lax.ppermute(part, 'rep', [(0, 1), (3, 2)]))]
  transfers between devices with their start and end apart: 96 -> 77, of which waited for: 38 -> 24; matrix products, arithmetic and copies ran while one was open for 11% -> 5% of each run, Pallas kernels for 30% -> 43%
where the time goes in v2:
time: 468 us; the launch traced here: 464 us
  Pallas kernels  205 us (44%)
  waiting for transfers between devices  126 us (27%)
  starting transfers between devices  78.9 us (17%)
  local copies, waits for them, and re-layouts  36.1 us (8%)
  other arithmetic  16.5 us (4%)
    ppermute x15, waiting for transfers between devices, swap_x(): return lax.ppermute(value, 'fsdp', [(at, at ^ 2) for at in range(8)])  57.3 us
    pallas_call x2, Pallas kernels, attn_backward(): pl.pallas_call(kernel, grid=(tokens // ROWS,), in_specs=[in_smem(), rows_...  46.3 us
    pallas_call x5, Pallas kernels, owner_terms(): pl.pallas_call(kernel, grid=(4,), in_specs=in_specs, out_specs=[pl.BlockS...  40.1 us
    pallas_call x2, Pallas kernels, ff_backward(): pl.pallas_call(kernel, grid=(tokens // ROWS,), in_specs=[in_smem(), rows_...  32.8 us
    ppermute x5, starting transfers between devices, to_middle(): return (part, lax.ppermute(part, 'rep', [(0, 1), (3, 2)]))  29.1 us
    unnamed x161, local copies, waits for them, and re-layouts  27.6 us
    ppermute x5, waiting for transfers between devices, to_ends(): return (total, lax.ppermute(total, 'rep', [(1, 0), (2, 3)]))  24.4 us
    pallas_call x2, Pallas kernels, attn_forward(): pl.pallas_call(kernel, grid=(tokens // ROWS,), in_specs=[in_smem(), rows_...  23.9 us
  transfers between devices with their start and end apart: 77, of which 24 were waited for; matrix products, arithmetic and copies ran while one was open for 5% of the time, Pallas kernels for 43%

profile of v2, /device:TPU:0, one launch (start us, length us, event | category | flops | bytes accessed | tf_op | source)
XLA Modules:
  0.0 464.1 jit_solution(17499521305594405421)
XLA Ops:
  11.5 3.0 collective-permute-start.5
  18.1 10.6 %collective-permute-done.5.refs_0_.refs_4_.rest_2_ = bf16[400,768]{1,0:T(8,128)(2,1)S(1)} collective-permute-done((bf16[400,768]{1,0:T(8,128)(2,1)}, bf16[400,768]{1,0:T(8,128)(2,1)S(1)}, u32[]{:S(2)}, u32[]{:S(2)}) %collective-permute-start.5) | collective-permute-done | bytes 614432 | tf_op jit(solution)/shard_map/ppermute | solution.py:387
  38.7 3.0 collective-permute-done.10.refs_1_
  41.7 29.4 %collective-permute-done.8.refs_2_.rest_3_.rest_1_ = bf16[960,768]{1,0:T(8,128)(2,1)S(1)} collective-permute-done((bf16[960,768]{1,0:T(8,128)(2,1)S(1)}, bf16[960,768]{1,0:T(8,128)(2,1)S(1)}, u32[]{:S(2)}, u32[]{:S(2)}) %collective-permute-start.8) | collective-permute-done | bytes 1474592 | tf_op jit(solution)/shard_map/ppermute | solution.py:383
  80.2 11.9 %attn_forward.2 = (f32[512,768]{1,0:T(8,128)}, bf16[512,768]{1,0:T(8,128)(2,1)}, bf16[512,2304]{1,0:T(8,128)(2,1)}, bf16[512,768]{1,0:T(8,128)(2,1)}) custom-call(s32[1]{0:T(128)} %bitcast.place_ref, bf16[512,768]{1,0:T(8,128)(2,1)} %bitcast.32, f32[8,768]{1,0:T(8,128)} %copy-done.33, bf16[400,768]{1,0:T(8,128)(2,1)} %own_packs.2.refs_0_.rest_0_, ...), custom_call_target="tpu_custom_call" | custom-call | flops 11000000 | bytes 1024 | tf_op jit(solution)/shard_map/attn_forward/pallas_call | solution.py:745
  92.1 10.9 %collective-permute-done.13.refs_2_.rest_3_.rest_1_ = bf16[784,768]{1,0:T(8,128)(2,1)S(1)} collective-permute-done((bf16[784,768]{1,0:T(8,128)(2,1)}, bf16[784,768]{1,0:T(8,128)(2,1)S(1)}, u32[]{:S(2)}, u32[]{:S(2)}) %collective-permute-start.13) | collective-permute-done | bytes 1204256 | tf_op jit(solution)/shard_map/ppermute | solution.py:383
  107.7 4.1 collective-permute-done.16.rest_9_.refs_5_.rest_7_
  111.8 11.1 %expand_forward.2 = (bf16[512,768]{1,0:T(8,128)(2,1)}, bf16[512,3072]{1,0:T(8,128)(2,1)}, bf16[512,3072]{1,0:T(8,128)(2,1)}) custom-call(s32[1]{0:T(128)} %bitcast.place_ref, f32[512,768]{1,0:T(8,128)} %get-tuple-element.364.middle_ref, f32[8,768]{1,0:T(8,128)} %copy-done.33, f32[4,1,768]{2,1,0:T(1,128)} %copy-done.38, bf16[768,768]{1,0:T(8,128)(2,1)} %copy-done.13, ...), custom_call_target="tpu_custom_call" | custom-call | flops 11000000 | bytes 1024 | tf_op jit(solution)/shard_map/expand_forward/pallas_call | solution.py:800
  122.9 9.4 %reduce_forward.2.hidden_ref = f32[512,768]{1,0:T(8,128)} custom-call(s32[1]{0:T(128)} %bitcast.place_ref, s32[2,1]{1,0:T(2,128)} %copy.29.live_ref, f32[512,768]{1,0:T(8,128)} %get-tuple-element.364.middle_ref, bf16[512,3072]{1,0:T(8,128)(2,1)} %get-tuple-element.407.active_ref.refs_2_, f32[8,768]{1,0:T(8,128)} %copy-done.33, bf16[768,768]{1,0:T(8,128)(2,1)} %copy-done.13, ...), custom_call_target="tpu_custom_call" | custom-call | flops 11000000 | bytes 1024 | tf_op jit(solution)/shard_map/reduce_forward/pallas_call | solution.py:864
  132.4 8.8 %collective-permute-done.17.refs_1_.rest_3_.rest_1_ = bf16[960,768]{1,0:T(8,128)(2,1)S(1)} collective-permute-done((bf16[960,768]{1,0:T(8,128)(2,1)}, bf16[960,768]{1,0:T(8,128)(2,1)S(1)}, u32[]{:S(2)}, u32[]{:S(2)}) %collective-permute-start.17) | collective-permute-done | bytes 1474592 | tf_op jit(solution)/shard_map/ppermute | solution.py:383
  143.3 6.7 %collective-permute-done.22.refs_7_.rest_9_.rest_7_ = bf16[976,768]{1,0:T(8,128)(2,1)S(1)} collective-permute-done((bf16[976,768]{1,0:T(8,128)(2,1)S(1)}, bf16[976,768]{1,0:T(8,128)(2,1)S(1)}, u32[]{:S(2)}, u32[]{:S(2)}) %collective-permute-start.22) | collective-permute-done | bytes 1499168 | tf_op jit(solution)/shard_map/ppermute | solution.py:379
  155.5 12.0 %attn_forward.3 = (f32[512,768]{1,0:T(8,128)}, bf16[512,768]{1,0:T(8,128)(2,1)}, bf16[512,2304]{1,0:T(8,128)(2,1)}, bf16[512,768]{1,0:T(8,128)(2,1)}) custom-call(s32[1]{0:T(128)} %bitcast.place_ref, f32[512,768]{1,0:T(8,128)} %reduce_forward.2.hidden_ref, f32[8,768]{1,0:T(8,128)} %copy-done.32, bf16[400,768]{1,0:T(8,128)(2,1)} %copy-done.14, ...), custom_call_target="tpu_custom_call" | custom-call | flops 11000000 | bytes 1024 | tf_op jit(solution)/shard_map/attn_forward/pallas_call | solution.py:745
  173.8 11.0 %expand_forward.3 = (bf16[512,768]{1,0:T(8,128)(2,1)}, bf16[512,3072]{1,0:T(8,128)(2,1)}, bf16[512,3072]{1,0:T(8,128)(2,1)}) custom-call(s32[1]{0:T(128)} %bitcast.place_ref, f32[512,768]{1,0:T(8,128)} %get-tuple-element.578.middle_ref, f32[8,768]{1,0:T(8,128)} %copy-done.32, f32[4,1,768]{2,1,0:T(1,128)} %copy-done.39, bf16[768,768]{1,0:T(8,128)(2,1)} %copy-done.12, ...), custom_call_target="tpu_custom_call" | custom-call | flops 11000000 | bytes 1024 | tf_op jit(solution)/shard_map/expand_forward/pallas_call | solution.py:800
  186.2 16.3 %ff_backward.2 = (f32[512,768]{1,0:T(8,128)}, bf16[4,384,512]{2,1,0:T(8,128)(2,1)}, bf16[4,384,512]{2,1,0:T(8,128)(2,1)}, bf16[4,96,512]{2,1,0:T(8,128)(2,1)}, b...) custom-call(s32[1]{0:T(128)} %bitcast.place_ref, bf16[512,768]{1,0:T(8,128)(2,1)} %get-tuple-element.409.grad_ref, ...), custom_call_target="tpu_custom_call" | custom-call | flops 11000000 | bytes 1024 | tf_op jit(solution)/shard_map/ff_backward/pallas_call | solution.py:997
  204.3 6.8 %owner_terms.5 = (bf16[2,384,384]{2,1,0:T(8,128)(2,1)}, bf16[2,384,384]{2,1,0:T(8,128)(2,1)}, bf16[2,384,384]{2,1,0:T(8,128)(2,1)}, bf16[2,384,384]{2,1,0:T(8,128)(2,1)}) custom-call(bf16[4,96,512]{2,1,0:T(8,128)(2,1)} %get-tuple-element.332.refs_0_, bf16[4,96,512]{2,1,0:T(8,128)(2,1)} %copy-done.67, ...), custom_call_target="tpu_custom_call" | custom-call | flops 11000000 | bytes 1024 | tf_op jit(solution)/shard_map/owner_terms/pallas_call | solution.py:1303
  212.5 8.7 %owner_terms.6 = (bf16[2,480,384]{2,1,0:T(8,128)(2,1)}, bf16[2,480,384]{2,1,0:T(8,128)(2,1)}, bf16[2,480,384]{2,1,0:T(8,128)(2,1)}, bf16[2,480,384]{2,1,0:T(8,128)(2,1)}) custom-call(bf16[4,384,512]{2,1,0:T(8,128)(2,1)} %get-tuple-element.438.refs_0_, bf16[4,384,512]{2,1,0:T(8,128)(2,1)} %copy-done.56, bf16[512,768]{1,0:T(8,128)(2,1)} %get-tuple-element.425.refs_2_, ...), custom_call_target="tpu_custom_call" | custom-call | flops 11000000 | bytes 1024 | tf_op jit(solution)/shard_map/owner_terms/pallas_call | solution.py:1303
  221.2 5.7 %collective-permute-done.35.refs_0_ = bf16[2,384,384]{2,1,0:T(8,128)(2,1)S(1)} collective-permute-done((bf16[2,384,384]{2,1,0:T(8,128)(2,1)}, bf16[2,384,384]{2,1,0:T(8,128)(2,1)S(1)}, u32[]{:S(2)}, u32[]{:S(2)}) %collective-permute-start.35) | collective-permute-done | bytes 589856 | tf_op jit(solution)/shard_map/ppermute | solution.py:383
  231.4 23.4 %attn_backward.2 = (f32[512,768]{1,0:T(8,128)}, bf16[3,4,96,512]{3,2,1,0:T(8,128)(2,1)}, bf16[3,4,96,512]{3,2,1,0:T(8,128)(2,1)}, f32[4,16,384]{2,1,0:T(8,128)},...) custom-call(s32[1]{0:T(128)} %bitcast.place_ref, ...), custom_call_target="tpu_custom_call" | custom-call | flops 11000000 | bytes 1024 | tf_op jit(solution)/shard_map/attn_backward/pallas_call | solution.py:1181
  255.1 3.7 collective-permute-start.41
  263.8 10.5 %owner_terms.7 = (bf16[2,688,384]{2,1,0:T(8,128)(2,1)}, bf16[2,672,384]{2,1,0:T(8,128)(2,1)}, bf16[2,688,384]{2,1,0:T(8,128)(2,1)}, bf16[2,672,384]{2,1,0:T(8,128)(2,1)}) custom-call(bf16[4,96,512]{2,1,0:T(8,128)(2,1)} %get-tuple-element.483.refs_0_, bf16[4,96,512]{2,1,0:T(8,128)(2,1)} %copy-done.66, ...), custom_call_target="tpu_custom_call" | custom-call | flops 11000000 | bytes 1024 | tf_op jit(solution)/shard_map/owner_terms/pallas_call | solution.py:1303
  279.6 16.5 %ff_backward.3 = (f32[512,768]{1,0:T(8,128)}, bf16[4,384,512]{2,1,0:T(8,128)(2,1)}, bf16[4,384,512]{2,1,0:T(8,128)(2,1)}, bf16[4,96,512]{2,1,0:T(8,128)(2,1)}, b...) custom-call(s32[1]{0:T(128)} %bitcast.place_ref, f32[512,768]{1,0:T(8,128)} %get-tuple-element.506.grad_ref, ...), custom_call_target="tpu_custom_call" | custom-call | flops 11000000 | bytes 1024 | tf_op jit(solution)/shard_map/ff_backward/pallas_call | solution.py:997
  296.1 3.7 collective-permute-done.48.refs_1_
  306.0 8.5 %owner_terms.8 = (bf16[2,480,384]{2,1,0:T(8,128)(2,1)}, bf16[2,480,384]{2,1,0:T(8,128)(2,1)}, bf16[2,480,384]{2,1,0:T(8,128)(2,1)}, bf16[2,480,384]{2,1,0:T(8,128)(2,1)}) custom-call(bf16[4,384,512]{2,1,0:T(8,128)(2,1)} %get-tuple-element.524.refs_0_, bf16[4,384,512]{2,1,0:T(8,128)(2,1)} %collective-permute-done.54.refs_1_, ...), custom_call_target="tpu_custom_call" | custom-call | flops 11000000 | bytes 1024 | tf_op jit(solution)/shard_map/owner_terms/pallas_call | solution.py:1303
  316.5 7.0 %collective-permute-start.58 = (bf16[1360,384]{1,0:T(8,128)(2,1)S(1)}, bf16[1360,384]{1,0:T(8,128)(2,1)S(1)}, u32[]{:S(2)}, u32[]{:S(2)}) collective-permute-start(bf16[1360,384]{1,0:T(8,128)(2,1)S(1)} %ends.7.refs_0_), channel_id=1, source_target_pairs={{0,1},{3,2},{4,5},{7,6},{8,9},{11,10},{12,13},{15,14},{16,17},{19,... | collective-permute-start | bytes 3133448 | tf_op jit(solution)/shard_map/ppermute | solution.py:663
  328.0 23.0 %attn_backward.3 = (bf16[512,768]{1,0:T(8,128)(2,1)}, bf16[3,4,96,512]{3,2,1,0:T(8,128)(2,1)}, bf16[3,4,96,512]{3,2,1,0:T(8,128)(2,1)}, f32[4,16,384]{2,1,0:T(8,128)}, f32[4,16,384]{2,1,0:T(8,128)}) custom-call(s32[1]{0:T(128)} %bitcast.place_ref, f32[512,768]{1,0:T(8,128)} %get-tuple-element.547.grad_ref, bf16[512,768]{1,0:T(8,128)(2,1)} %bitcast.33, ...), custom_call_target="tpu_custom_call" | custom-call | flops 11000000 | bytes 1024 | tf_op jit(solution)/shard_map/attn_backward/pallas_call | solution.py:1181
  351.0 5.1 %collective-permute-done.59 = bf16[768,384]{1,0:T(8,128)(2,1)S(1)} collective-permute-done((bf16[768,384]{1,0:T(8,128)(2,1)S(1)}, bf16[768,384]{1,0:T(8,128)(2,1)S(1)}, u32[]{:S(2)}, u32[]{:S(2)}) %collective-permute-start.59) | collective-permute-done | bytes 589856 | tf_op jit(solution)/shard_map/ppermute | solution.py:680
  363.6 5.6 %owner_terms.9 = (bf16[2,304,384]{2,1,0:T(8,128)(2,1)}, bf16[2,288,384]{2,1,0:T(8,128)(2,1)}, bf16[2,304,384]{2,1,0:T(8,128)(2,1)}, bf16[2,288,384]{2,1,0:T(8,128)(2,1)}) custom-call(bf16[3,4,96,512]{3,2,1,0:T(8,128)(2,1)} %get-tuple-element.565.refs_0_, bf16[3,4,96,512]{3,2,1,0:T(8,128)(2,1)} %collective-permute-done.64.refs_1_, ...), custom_call_target="tpu_custom_call" | custom-call | flops 11000000 | bytes 1024 | tf_op jit(solution)/shard_map/owner_terms/pallas_call | solution.py:1303
  378.5 14.9 %collective-permute-start.71 = (bf16[960,384]{1,0:T(8,128)(2,1)S(1)}, bf16[960,384]{1,0:T(8,128)(2,1)S(1)}, u32[]{:S(2)}, u32[]{:S(2)}) collective-permute-start(bf16[960,384]{1,0:T(8,128)(2,1)S(1)} %ends.9.refs_0_), channel_id=1, source_target_pairs={{0,1},{3,2},{4,5},{7,6},{8,9},{11,10},{12,13},{15,14},{16,17},{19,... | collective-permute-start | bytes 2211848 | tf_op jit(solution)/shard_map/ppermute | solution.py:663
  394.4 9.3 %reduce_forward.3 = bf16[512,768]{1,0:T(8,128)(2,1)} custom-call(s32[1]{0:T(128)} %bitcast.place_ref, s32[2,1]{1,0:T(2,128)} %copy.29.live_ref, f32[512,768]{1,0:T(8,128)} %get-tuple-element.578.middle_ref, bf16[512,3072]{1,0:T(8,128)(2,1)} %get-tuple-element.579.refs_2_.active_ref, f32[8,768]{1,0:T(8,128)} %copy-done.32, bf16[768,768]{1,0:T(8,128)(2,1)} %copy-done.12, ...), custom_call_target="tpu_custom_call" | custom-call | flops 11000000 | bytes 1024 | tf_op jit(solution)/shard_map/reduce_forward/pallas_call | solution.py:864
  417.9 6.0 %collective-permute-done.70.refs_1_ = bf16[592,384]{1,0:T(8,128)(2,1)S(1)} collective-permute-done((bf16[592,384]{1,0:T(8,128)(2,1)S(1)}, bf16[592,384]{1,0:T(8,128)(2,1)S(1)}, u32[]{:S(2)}, u32[]{:S(2)}) %collective-permute-start.70) | collective-permute-done | bytes 454688 | tf_op jit(solution)/shard_map/ppermute | solution.py:663
  430.1 3.3 pad_maximum_fusion.1
  434.8 17.3 %collective-permute-done.76 = bf16[960,384]{1,0:T(8,128)(2,1)} collective-permute-done((bf16[960,384]{1,0:T(8,128)(2,1)S(1)}, bf16[960,384]{1,0:T(8,128)(2,1)}, u32[]{:S(2)}, u32[]{:S(2)}) %collective-permute-start.76) | collective-permute-done | bytes 737312 | tf_op jit(solution)/shard_map/ppermute | solution.py:680
  (367 shorter events, 135.0 us)
Async XLA Ops:
  35.2 35.9 %collective-permute-start.9 = (bf16[976,768]{1,0:T(8,128)(2,1)S(1)}, bf16[976,768]{1,0:T(8,128)(2,1)S(1)}, u32[]{:S(2)}, u32[]{:S(2)}) collective-permute-start(bf16[976,768]{1,0:T(8,128)(2,1)S(1)} %get-tuple-element.328), channel_id=1, source_target_pairs={{0,16},{4,20},{8,24},{12,28},{16,0},{20,4},{24,8},{28,12},{1,17},{... | collective-permute-start | bytes 4497416 | tf_op jit(solution)/shard_map/ppermute | solution.py:387
  36.7 34.4 %collective-permute-start.8 = (bf16[960,768]{1,0:T(8,128)(2,1)S(1)}, bf16[960,768]{1,0:T(8,128)(2,1)S(1)}, u32[]{:S(2)}, u32[]{:S(2)}) collective-permute-start(bf16[960,768]{1,0:T(8,128)(2,1)S(1)} %get-tuple-element.327), channel_id=1, source_target_pairs={{0,8},{4,12},{8,0},{12,4},{16,24},{20,28},{24,16},{28,20},{1,9},{5... | collective-permute-start | bytes 4423688 | tf_op jit(solution)/shard_map/ppermute | solution.py:383
  74.7 28.3 %collective-permute-start.13 = (bf16[784,768]{1,0:T(8,128)(2,1)}, bf16[784,768]{1,0:T(8,128)(2,1)S(1)}, u32[]{:S(2)}, u32[]{:S(2)}) collective-permute-start(bf16[784,768]{1,0:T(8,128)(2,1)} %get-tuple-element.344), channel_id=1, source_target_pairs={{0,8},{4,12},{8,0},{12,4},{16,24},{20,28},{24,16},{28,20},{1,9},{5... | collective-permute-start | bytes 3612680 | tf_op jit(solution)/shard_map/ppermute | solution.py:383
  76.2 28.0 %collective-permute-start.14 = (bf16[784,768]{1,0:T(8,128)(2,1)}, bf16[784,768]{1,0:T(8,128)(2,1)S(1)}, u32[]{:S(2)}, u32[]{:S(2)}) collective-permute-start(bf16[784,768]{1,0:T(8,128)(2,1)} %get-tuple-element.345), channel_id=1, source_target_pairs={{0,16},{4,20},{8,24},{12,28},{16,0},{20,4},{24,8},{28,12},{1,17},{... | collective-permute-start | bytes 3612680 | tf_op jit(solution)/shard_map/ppermute | solution.py:387
  105.9 35.5 %collective-permute-start.18 = (bf16[976,768]{1,0:T(8,128)(2,1)}, bf16[976,768]{1,0:T(8,128)(2,1)S(1)}, u32[]{:S(2)}, u32[]{:S(2)}) collective-permute-start(bf16[976,768]{1,0:T(8,128)(2,1)} %get-tuple-element.363), channel_id=1, source_target_pairs={{0,16},{4,20},{8,24},{12,28},{16,0},{20,4},{24,8},{28,12},{1,17},{... | collective-permute-start | bytes 4497416 | tf_op jit(solution)/shard_map/ppermute | solution.py:387
  106.6 34.6 %collective-permute-start.17 = (bf16[960,768]{1,0:T(8,128)(2,1)}, bf16[960,768]{1,0:T(8,128)(2,1)S(1)}, u32[]{:S(2)}, u32[]{:S(2)}) collective-permute-start(bf16[960,768]{1,0:T(8,128)(2,1)} %get-tuple-element.362), channel_id=1, source_target_pairs={{0,8},{4,12},{8,0},{12,4},{16,24},{20,28},{24,16},{28,20},{1,9},{5... | collective-permute-start | bytes 4423688 | tf_op jit(solution)/shard_map/ppermute | solution.py:383
  107.1 25.3 %collective-permute-start.19 = (bf16[512,768]{1,0:T(8,128)(2,1)}, bf16[512,768]{1,0:T(8,128)(2,1)}, u32[]{:S(2)}, u32[]{:S(2)}) collective-permute-start(bf16[512,768]{1,0:T(8,128)(2,1)} %get-tuple-element.371.refs_2_), channel_id=1, source_target_pairs={{0,4},{4,0},{8,12},{12,8},{16,20},{20,16},{24,28},{28,24},{1,5},{5... | collective-permute-start | bytes 2359304 | tf_op jit(solution)/shard_map/ppermute | solution.py:379
  107.7 24.7 %collective-permute-start.20 = (bf16[512,768]{1,0:T(8,128)(2,1)S(1)}, bf16[512,768]{1,0:T(8,128)(2,1)S(1)}, u32[]{:S(2)}, u32[]{:S(2)}) collective-permute-start(bf16[512,768]{1,0:T(8,128)(2,1)S(1)} %copy-done.58), channel_id=1, source_target_pairs={{0,4},{4,0},{8,12},{12,8},{16,20},{20,16},{24,28},{28,24},{1,5},{5... | collective-permute-start | bytes 2359304 | tf_op jit(solution)/shard_map/ppermute | solution.py:379
  141.4 43.5 %collective-permute-start.30 = (bf16[512,3072]{1,0:T(8,128)(2,1)}, bf16[512,3072]{1,0:T(8,128)(2,1)}, u32[]{:S(2)}, u32[]{:S(2)}) collective-permute-start(bf16[512,3072]{1,0:T(8,128)(2,1)} %get-tuple-element.407.active_ref.refs_2_), channel_id=1, source_target_pairs={{0,4},{4,0},{8,12},{12,8},{16,20},{20,16},{24,28},{28,24},{1,5},{5... | collective-permute-start | bytes 9437192 | tf_op jit(solution)/shard_map/ppermute | solution.py:379
  142.0 25.6 %collective-permute-start.25 = (bf16[512,768]{1,0:T(8,128)(2,1)}, bf16[512,768]{1,0:T(8,128)(2,1)}, u32[]{:S(2)}, u32[]{:S(2)}) collective-permute-start(bf16[512,768]{1,0:T(8,128)(2,1)} %get-tuple-element.390.refs_2_), channel_id=1, source_target_pairs={{0,4},{4,0},{8,12},{12,8},{16,20},{20,16},{24,28},{28,24},{1,5},{5... | collective-permute-start | bytes 2359304 | tf_op jit(solution)/shard_map/ppermute | solution.py:379
  142.7 24.9 %collective-permute-start.23 = (bf16[384,768]{1,0:T(8,128)(2,1)S(1)}, bf16[384,768]{1,0:T(8,128)(2,1)S(1)}, u32[]{:S(2)}, u32[]{:S(2)}) collective-permute-start(bf16[384,768]{1,0:T(8,128)(2,1)S(1)} %get-tuple-element.379), channel_id=1, source_target_pairs={{0,8},{4,12},{8,0},{12,4},{16,24},{20,28},{24,16},{28,20},{1,9},{5... | collective-permute-start | bytes 1769480 | tf_op jit(solution)/shard_map/ppermute | solution.py:383
  149.9 17.6 %collective-permute-start.24 = (bf16[384,768]{1,0:T(8,128)(2,1)S(1)}, bf16[384,768]{1,0:T(8,128)(2,1)}, u32[]{:S(2)}, u32[]{:S(2)}) collective-permute-start(bf16[384,768]{1,0:T(8,128)(2,1)S(1)} %get-tuple-element.380), channel_id=1, source_target_pairs={{0,16},{4,20},{8,24},{12,28},{16,0},{20,4},{24,8},{28,12},{1,17},{... | collective-permute-start | bytes 1769480 | tf_op jit(solution)/shard_map/ppermute | solution.py:387
  167.6 17.3 %collective-permute-start.28 = (bf16[512,768]{1,0:T(8,128)(2,1)}, bf16[512,768]{1,0:T(8,128)(2,1)S(1)}, u32[]{:S(2)}, u32[]{:S(2)}) collective-permute-start(bf16[512,768]{1,0:T(8,128)(2,1)} %get-tuple-element.405.refs_6_), channel_id=1, source_target_pairs={{0,4},{4,0},{8,12},{12,8},{16,20},{20,16},{24,28},{28,24},{1,5},{5... | collective-permute-start | bytes 2359304 | tf_op jit(solution)/shard_map/ppermute | solution.py:379
  227.0 27.8 %collective-permute-start.39 = (bf16[2,480,384]{2,1,0:T(8,128)(2,1)}, bf16[2,480,384]{2,1,0:T(8,128)(2,1)S(1)}, u32[]{:S(2)}, u32[]{:S(2)}) collective-permute-start(bf16[2,480,384]{2,1,0:T(8,128)(2,1)} %get-tuple-element.457), channel_id=1, source_target_pairs={{0,8},{4,12},{8,0},{12,4},{16,24},{20,28},{24,16},{28,20},{1,9},{5... | collective-permute-start | bytes 2211848 | tf_op jit(solution)/shard_map/ppermute | solution.py:383
  228.5 26.3 %collective-permute-start.40 = (bf16[2,480,384]{2,1,0:T(8,128)(2,1)}, bf16[2,480,384]{2,1,0:T(8,128)(2,1)S(1)}, u32[]{:S(2)}, u32[]{:S(2)}) collective-permute-start(bf16[2,480,384]{2,1,0:T(8,128)(2,1)} %get-tuple-element.458), channel_id=1, source_target_pairs={{0,16},{4,20},{8,24},{12,28},{16,0},{20,4},{24,8},{28,12},{1,17},{... | collective-permute-start | bytes 2211848 | tf_op jit(solution)/shard_map/ppermute | solution.py:387
  229.6 25.3 %collective-permute-start.37 = (bf16[384,384]{1,0:T(8,128)(2,1)S(1)}, bf16[384,384]{1,0:T(8,128)(2,1)S(1)}, u32[]{:S(2)}, u32[]{:S(2)}) collective-permute-start(bf16[384,384]{1,0:T(8,128)(2,1)S(1)} %get-tuple-element.453), channel_id=1, source_target_pairs={{0,16},{4,20},{8,24},{12,28},{16,0},{20,4},{24,8},{28,12},{1,17},{... | collective-permute-start | bytes 884744 | tf_op jit(solution)/shard_map/ppermute | solution.py:387
  230.9 23.9 %collective-permute-start.38 = (bf16[384,384]{1,0:T(8,128)(2,1)S(1)}, bf16[384,384]{1,0:T(8,128)(2,1)S(1)}, u32[]{:S(2)}, u32[]{:S(2)}) collective-permute-start(bf16[384,384]{1,0:T(8,128)(2,1)S(1)} %get-tuple-element.454), channel_id=1, source_target_pairs={{0,8},{4,12},{8,0},{12,4},{16,24},{20,28},{24,16},{28,20},{1,9},{5... | collective-permute-start | bytes 884744 | tf_op jit(solution)/shard_map/ppermute | solution.py:383
  255.1 19.2 %collective-permute-start.41 = (bf16[768,384]{1,0:T(8,128)(2,1)S(1)}, bf16[768,384]{1,0:T(8,128)(2,1)S(1)}, u32[]{:S(2)}, u32[]{:S(2)}) collective-permute-start(bf16[768,384]{1,0:T(8,128)(2,1)S(1)} %ends.5.refs_0_), channel_id=1, source_target_pairs={{0,1},{3,2},{4,5},{7,6},{8,9},{11,10},{12,13},{15,14},{16,17},{19,... | collective-permute-start | bytes 1769480 | tf_op jit(solution)/shard_map/ppermute | solution.py:663
  274.3 25.5 %collective-permute-start.47 = (bf16[2,688,384]{2,1,0:T(8,128)(2,1)}, bf16[2,688,384]{2,1,0:T(8,128)(2,1)S(1)}, u32[]{:S(2)}, u32[]{:S(2)}) collective-permute-start(bf16[2,688,384]{2,1,0:T(8,128)(2,1)} %get-tuple-element.496), channel_id=1, source_target_pairs={{0,8},{4,12},{8,0},{12,4},{16,24},{20,28},{24,16},{28,20},{1,9},{5... | collective-permute-start | bytes 3170312 | tf_op jit(solution)/shard_map/ppermute | solution.py:383
  274.9 24.9 %collective-permute-start.48 = (bf16[2,672,384]{2,1,0:T(8,128)(2,1)}, bf16[2,672,384]{2,1,0:T(8,128)(2,1)S(1)}, u32[]{:S(2)}, u32[]{:S(2)}) collective-permute-start(bf16[2,672,384]{2,1,0:T(8,128)(2,1)} %get-tuple-element.497), channel_id=1, source_target_pairs={{0,16},{4,20},{8,24},{12,28},{16,0},{20,4},{24,8},{28,12},{1,17},{... | collective-permute-start | bytes 3096584 | tf_op jit(solution)/shard_map/ppermute | solution.py:387
  276.4 19.7 %collective-permute-start.49 = (bf16[960,384]{1,0:T(8,128)(2,1)S(1)}, bf16[960,384]{1,0:T(8,128)(2,1)S(1)}, u32[]{:S(2)}, u32[]{:S(2)}) collective-permute-start(bf16[960,384]{1,0:T(8,128)(2,1)S(1)} %ends.6.refs_0_), channel_id=1, source_target_pairs={{0,1},{3,2},{4,5},{7,6},{8,9},{11,10},{12,13},{15,14},{16,17},{19,... | collective-permute-start | bytes 2211848 | tf_op jit(solution)/shard_map/ppermute | solution.py:663
  316.5 39.6 %collective-permute-start.58 = (bf16[1360,384]{1,0:T(8,128)(2,1)S(1)}, bf16[1360,384]{1,0:T(8,128)(2,1)S(1)}, u32[]{:S(2)}, u32[]{:S(2)}) collective-permute-start(bf16[1360,384]{1,0:T(8,128)(2,1)S(1)} %ends.7.refs_0_), channel_id=1, source_target_pairs={{0,1},{3,2},{4,5},{7,6},{8,9},{11,10},{12,13},{15,14},{16,17},{19,... | collective-permute-start | bytes 3133448 | tf_op jit(solution)/shard_map/ppermute | solution.py:663
  323.7 32.4 %collective-permute-start.60 = (bf16[960,384]{1,0:T(8,128)(2,1)S(1)}, bf16[960,384]{1,0:T(8,128)(2,1)S(1)}, u32[]{:S(2)}, u32[]{:S(2)}) collective-permute-start(bf16[960,384]{1,0:T(8,128)(2,1)S(1)} %plus.13), channel_id=1, source_target_pairs={{1,0},{2,3},{5,4},{6,7},{9,8},{10,11},{13,12},{14,15},{17,16},{18,... | collective-permute-start | bytes 2211848 | tf_op jit(solution)/shard_map/ppermute | solution.py:680
  325.0 31.1 %collective-permute-start.56 = (bf16[2,480,384]{2,1,0:T(8,128)(2,1)}, bf16[2,480,384]{2,1,0:T(8,128)(2,1)S(1)}, u32[]{:S(2)}, u32[]{:S(2)}) collective-permute-start(bf16[2,480,384]{2,1,0:T(8,128)(2,1)} %get-tuple-element.535), channel_id=1, source_target_pairs={{0,8},{4,12},{8,0},{12,4},{16,24},{20,28},{24,16},{28,20},{1,9},{5... | collective-permute-start | bytes 2211848 | tf_op jit(solution)/shard_map/ppermute | solution.py:383
  325.9 30.2 %collective-permute-start.57 = (bf16[2,480,384]{2,1,0:T(8,128)(2,1)S(1)}, bf16[2,480,384]{2,1,0:T(8,128)(2,1)S(1)}, u32[]{:S(2)}, u32[]{:S(2)}) collective-permute-start(bf16[2,480,384]{2,1,0:T(8,128)(2,1)S(1)} %copy-done.72), channel_id=1, source_target_pairs={{0,16},{4,20},{8,24},{12,28},{16,0},{20,4},{24,8},{28,12},{1,17},{... | collective-permute-start | bytes 2211848 | tf_op jit(solution)/shard_map/ppermute | solution.py:387
  326.7 29.4 %collective-permute-start.59 = (bf16[768,384]{1,0:T(8,128)(2,1)S(1)}, bf16[768,384]{1,0:T(8,128)(2,1)S(1)}, u32[]{:S(2)}, u32[]{:S(2)}) collective-permute-start(bf16[768,384]{1,0:T(8,128)(2,1)S(1)} %plus.12), channel_id=1, source_target_pairs={{1,0},{2,3},{5,4},{6,7},{9,8},{10,11},{13,12},{14,15},{17,16},{18,... | collective-permute-start | bytes 1769480 | tf_op jit(solution)/shard_map/ppermute | solution.py:680
  373.5 42.9 %collective-permute-start.75 = (bf16[1360,384]{1,0:T(8,128)(2,1)S(1)}, bf16[1360,384]{1,0:T(8,128)(2,1)}, u32[]{:S(2)}, u32[]{:S(2)}) collective-permute-start(bf16[1360,384]{1,0:T(8,128)(2,1)S(1)} %plus.18), channel_id=1, source_target_pairs={{1,0},{2,3},{5,4},{6,7},{9,8},{10,11},{13,12},{14,15},{17,16},{18,... | collective-permute-start | bytes 3133448 | tf_op jit(solution)/shard_map/ppermute | solution.py:680
  375.0 28.6 %collective-permute-start.67 = (bf16[2,288,384]{2,1,0:T(8,128)(2,1)S(1)}, bf16[2,288,384]{2,1,0:T(8,128)(2,1)S(1)}, u32[]{:S(2)}, u32[]{:S(2)}) collective-permute-start(bf16[2,288,384]{2,1,0:T(8,128)(2,1)S(1)} %copy-done.74), channel_id=1, source_target_pairs={{0,16},{4,20},{8,24},{12,28},{16,0},{20,4},{24,8},{28,12},{1,17},{... | collective-permute-start | bytes 1327112 | tf_op jit(solution)/shard_map/ppermute | solution.py:387
  376.4 27.2 %collective-permute-start.66 = (bf16[2,304,384]{2,1,0:T(8,128)(2,1)S(1)}, bf16[2,304,384]{2,1,0:T(8,128)(2,1)S(1)}, u32[]{:S(2)}, u32[]{:S(2)}) collective-permute-start(bf16[2,304,384]{2,1,0:T(8,128)(2,1)S(1)} %copy-done.73), channel_id=1, source_target_pairs={{0,8},{4,12},{8,0},{12,4},{16,24},{20,28},{24,16},{28,20},{1,9},{5... | collective-permute-start | bytes 1400840 | tf_op jit(solution)/shard_map/ppermute | solution.py:383
  378.5 37.0 %collective-permute-start.71 = (bf16[960,384]{1,0:T(8,128)(2,1)S(1)}, bf16[960,384]{1,0:T(8,128)(2,1)S(1)}, u32[]{:S(2)}, u32[]{:S(2)}) collective-permute-start(bf16[960,384]{1,0:T(8,128)(2,1)S(1)} %ends.9.refs_0_), channel_id=1, source_target_pairs={{0,1},{3,2},{4,5},{7,6},{8,9},{11,10},{12,13},{15,14},{16,17},{19,... | collective-permute-start | bytes 2211848 | tf_op jit(solution)/shard_map/ppermute | solution.py:663
  424.1 28.0 %collective-permute-start.76 = (bf16[960,384]{1,0:T(8,128)(2,1)S(1)}, bf16[960,384]{1,0:T(8,128)(2,1)}, u32[]{:S(2)}, u32[]{:S(2)}) collective-permute-start(bf16[960,384]{1,0:T(8,128)(2,1)S(1)} %plus.19), channel_id=1, source_target_pairs={{1,0},{2,3},{5,4},{6,7},{9,8},{10,11},{13,12},{14,15},{17,16},{18,... | collective-permute-start | bytes 2211848 | tf_op jit(solution)/shard_map/ppermute | solution.py:680
  433.5 25.9 %collective-permute-start.74 = (bf16[592,384]{1,0:T(8,128)(2,1)S(1)}, bf16[592,384]{1,0:T(8,128)(2,1)S(1)}, u32[]{:S(2)}, u32[]{:S(2)}) collective-permute-start(bf16[592,384]{1,0:T(8,128)(2,1)S(1)} %plus.17), channel_id=1, source_target_pairs={{1,0},{2,3},{5,4},{6,7},{9,8},{10,11},{13,12},{14,15},{17,16},{18,... | collective-permute-start | bytes 1363976 | tf_op jit(solution)/shard_map/ppermute | solution.py:680
  (126 other events, 1064.7 us)

commit v3 on v2

--- a/solution.py
+++ b/solution.py
@@ -363,8 +363,9 @@
 FF_PARTS = 4
 f32 = jnp.float32
 bf16 = jnp.bfloat16
-VMEM_BYTES = 56 * 1024 * 1024
+VMEM_BYTES = 58 * 1024 * 1024
 SMALL_VMEM_BYTES = 24 * 1024 * 1024
+LARGE_VMEM_BYTES = 60 * 1024 * 1024
 
 
 def dot_nt(left, right):
@@ -425,7 +426,7 @@
 
 
 def in_any():
-    return pl.BlockSpec(memory_space=pl.ANY)
+    return pl.BlockSpec(memory_space=pltpu.HBM)
 
 
 def in_smem():
@@ -444,6 +445,10 @@
 
 def rows_spec(width):
     return pl.BlockSpec((ROWS, width), lambda image: (image, 0))
+
+
+def part_spec(tokens):
+    return pl.BlockSpec((tokens, WIDTH), lambda part: (0, part))
 
 
 def fixed(shape):
@@ -456,71 +461,60 @@
     return centre * root, root
 
 
-def own_copies(sources, target, sems, kind, layer):
-    if kind == "attn":
-        heads, merge = sources[:2]
-        pairs = [(heads.at[layer, at], target.at[pl.ds(96 * at, 96)]) for at in range(3)]
-        pairs.append((merge.at[layer], target.at[pl.ds(288, 96)]))
-    else:
-        expand, reduce = sources[2:]
-        pairs = [(expand.at[layer], target.at[pl.ds(0, 384)])]
-        for part in range(FF_PARTS):
-            pairs.append(
-                (
-                    reduce.at[layer, :, pl.ds(WIDTH * part, WIDTH)],
-                    target.at[pl.ds(384 + 96 * part, 96)],
-                )
-            )
-    return [pltpu.make_async_copy(*pair, sems.at[at]) for at, pair in enumerate(pairs)]
+PACK_ROWS = {"attn": 400, "ff": 768, "expand": 384, "reduce": 384}
+PACK_CUTS = {"attn": 192, "ff": 384, "expand": 192, "reduce": 192}
 
 
 def own_packs(wanted, matrices, vectors):
     count = len(wanted)
+    needed = [
+        at
+        for at, users in enumerate(
+            (("attn",), ("attn",), ("ff", "expand"), ("ff", "reduce"))
+        )
+        if any(kind in users for kind, layer in wanted)
+    ]
 
     def kernel(*refs):
-        sources, vector_refs = refs[:4], refs[4:12]
-        outs = refs[12 : 12 + count]
-        rows, low_rows, sems, vector_sems = refs[12 + count :]
-        copies = []
-        for at, (kind, layer) in enumerate(wanted):
-            copies += own_copies(sources, outs[at], sems.at[at], kind, layer)
-        run_all(copies, "start")
-        vector_copies = []
-        for at, (kind, layer) in enumerate(wanted):
+        heads_ref, merge_ref, expand_ref, reduce_ref = (
+            refs[needed.index(at)] if at in needed else None for at in range(4)
+        )
+        vector_refs = refs[len(needed) : len(needed) + 8]
+        outs, rows = refs[len(needed) + 8 : -1], refs[-1]
+        for out, (kind, layer) in zip(outs, wanted):
             if kind == "attn":
+                for at in range(3):
+                    out[96 * at : 96 * at + 96] = heads_ref[layer, at]
+                out[288:384] = merge_ref[layer]
                 rows[...] = jnp.zeros_like(rows)
                 rows[0:2, 0:96] = vector_refs[0][layer].astype(f32)
                 for row in range(2, 8):
                     values = vector_refs[row - 1][...].astype(f32)
                     rows[row : row + 1, 0:96] = values[layer : layer + 1]
                 rows[8:9, 0:384] = vector_refs[7][...].astype(f32)[layer : layer + 1]
-                low_rows[at] = rows[...].astype(bf16)
-                vector_copies.append(
-                    pltpu.make_async_copy(
-                        low_rows.at[at], outs[at].at[pl.ds(384, 16)], vector_sems.at[at]
-                    )
-                )
-        run_all(vector_copies, "start")
-        run_all(copies + vector_copies, "wait")
-
+                out[384:400] = rows[...].astype(bf16)
+            if kind in ("ff", "expand"):
+                out[0:384] = expand_ref[layer]
+            if kind in ("ff", "reduce"):
+                first = 384 if kind == "ff" else 0
+                for part in range(FF_PARTS):
+                    out[first + 96 * part : first + 96 * part + 96] = reduce_ref[
+                        layer, :, WIDTH * part : WIDTH * (part + 1)
+                    ]
+
+    in_vmem = pl.BlockSpec(memory_space=pltpu.VMEM)
     return pl.pallas_call(
         kernel,
-        in_specs=[in_any()] * 4 + [pl.BlockSpec(memory_space=pltpu.VMEM)] * 8,
-        out_specs=[in_any()] * count,
+        in_specs=[in_vmem] * (len(needed) + 8),
+        out_specs=[in_vmem] * count,
         out_shape=[
-            jax.ShapeDtypeStruct((400 if kind == "attn" else 768, WIDTH), bf16)
-            for kind, layer in wanted
+            jax.ShapeDtypeStruct((PACK_ROWS[kind], WIDTH), bf16) for kind, layer in wanted
         ],
-        scratch_shapes=[
-            pltpu.VMEM((16, WIDTH), f32),
-            pltpu.VMEM((count, 16, WIDTH), bf16),
-            pltpu.SemaphoreType.DMA((count, 5)),
-            pltpu.SemaphoreType.DMA((count,)),
-        ],
-        compiler_params=pltpu.CompilerParams(vmem_limit_bytes=SMALL_VMEM_BYTES),
+        scratch_shapes=[pltpu.VMEM((16, WIDTH), f32)],
+        compiler_params=pltpu.CompilerParams(vmem_limit_bytes=LARGE_VMEM_BYTES),
         cost_estimate=cost(0.01),
         name="own_packs",
-    )(*matrices, *vectors)
+    )(*[matrices[at] for at in needed], *vectors)
 
 
 def join_rows(pieces_of):
@@ -546,7 +540,7 @@
     return pl.pallas_call(
         kernel,
         in_specs=[in_any()] * len(flat),
-        out_specs=[in_any()] * len(heights),
+        out_specs=[pl.BlockSpec(memory_space=pltpu.VMEM)] * len(heights),
         out_shape=[jax.ShapeDtypeStruct((rows, WIDTH), bf16) for rows in heights],
         scratch_shapes=[pltpu.SemaphoreType.DMA((len(flat),))],
         compiler_params=pltpu.CompilerParams(vmem_limit_bytes=SMALL_VMEM_BYTES),
@@ -600,7 +594,7 @@
         out_specs=[pl.BlockSpec(memory_space=pltpu.VMEM)] * 2,
         out_shape=[shape((8, WIDTH), f32), shape((4, 1, WIDTH), f32)],
         scratch_shapes=[pltpu.VMEM((8, 16, WIDTH), bf16), pltpu.SemaphoreType.DMA((8,))],
-        compiler_params=pltpu.CompilerParams(vmem_limit_bytes=SMALL_VMEM_BYTES),
+        compiler_params=pltpu.CompilerParams(vmem_limit_bytes=LARGE_VMEM_BYTES),
         cost_estimate=cost(0.01),
         name="gathered_vectors",
     )(place, *[used[delta][0] for delta in deltas])
@@ -683,11 +677,22 @@
 SM_HB0, SM_HB1, SM_MB, SM_G1, SM_S1, SM_G2, SM_S2, SM_RB = range(8)
 
 
-def heads_copies(place_now, packs, regions, blocks, sems):
-    return [
-        block_copies(place_now, packs, regions, 96 * at, 96, blocks.at[at], sems.at[at])
-        for at in range(4)
-    ]
+def unit_copies(place, refs, regions, first, blocks, sems):
+    copies = []
+    count = 96 * blocks.shape[0]
+    for array_at, delta, low, high, start in regions:
+        begin, end = max(low, first), min(high, first + count)
+        if begin < end:
+            units = (end - begin) // 96
+            source = refs[array_at].at[pl.ds(start + begin - low, end - begin)]
+            copies.append(
+                pltpu.make_async_copy(
+                    source.reshape(units, 96, WIDTH),
+                    blocks.at[pl.ds((begin - first) // 96, units), place ^ delta],
+                    sems.at[len(copies)],
+                )
+            )
+    return copies
 
 
 def attn_forward(place, hidden, small, pack):
@@ -697,12 +702,11 @@
         middle_ref, normed_ref, qkv_ref, mixed_ref, blocks, sems = rest[PIECES:]
         place_now = place_ref[0]
         image = pl.program_id(0)
-        copies = heads_copies(place_now, packs, pack[1], blocks, sems)
+        copies = unit_copies(place_now, packs, pack[1], 0, blocks, sems)
 
         @pl.when(image == 0)
         def begin():
-            for group in copies:
-                run_all(group, "start")
+            run_all(copies, "start")
 
         rows = hidden_ref[...].astype(f32)
         unit, root = normalise(rows)
@@ -711,8 +715,7 @@
 
         @pl.when(image == 0)
         def arrive():
-            for group in copies:
-                run_all(group, "wait")
+            run_all(copies, "wait")
 
         for member, bias in ((0, SM_HB0), (1, None), (2, SM_HB1)):
             block = blocks[member].reshape(WIDTH, WIDTH)
@@ -722,20 +725,19 @@
             qkv_ref[:, WIDTH * member : WIDTH * (member + 1)] = made.astype(bf16)
         lane = lax.broadcasted_iota(jnp.int32, (ROWS, 128), 1)
         for pair in range(HEADS // 2):
-            q_pair = qkv_ref[:, 128 * pair : 128 * pair + 128]
+            q_pair = qkv_ref[:, 128 * pair : 128 * pair + 128] * HEAD_DIM**-0.5
             k_pair = qkv_ref[:, WIDTH + 128 * pair : WIDTH + 128 * pair + 128]
             v_pair = qkv_ref[:, 2 * WIDTH + 128 * pair : 2 * WIDTH + 128 * pair + 128]
             parts = []
             for half in range(2):
-                q_one = jnp.where((lane < 64) == (half == 0), q_pair, jnp.zeros_like(q_pair))
-                scores = dot_nt(q_one, k_pair) * (HEAD_DIM**-0.5)
+                here = (lane < 64) == (half == 0)
+                scores = dot_nt(jnp.where(here, q_pair, jnp.zeros_like(q_pair)), k_pair)
                 peak = jnp.max(scores, axis=-1, keepdims=True)
-                powers = jnp.exp(scores - peak)
-                total = jnp.sum(powers, axis=-1, keepdims=True)
-                attend = (powers / total).astype(bf16)
-                parts.append(dot_nn(attend, v_pair))
-            mixed_ref[:, 128 * pair : 128 * pair + 128] = jnp.where(
-                lane < 64, parts[0], parts[1]
+                powers = jnp.exp(scores - peak).astype(bf16)
+                parts.append(dot_nn(powers, jnp.where(here, v_pair, jnp.ones_like(v_pair))))
+            totals = pltpu.roll(jnp.where(lane < 64, parts[1], parts[0]), 64, 1)
+            mixed_ref[:, 128 * pair : 128 * pair + 128] = (
+                jnp.where(lane < 64, parts[0], parts[1]) / totals
             ).astype(bf16)
         merged = dot_nt(mixed_ref[...], blocks[3].reshape(WIDTH, WIDTH))
         middle_ref[...] = rows + (merged + small_ref[SM_MB : SM_MB + 1])
@@ -755,7 +757,7 @@
         ],
         scratch_shapes=[
             pltpu.VMEM((4, 8, 96, WIDTH), bf16),
-            pltpu.SemaphoreType.DMA((4, PIECES)),
+            pltpu.SemaphoreType.DMA((PIECES,)),
         ],
         compiler_params=params(),
         cost_estimate=cost(0.01),
@@ -764,50 +766,45 @@
 
 
 def expand_forward(place, middle, small, expand_bias, pack, first):
+    tokens = middle.shape[0]
 
     def kernel(place_ref, middle_ref, small_ref, bias_ref, *rest):
         packs = rest[:PIECES]
         normed_ref, active_ref, slope_ref, block, sems = rest[PIECES:]
-        image = pl.program_id(0)
+        part = pl.program_id(0)
         copies = block_copies(place_ref[0], packs, pack[1], first, 384, block, sems)
 
-        @pl.when(image == 0)
+        @pl.when(part == 0)
         def begin():
             run_all(copies, "start")
-
-        unit, root = normalise(middle_ref[...])
-        normed = (unit * small_ref[SM_G2 : SM_G2 + 1] + small_ref[SM_S2 : SM_S2 + 1]).astype(bf16)
-        normed_ref[...] = normed
-
-        @pl.when(image == 0)
-        def arrive():
+            unit, root = normalise(middle_ref[...])
+            normed_ref[...] = (
+                unit * small_ref[SM_G2 : SM_G2 + 1] + small_ref[SM_S2 : SM_S2 + 1]
+            ).astype(bf16)
             run_all(copies, "wait")
 
-        for part in range(FF_PARTS):
-            weight = block[2 * part : 2 * part + 2].reshape(WIDTH, WIDTH)
-            point = dot_nt(normed, weight) + bias_ref[part]
-            square = point * point
-            slant = jnp.tanh(0.7978845608028654 * point * (1.0 + 0.044715 * square))
-            upper = 0.5 + 0.5 * slant
-            columns = slice(WIDTH * part, WIDTH * (part + 1))
-            active_ref[:, columns] = (point * upper).astype(bf16)
-            bend = point * (0.7978845608028654 + (3 * 0.044715 * 0.7978845608028654) * square)
-            slope_ref[:, columns] = (upper + 0.5 * bend * (1.0 - slant * slant)).astype(bf16)
-
-    tokens = middle.shape[0]
+        weight = block[pl.ds(2 * part, 2)].reshape(WIDTH, WIDTH)
+        point = dot_nt(normed_ref[...], weight) + bias_ref[part]
+        square = point * point
+        slant = jnp.tanh(0.7978845608028654 * point * (1.0 + 0.044715 * square))
+        upper = 0.5 + 0.5 * slant
+        active_ref[...] = (point * upper).astype(bf16)
+        bend = point * (0.7978845608028654 + (3 * 0.044715 * 0.7978845608028654) * square)
+        slope_ref[...] = (upper + 0.5 * bend * (1.0 - slant * slant)).astype(bf16)
+
     hidden_units = FF_PARTS * WIDTH
     shape = jax.ShapeDtypeStruct
     return pl.pallas_call(
         kernel,
-        grid=(tokens // ROWS,),
+        grid=(FF_PARTS,),
         in_specs=[
             in_smem(),
-            rows_spec(WIDTH),
+            fixed(middle.shape),
             fixed(small.shape),
             fixed(expand_bias.shape),
         ]
         + [in_any()] * PIECES,
-        out_specs=[rows_spec(WIDTH), rows_spec(hidden_units), rows_spec(hidden_units)],
+        out_specs=[fixed(middle.shape), part_spec(tokens), part_spec(tokens)],
         out_shape=[
             shape((tokens, WIDTH), bf16),
             shape((tokens, hidden_units), bf16),
@@ -832,51 +829,60 @@
     ]
 
 
+def for_part(part, groups, what):
+    for at, group in enumerate(groups):
+
+        @pl.when(part == at)
+        def run():
+            run_all(group, what)
+
+
 def reduce_forward(place, live, middle, active, small, pack, first, last):
+    tokens = middle.shape[0]
 
     def kernel(place_ref, live_ref, middle_ref, active_ref, small_ref, *rest):
         packs = rest[:PIECES]
-        result_ref, blocks, sems = rest[PIECES:]
-        image = pl.program_id(0)
+        result_ref, total, blocks, sems = rest[PIECES:]
+        part = pl.program_id(0)
         copies = reduce_copies(place_ref[0], packs, pack[1], first, blocks, sems)
 
-        @pl.when(image == 0)
+        @pl.when(part == 0)
         def begin():
             for group in copies:
                 run_all(group, "start")
-
-        total = middle_ref[...] + small_ref[SM_RB : SM_RB + 1]
-        for part in range(FF_PARTS):
-
-            @pl.when(image == 0)
-            def arrive():
-                run_all(copies[part], "wait")
-
-            total = total + dot_nt(
-                active_ref[:, WIDTH * part : WIDTH * (part + 1)],
-                blocks[part].reshape(WIDTH, WIDTH),
-            )
-        if last:
-            total = total * live_ref[image, 0].astype(f32)
-        result_ref[...] = total.astype(result_ref.dtype)
-
-    tokens = middle.shape[0]
+            total[...] = middle_ref[...] + small_ref[SM_RB : SM_RB + 1]
+
+        for_part(part, copies, "wait")
+        total[...] += dot_nt(active_ref[...], blocks[part].reshape(WIDTH, WIDTH))
+
+        @pl.when(part == FF_PARTS - 1)
+        def end():
+            if last:
+                for image in range(tokens // ROWS):
+                    rows = slice(ROWS * image, ROWS * (image + 1))
+                    result_ref[rows] = (
+                        total[rows] * live_ref[image, 0].astype(f32)
+                    ).astype(result_ref.dtype)
+            else:
+                result_ref[...] = total[...].astype(result_ref.dtype)
+
     return pl.pallas_call(
         kernel,
-        grid=(tokens // ROWS,),
+        grid=(FF_PARTS,),
         in_specs=[
             in_smem(),
             in_smem(),
-            rows_spec(WIDTH),
-            rows_spec(FF_PARTS * WIDTH),
+            fixed(middle.shape),
+            part_spec(tokens),
             fixed(small.shape),
         ]
         + [in_any()] * PIECES,
-        out_specs=rows_spec(WIDTH),
+        out_specs=fixed(middle.shape),
         out_shape=jax.ShapeDtypeStruct((tokens, WIDTH), bf16 if last else f32),
         scratch_shapes=[
+            pltpu.VMEM((tokens, WIDTH), f32),
             pltpu.VMEM((FF_PARTS, 8, 96, WIDTH), bf16),
-            pltpu.SemaphoreType.DMA((4, PIECES)),
+            pltpu.SemaphoreType.DMA((FF_PARTS, PIECES)),
         ],
         compiler_params=params(),
         cost_estimate=cost(0.01),
@@ -919,9 +925,17 @@
     )(place, live, cotangent)
 
 
-def ff_backward(place, grad, slope, middle, small, pack):
-    def kernel(place_ref, grad_ref, slope_ref, middle_ref, small_ref, *rest):
-        packs = rest[:PIECES]
+def fetch(source, target, sem):
+    return pltpu.make_async_copy(source, target, sem)
+
+
+def ff_backward(place, grad, slope, middle, small, expand_pack, reduce_pack):
+    tokens = middle.shape[0]
+    (expand_arrays, expand_regions), expand_first = expand_pack
+    (reduce_arrays, reduce_regions), reduce_first = reduce_pack
+
+    def kernel(place_ref, grad_in, slope_in, middle_in, small_ref, *rest):
+        expand_packs, reduce_packs = rest[:PIECES], rest[PIECES : 2 * PIECES]
         (
             out_ref,
             pre_mine,
@@ -929,280 +943,311 @@
             attn_mine,
             attn_theirs,
             sums_ref,
+            grad_ref,
+            slope_ref,
+            middle_ref,
             expand_block,
             reduce_blocks,
             turned_pre,
             turned_attn,
+            pre_low,
             expand_sems,
             reduce_sems,
-        ) = rest[PIECES:]
+            in_sems,
+            out_sems,
+        ) = rest[2 * PIECES :]
         place_now = place_ref[0]
-        image = pl.program_id(0)
-        copies = reduce_copies(place_now, packs, pack[1], 384, reduce_blocks, reduce_sems)
-        expand_copies = block_copies(
-            place_now, packs, pack[1], 0, 384, expand_block, expand_sems
-        )
-
-        @pl.when(image == 0)
-        def begin():
-            for group in copies:
-                run_all(group, "start")
-            run_all(expand_copies, "start")
-            sums_ref[...] = jnp.zeros_like(sums_ref)
-
-        grad_rows = grad_ref[...].astype(f32)
-        low = grad_rows.astype(bf16)
-        sums_ref[2:3] += jnp.sum(low.astype(f32), axis=0, keepdims=True)
         core = place_now & 1
         chip = place_now >> 1
-        back = jnp.zeros((ROWS, WIDTH), f32)
+        copies = reduce_copies(
+            place_now, reduce_packs, reduce_regions, reduce_first, reduce_blocks, reduce_sems
+        )
+        expand_copies = block_copies(
+            place_now, expand_packs, expand_regions, expand_first, 384, expand_block, expand_sems
+        )
+        grad_copy = fetch(grad_in, grad_ref, in_sems.at[0])
+        middle_copy = fetch(middle_in, middle_ref, in_sems.at[1])
+        slope_copies = [
+            fetch(
+                slope_in.at[:, pl.ds(WIDTH * part, WIDTH)], slope_ref.at[part], in_sems.at[2 + part]
+            )
+            for part in range(FF_PARTS)
+        ]
+        grad_copy.start()
         for part in range(FF_PARTS):
-
-            @pl.when(image == 0)
-            def arrive():
-                run_all(copies[part], "wait")
-                if part == 0:
-                    run_all(expand_copies, "wait")
-
-            columns = slice(WIDTH * part, WIDTH * (part + 1))
+            run_all(copies[part], "start")
+            slope_copies[part].start()
+        run_all(expand_copies, "start")
+        middle_copy.start()
+
+        sent = []
+
+        def send(source, target):
+            copy = pltpu.make_async_copy(source, target, out_sems.at[len(sent)])
+            copy.start()
+            sent.append(copy)
+
+        grad_copy.wait()
+        low = grad_ref[...].astype(bf16)
+        sums_ref[2:3] = jnp.sum(low.astype(f32), axis=0, keepdims=True)
+        for part in range(FF_PARTS):
+            run_all(copies[part], "wait")
+            slope_copies[part].wait()
             up = dot_nn(low, reduce_blocks[part].reshape(WIDTH, WIDTH))
-            pre = up * slope_ref[:, columns].astype(f32)
-            pre_low = pre.astype(bf16)
-            sums_ref[4 + part : 5 + part] += jnp.sum(
-                pre_low.astype(f32), axis=0, keepdims=True
+            pre = (up * slope_ref[part].astype(f32)).astype(bf16)
+            pre_low[part] = pre
+            sums_ref[4 + part : 5 + part] = jnp.sum(pre.astype(f32), axis=0, keepdims=True)
+            turned_pre[2 * part : 2 * part + 2] = pre.T.reshape(2, 384, tokens)
+            send(turned_pre.at[2 * part + core], pre_mine.at[part ^ chip])
+            send(turned_pre.at[2 * part + 1 - core], pre_theirs.at[part ^ chip])
+        run_all(expand_copies, "wait")
+        back = dot_nn(pre_low[0], expand_block[0:2].reshape(WIDTH, WIDTH))
+        for part in range(1, FF_PARTS):
+            back = back + dot_nn(
+                pre_low[part], expand_block[2 * part : 2 * part + 2].reshape(WIDTH, WIDTH)
             )
-            turned_pre[...] = pre_low.T.reshape(2, 384, ROWS)
-            pre_mine[part ^ chip] = turned_pre[core]
-            pre_theirs[part ^ chip] = turned_pre[1 - core]
-            back = back + dot_nn(
-                pre_low, expand_block[2 * part : 2 * part + 2].reshape(WIDTH, WIDTH)
-            )
+        middle_copy.wait()
         unit, root = normalise(middle_ref[...])
-        sums_ref[0:1] += jnp.sum(back * unit, axis=0, keepdims=True)
-        sums_ref[1:2] += jnp.sum(back, axis=0, keepdims=True)
+        sums_ref[0:1] = jnp.sum(back * unit, axis=0, keepdims=True)
+        sums_ref[1:2] = jnp.sum(back, axis=0, keepdims=True)
         scaled = back * small_ref[SM_G2 : SM_G2 + 1]
-        result = grad_rows + root * (
+        result = grad_ref[...].astype(f32) + root * (
             scaled
             - jnp.mean(scaled, axis=-1, keepdims=True)
             - unit * jnp.mean(scaled * unit, axis=-1, keepdims=True)
         )
         out_ref[...] = result
         result_low = result.astype(bf16)
-        sums_ref[3:4] += jnp.sum(result_low.astype(f32), axis=0, keepdims=True)
-        turned_attn[...] = result_low.T.reshape(8, 96, ROWS)
-        split_owners(place_now, turned_attn, attn_mine, attn_theirs, 96)
-
-    tokens = middle.shape[0]
+        sums_ref[3:4] = jnp.sum(result_low.astype(f32), axis=0, keepdims=True)
+        turned_attn[...] = result_low.T.reshape(8, 96, tokens)
+        for owner in range(4):
+            send(turned_attn.at[2 * owner + core], attn_mine.at[owner ^ chip])
+            send(turned_attn.at[2 * owner + 1 - core], attn_theirs.at[owner ^ chip])
+        run_all(sent, "wait")
+
     shape = jax.ShapeDtypeStruct
+    in_vmem = pl.BlockSpec(memory_space=pltpu.VMEM)
     return pl.pallas_call(
         kernel,
-        grid=(tokens // ROWS,),
-        in_specs=[
-            in_smem(),
-            rows_spec(WIDTH),
-            rows_spec(FF_PARTS * WIDTH),
-            rows_spec(WIDTH),
-            fixed(small.shape),
-        ]
-        + [in_any()] * PIECES,
-        out_specs=[
-            rows_spec(WIDTH),
-            halves_spec(384),
-            halves_spec(384),
-            halves_spec(96),
-            halves_spec(96),
-            fixed((8, WIDTH)),
-        ],
+        in_specs=[in_smem()] + [in_any()] * 3 + [in_vmem] + [in_any()] * (2 * PIECES),
+        out_specs=[in_vmem] + [in_any()] * 4 + [in_vmem],
         out_shape=[shape((tokens, WIDTH), f32)]
         + [shape((4, 384, tokens), bf16)] * 2
         + [shape((4, 96, tokens), bf16)] * 2
         + [shape((8, WIDTH), f32)],
         scratch_shapes=[
+            pltpu.VMEM((tokens, WIDTH), grad.dtype),
+            pltpu.VMEM((FF_PARTS, tokens, WIDTH), bf16),
+            pltpu.VMEM((tokens, WIDTH), f32),
             pltpu.VMEM((8, 384, WIDTH), bf16),
             pltpu.VMEM((FF_PARTS, 8, 96, WIDTH), bf16),
-            pltpu.VMEM((2, 384, ROWS), bf16),
-            pltpu.VMEM((8, 96, ROWS), bf16),
+            pltpu.VMEM((8, 384, tokens), bf16),
+            pltpu.VMEM((8, 96, tokens), bf16),
+            pltpu.VMEM((FF_PARTS, tokens, WIDTH), bf16),
             pltpu.SemaphoreType.DMA((PIECES,)),
-            pltpu.SemaphoreType.DMA((4, PIECES)),
+            pltpu.SemaphoreType.DMA((FF_PARTS, PIECES)),
+            pltpu.SemaphoreType.DMA((2 + FF_PARTS,)),
+            pltpu.SemaphoreType.DMA((16,)),
         ],
-        compiler_params=params(),
+        compiler_params=pltpu.CompilerParams(vmem_limit_bytes=VMEM_BYTES),
         cost_estimate=cost(0.01),
         name="ff_backward",
-    )(place, grad, slope, middle, small, *pack[0])
-
-
-def attn_backward(place, grad, hidden, qkv, small, ff_sums, pack, last):
-    def kernel(place_ref, grad_ref, hidden_ref, qkv_ref, small_ref, ff_sums_ref, *rest):
+    )(place, grad, slope, middle, small, *expand_arrays, *reduce_arrays)
+
+
+def attn_backward(place, grad, hidden, qkv, mixed, small, ff_sums, pack, last):
+    tokens = grad.shape[0]
+
+    def kernel(place_ref, grad_in, hidden_in, qkv_in, mixed_in, small_ref, ff_sums_ref, *rest):
         packs = rest[:PIECES]
-        if last:
-            out_ref, qkv_mine, qkv_theirs, vec_mine, vec_theirs = rest[PIECES : PIECES + 5]
-        else:
-            (
-                out_ref,
-                qkv_mine,
-                qkv_theirs,
-                vec_mine,
-                vec_theirs,
-                low_mine,
-                low_theirs,
-            ) = rest[PIECES : PIECES + 7]
-        blocks, turned, straight, sums_ref, sems = rest[-5:]
+        out_ref, qkv_mine, qkv_theirs, vec_mine, vec_theirs = rest[PIECES : PIECES + 5]
+        if not last:
+            low_mine, low_theirs = rest[PIECES + 5 : PIECES + 7]
+        (
+            grad_ref,
+            hidden_ref,
+            qkv_ref,
+            mixed_ref,
+            blocks,
+            turned,
+            sums_ref,
+            sems,
+            in_sems,
+            out_sems,
+        ) = rest[-10:]
         place_now = place_ref[0]
-        image = pl.program_id(0)
-        copies = heads_copies(place_now, packs, pack[1], blocks, sems)
-
-        @pl.when(image == 0)
-        def begin():
-            for member in (3, 0, 1, 2):
-                run_all(copies[member], "start")
-            sums_ref[...] = jnp.zeros_like(sums_ref)
-
+        core = place_now & 1
+        chip = place_now >> 1
+        copies = unit_copies(place_now, packs, pack[1], 0, blocks, sems)
+        fetches = [
+            fetch(source, target, in_sems.at[at])
+            for at, (source, target) in enumerate(
+                (
+                    (grad_in, grad_ref),
+                    (mixed_in, mixed_ref),
+                    (qkv_in, qkv_ref),
+                    (hidden_in, hidden_ref),
+                )
+            )
+        ]
+        fetches[0].start()
+        run_all(copies, "start")
+        run_all(fetches[1:], "start")
+        sent = []
+
+        def send(source, target):
+            copy = pltpu.make_async_copy(source, target, out_sems.at[len(sent)])
+            copy.start()
+            sent.append(copy)
+
+        fetches[0].wait()
+        run_all(copies, "wait")
         grad_rows = grad_ref[...]
-
-        @pl.when(image == 0)
-        def arrive():
-            for member in (3, 0, 1, 2):
-                run_all(copies[member], "wait")
-
         mixed_back = dot_nn(grad_rows.astype(bf16), blocks[3].reshape(WIDTH, WIDTH)).astype(bf16)
+        fetches[1].wait()
+        product = mixed_back.astype(f32) * mixed_ref[...].astype(f32)
+        product_high = product.astype(bf16)
+        product_low = (product - product_high.astype(f32)).astype(bf16)
+        head_row = lax.broadcasted_iota(jnp.int32, (16, WIDTH), 0)
+        head_column = lax.broadcasted_iota(jnp.int32, (16, WIDTH), 1) >> 6
+        of_head = jnp.where(head_row == head_column, 1.0, 0.0).astype(bf16)
+        inner = dot_nt(of_head, product_high) + dot_nt(of_head, product_low)
+        fetches[2].wait()
         lane = lax.broadcasted_iota(jnp.int32, (ROWS, 128), 1)
         line = lax.broadcasted_iota(jnp.int32, (128, ROWS), 0)
-        for pair in range(HEADS // 2):
-            q_pair = qkv_ref[:, 128 * pair : 128 * pair + 128]
-            k_pair = qkv_ref[:, WIDTH + 128 * pair : WIDTH + 128 * pair + 128]
-            v_pair = qkv_ref[:, 2 * WIDTH + 128 * pair : 2 * WIDTH + 128 * pair + 128]
-            g_pair = mixed_back[:, 128 * pair : 128 * pair + 128]
-            q_turned = q_pair.T
-            k_turned = k_pair.T
-            g_turned = g_pair.T
-            made = []
-            for half in range(2):
-                here = (lane < 64) == (half == 0)
-                k_one = jnp.where(here, k_pair, jnp.zeros_like(k_pair))
-                v_one = jnp.where(here, v_pair, jnp.zeros_like(v_pair))
-                scores = dot_nt(k_one, q_pair) * (HEAD_DIM**-0.5)
-                peak = jnp.max(scores, axis=0, keepdims=True)
-                powers = jnp.exp(scores - peak)
-                attend = powers / jnp.sum(powers, axis=0, keepdims=True)
-                back = dot_nt(v_one, g_pair)
-                inner = jnp.sum(back * attend, axis=0, keepdims=True)
-                scores_back = (attend * (back - inner)).astype(bf16)
-                made.append(
-                    (
-                        dot_nn(k_turned, scores_back) * (HEAD_DIM**-0.5),
-                        dot_nt(q_turned, scores_back) * (HEAD_DIM**-0.5),
-                        dot_nt(g_turned, attend.astype(bf16)),
+        scale = HEAD_DIM**-0.5
+        for image in range(tokens // ROWS):
+            rows = slice(ROWS * image, ROWS * (image + 1))
+            for pair in range(HEADS // 2):
+                q_pair = qkv_ref[rows, 128 * pair : 128 * pair + 128]
+                k_pair = qkv_ref[rows, WIDTH + 128 * pair : WIDTH + 128 * pair + 128]
+                v_pair = qkv_ref[rows, 2 * WIDTH + 128 * pair : 2 * WIDTH + 128 * pair + 128]
+                g_pair = mixed_back[rows, 128 * pair : 128 * pair + 128]
+                k_turned = k_pair.T
+                weights, powers, inverses = [], [], []
+                for half in range(2):
+                    here = (lane < 64) == (half == 0)
+                    k_one = jnp.where(here, k_pair * scale, jnp.zeros_like(k_pair))
+                    v_one = jnp.where(here, v_pair, jnp.zeros_like(v_pair))
+                    scores = dot_nt(k_one, q_pair)
+                    power = jnp.exp(scores - jnp.max(scores, axis=0, keepdims=True))
+                    inverses.append(1.0 / jnp.sum(power, axis=0, keepdims=True))
+                    head = 2 * pair + half
+                    back = dot_nt(v_one, g_pair) - inner[head : head + 1, rows]
+                    weights.append((power * back).astype(bf16))
+                    powers.append(power.astype(bf16))
+                inverse = jnp.where(line < 64, inverses[0], inverses[1])
+                q_turned = (q_pair.T.astype(f32) * (inverse * scale)).astype(bf16)
+                g_turned = (g_pair.T.astype(f32) * inverse).astype(bf16)
+                made = (
+                    jnp.where(
+                        line < 64, dot_nn(k_turned, weights[0]), dot_nn(k_turned, weights[1])
                     )
+                    * (inverse * scale),
+                    jnp.where(
+                        line < 64, dot_nt(q_turned, weights[0]), dot_nt(q_turned, weights[1])
+                    ),
+                    jnp.where(
+                        line < 64, dot_nt(g_turned, powers[0]), dot_nt(g_turned, powers[1])
+                    ),
                 )
-            for member in range(3):
-                both = jnp.where(line < 64, made[0][member], made[1][member]).astype(bf16)
-                turned[member, pl.ds(128 * pair, 128)] = both
-                straight[:, WIDTH * member + 128 * pair : WIDTH * member + 128 * pair + 128] = (
-                    both.T
-                )
-        core = place_now & 1
-        chip = place_now >> 1
-        back = jnp.zeros((ROWS, WIDTH), f32)
+                for member in range(3):
+                    turned[member, 128 * pair : 128 * pair + 128, rows] = made[member].astype(bf16)
         for member in range(3):
             for owner in range(4):
                 for odd in range(2):
-                    rows = turned[
-                        member,
-                        pl.ds(pl.multiple_of(192 * owner + 96 * (core ^ odd), 96), 96),
-                    ]
                     target = qkv_theirs if odd else qkv_mine
-                    target[member, owner ^ chip] = rows
-            straight_one = straight[:, WIDTH * member : WIDTH * (member + 1)]
-            back = back + dot_nn(straight_one, blocks[member].reshape(WIDTH, WIDTH))
-            if member != 1:
-                row = 0 if member == 0 else 1
-                sums_ref[row : row + 1] += jnp.sum(
-                    straight_one.astype(f32), axis=0, keepdims=True
-                )
+                    first = pl.multiple_of(192 * owner + 96 * (core ^ odd), 96)
+                    send(turned.at[member, pl.ds(first, 96)], target.at[member, owner ^ chip])
+        back = jnp.zeros((tokens, WIDTH), f32)
+        ones = jnp.ones((8, tokens), bf16)
+        for member in range(3):
+            back = back + lax.dot_general(
+                turned[member],
+                blocks[member].reshape(WIDTH, WIDTH),
+                (((0,), (0,)), ((), ())),
+                preferred_element_type=f32,
+            )
+        sums_ref[0:1] = dot_nt(ones, turned[0])[0:1]
+        sums_ref[1:2] = dot_nt(ones, turned[2])[0:1]
+        fetches[3].wait()
         unit, root = normalise(hidden_ref[...].astype(f32))
-        sums_ref[3:4] += jnp.sum(back * unit, axis=0, keepdims=True)
-        sums_ref[4:5] += jnp.sum(back, axis=0, keepdims=True)
-
-        @pl.when(image == pl.num_programs(0) - 1)
-        def vectors():
-            sums_ref[2:3] = ff_sums_ref[3:4]
-            sums_ref[5:8] = ff_sums_ref[0:3]
-            row = lax.broadcasted_iota(jnp.int32, (WIDTH, 1024), 0)
-            column = lax.broadcasted_iota(jnp.int32, (WIDTH, 1024), 1)
-            at = column & 127
-            wanted = 96 * ((column >> 7) ^ place_now) + at
-            chosen = jnp.where((row == wanted) & (at < 96), 1.0, 0.0)
-            cut = jnp.dot(
-                sums_ref[...],
-                chosen,
-                preferred_element_type=f32,
-                precision=lax.Precision.HIGHEST,
-            )
-            for delta in range(8):
-                owner = place_now ^ delta
-                target = vec_theirs if delta & 1 else vec_mine
-                target[delta >> 1] = jnp.zeros((16, WIDTH // 2), f32)
-                target[delta >> 1, 0:8, 0:128] = cut[:, 128 * delta : 128 * delta + 128]
-                line = ff_sums_ref[pl.ds(4 + (owner >> 1), 1)]
-                target[delta >> 1, 8:9] = jnp.where(
-                    (owner & 1) == 0, line[:, : WIDTH // 2], line[:, WIDTH // 2 :]
-                )
-
+        sums_ref[3:4] = jnp.sum(back * unit, axis=0, keepdims=True)
+        sums_ref[4:5] = jnp.sum(back, axis=0, keepdims=True)
         scaled = back * small_ref[SM_G1 : SM_G1 + 1]
-        result = grad_rows + root * (
+        result = grad_ref[...] + root * (
             scaled
             - jnp.mean(scaled, axis=-1, keepdims=True)
             - unit * jnp.mean(scaled * unit, axis=-1, keepdims=True)
         )
         out_ref[...] = result.astype(out_ref.dtype)
+        run_all(sent, "wait")
+        sent.clear()
         if not last:
             turned[0] = result.astype(bf16).T
             for owner in range(4):
                 for odd in range(2):
-                    rows = turned[
-                        0, pl.ds(pl.multiple_of(192 * owner + 96 * (core ^ odd), 96), 96)
-                    ]
                     target = low_theirs if odd else low_mine
-                    target[owner ^ chip] = rows
-
-    tokens = grad.shape[0]
+                    first = pl.multiple_of(192 * owner + 96 * (core ^ odd), 96)
+                    send(turned.at[0, pl.ds(first, 96)], target.at[owner ^ chip])
+
+        sums_ref[2:3] = ff_sums_ref[3:4]
+        sums_ref[5:8] = ff_sums_ref[0:3]
+        row = lax.broadcasted_iota(jnp.int32, (WIDTH, 1024), 0)
+        column = lax.broadcasted_iota(jnp.int32, (WIDTH, 1024), 1)
+        at = column & 127
+        wanted = 96 * ((column >> 7) ^ place_now) + at
+        chosen = jnp.where((row == wanted) & (at < 96), 1.0, 0.0).astype(bf16)
+        rest_of = sums_ref[...]
+        cut = jnp.zeros((8, 1024), f32)
+        for term in range(3):
+            term_low = rest_of.astype(bf16)
+            rest_of = rest_of - term_low.astype(f32)
+            cut = cut + dot_nn(term_low, chosen)
+        for delta in range(8):
+            owner = place_now ^ delta
+            target = vec_theirs if delta & 1 else vec_mine
+            target[delta >> 1] = jnp.zeros((16, WIDTH // 2), f32)
+            target[delta >> 1, 0:8, 0:128] = cut[:, 128 * delta : 128 * delta + 128]
+            values = ff_sums_ref[pl.ds(4 + (owner >> 1), 1)]
+            target[delta >> 1, 8:9] = jnp.where(
+                (owner & 1) == 0, values[:, : WIDTH // 2], values[:, WIDTH // 2 :]
+            )
+        run_all(sent, "wait")
+
     shape = jax.ShapeDtypeStruct
-    heads_spec = pl.BlockSpec((3, 4, 96, ROWS), lambda image: (0, 0, 0, image))
+    in_vmem = pl.BlockSpec(memory_space=pltpu.VMEM)
     vector_shape = (4, 16, WIDTH // 2)
-    out_specs = [rows_spec(WIDTH), heads_spec, heads_spec, fixed(vector_shape), fixed(vector_shape)]
+    out_specs = [in_vmem] + [in_any()] * 2 + [in_vmem] * 2
     out_shape = (
         [shape((tokens, WIDTH), bf16 if last else f32)]
         + [shape((3, 4, 96, tokens), bf16)] * 2
         + [shape(vector_shape, f32)] * 2
     )
     if not last:
-        out_specs += [halves_spec(96)] * 2
+        out_specs += [in_any()] * 2
         out_shape += [shape((4, 96, tokens), bf16)] * 2
     return pl.pallas_call(
         kernel,
-        grid=(tokens // ROWS,),
-        in_specs=[
-            in_smem(),
-            rows_spec(WIDTH),
-            rows_spec(WIDTH),
-            rows_spec(3 * WIDTH),
-            fixed(small.shape),
-            fixed(ff_sums.shape),
-        ]
-        + [in_any()] * PIECES,
+        in_specs=[in_smem()] + [in_any()] * 4 + [in_vmem] * 2 + [in_any()] * PIECES,
         out_specs=out_specs,
         out_shape=out_shape,
         scratch_shapes=[
+            pltpu.VMEM((tokens, WIDTH), grad.dtype),
+            pltpu.VMEM((tokens, WIDTH), hidden.dtype),
+            pltpu.VMEM((tokens, 3 * WIDTH), bf16),
+            pltpu.VMEM((tokens, WIDTH), bf16),
             pltpu.VMEM((4, 8, 96, WIDTH), bf16),
-            pltpu.VMEM((3, WIDTH, ROWS), bf16),
-            pltpu.VMEM((ROWS, 3 * WIDTH), bf16),
+            pltpu.VMEM((3, WIDTH, tokens), bf16),
             pltpu.VMEM((8, WIDTH), f32),
-            pltpu.SemaphoreType.DMA((4, PIECES)),
+            pltpu.SemaphoreType.DMA((PIECES,)),
+            pltpu.SemaphoreType.DMA((4,)),
+            pltpu.SemaphoreType.DMA((24,)),
         ],
-        compiler_params=params(),
+        compiler_params=pltpu.CompilerParams(vmem_limit_bytes=VMEM_BYTES),
         cost_estimate=cost(0.01),
         name="attn_backward",
-    )(place, grad, hidden, qkv, small, ff_sums, *pack[0])
+    )(place, grad, hidden, qkv, mixed, small, ff_sums, *pack[0])
 
 
 def spread(result, owner, rows, out_refs):
@@ -1312,6 +1357,152 @@
     )(*given)
 
 
+def taken(end_ref, pair, rows, scale):
+    total, outward = pair
+    part = jnp.where(end_ref[0] == 1, outward[rows], total[rows])
+    return part.astype(f32) * scale
+
+
+def put_halves(target, end_ref, pair, low, high, rows, scale):
+    half = WIDTH // 2
+    target[:, :half] = taken(end_ref, pair, slice(low, low + rows), scale)
+    target[:, half:] = taken(end_ref, pair, slice(high, high + rows), scale)
+
+
+def in_full():
+    return pl.BlockSpec(memory_space=pltpu.VMEM)
+
+
+def finish_most(at_end, reduce_1, em_1, both_01, scale):
+    layers = 2
+    half = WIDTH // 2
+
+    def kernel(end_ref, *refs):
+        r_pair, em_pair, hr_pair = refs[0:2], refs[2:4], refs[4:6]
+        heads_out, merge_out, expand_out, reduce_out, vectors_out = refs[6:11]
+        heads, merge, expand, reduce, sems = refs[11:]
+        for layer, pair, high in ((0, hr_pair, 688), (1, r_pair, 384)):
+            for part in range(FF_PARTS):
+                for first, column in ((96 * part, WIDTH * part), (high + 96 * part, WIDTH * part + half)):
+                    reduce[layer, :, column : column + half] = taken(
+                        end_ref, pair, slice(first, first + 96), scale
+                    )
+        copies = [pltpu.make_async_copy(reduce, reduce_out, sems.at[0])]
+        copies[0].start()
+        put_halves(expand, end_ref, em_pair, 0, 480, 384, scale)
+        put_halves(merge, end_ref, em_pair, 384, 864, 96, scale)
+        for member in range(3):
+            put_halves(
+                heads.at[member],
+                end_ref,
+                hr_pair,
+                384 + 96 * member,
+                688 + 384 + 96 * member,
+                96,
+                scale,
+            )
+        last = layers - 1
+        copies.append(pltpu.make_async_copy(expand, expand_out.at[last], sems.at[1]))
+        copies.append(pltpu.make_async_copy(merge, merge_out.at[last], sems.at[2]))
+        copies.append(pltpu.make_async_copy(heads, heads_out.at[last], sems.at[3]))
+        run_all(copies[1:], "start")
+        vectors_out[...] = taken(end_ref, hr_pair, slice(672, 688), scale)
+        run_all(copies, "wait")
+
+    shape = jax.ShapeDtypeStruct
+    return pl.pallas_call(
+        kernel,
+        in_specs=[in_smem()] + [in_full()] * 6,
+        out_specs=[in_any()] * 4 + [in_full()],
+        out_shape=[
+            shape((layers, 3, 96, WIDTH), f32),
+            shape((layers, 96, WIDTH), f32),
+            shape((layers, 384, WIDTH), f32),
+            shape((layers, 96, FF_PARTS * WIDTH), f32),
+            shape((16, half), f32),
+        ],
+        scratch_shapes=[
+            pltpu.VMEM((3, 96, WIDTH), f32),
+            pltpu.VMEM((96, WIDTH), f32),
+            pltpu.VMEM((384, WIDTH), f32),
+            pltpu.VMEM((layers, 96, FF_PARTS * WIDTH), f32),
+            pltpu.SemaphoreType.DMA((4,)),
+        ],
+        compiler_params=pltpu.CompilerParams(vmem_limit_bytes=SMALL_VMEM_BYTES),
+        cost_estimate=cost(0.01),
+        name="finish_most",
+    )(at_end, *reduce_1, *em_1, *both_01)
+
+
+def finish_expand(at_end, em_0, merge_grad, expand_grad, scale):
+    def kernel(end_ref, total, outward, merge_in, expand_in, merge_out, expand_out, *rest):
+        merge, expand, sems = rest
+        put_halves(expand, end_ref, (total, outward), 0, 480, 384, scale)
+        put_halves(merge, end_ref, (total, outward), 384, 864, 96, scale)
+        copies = [
+            pltpu.make_async_copy(expand, expand_out.at[0], sems.at[0]),
+            pltpu.make_async_copy(merge, merge_out.at[0], sems.at[1]),
+        ]
+        run_all(copies, "start")
+        run_all(copies, "wait")
+
+    return pl.pallas_call(
+        kernel,
+        in_specs=[in_smem()] + [in_full()] * 2 + [in_any()] * 2,
+        out_specs=[in_any()] * 2,
+        out_shape=[jax.ShapeDtypeStruct(a.shape, f32) for a in (merge_grad, expand_grad)],
+        scratch_shapes=[
+            pltpu.VMEM((96, WIDTH), f32),
+            pltpu.VMEM((384, WIDTH), f32),
+            pltpu.SemaphoreType.DMA((2,)),
+        ],
+        input_output_aliases={3: 0, 4: 1},
+        compiler_params=pltpu.CompilerParams(vmem_limit_bytes=SMALL_VMEM_BYTES),
+        cost_estimate=cost(0.01),
+        name="finish_expand",
+    )(at_end, *em_0, merge_grad, expand_grad)
+
+
+def finish_heads(at_end, heads_0, vectors_1, heads_grad, scale):
+    def kernel(end_ref, total, outward, vectors_ref, heads_in, heads_out, *rest):
+        outs, (heads, sems) = rest[:8], rest[8:]
+        for member in range(3):
+            put_halves(
+                heads.at[member],
+                end_ref,
+                (total, outward),
+                96 * member,
+                304 + 96 * member,
+                96,
+                scale,
+            )
+        copy = pltpu.make_async_copy(heads, heads_out.at[0], sems.at[0])
+        copy.start()
+        own = taken(end_ref, (total, outward), slice(288, 304), scale)
+        for layer, values in ((0, own), (1, vectors_ref[...])):
+            outs[0][layer] = values[0:2, :96]
+            for row in range(2, 8):
+                outs[row - 1][layer : layer + 1] = values[row : row + 1, :96]
+            outs[7][layer : layer + 1] = values[8:9]
+        copy.wait()
+
+    shape = jax.ShapeDtypeStruct
+    layers = heads_grad.shape[0]
+    return pl.pallas_call(
+        kernel,
+        in_specs=[in_smem()] + [in_full()] * 3 + [in_any()],
+        out_specs=[in_any()] + [in_full()] * 8,
+        out_shape=[shape(heads_grad.shape, f32), shape((layers, 2, 96), f32)]
+        + [shape((layers, 96), f32)] * 6
+        + [shape((layers, 384), f32)],
+        scratch_shapes=[pltpu.VMEM((3, 96, WIDTH), f32), pltpu.SemaphoreType.DMA((1,))],
+        input_output_aliases={4: 0},
+        compiler_params=pltpu.CompilerParams(vmem_limit_bytes=SMALL_VMEM_BYTES),
+        cost_estimate=cost(0.01),
+        name="finish_heads",
+    )(at_end, *heads_0, vectors_1, heads_grad)
+
+
 def shards(
     images,
     cotangent,
@@ -1346,9 +1537,9 @@
         reduce_bias,
         expand_bias,
     )
-    kinds = [(kind, layer) for layer in range(layers) for kind in ("attn", "ff")]
-    rows_of = [400 if kind == "attn" else 768 for kind, layer in kinds]
-    cut_of = [192 if kind == "attn" else 384 for kind, layer in kinds]
+    kinds = [("attn", 0), ("ff", 0), ("attn", 1), ("expand", 1), ("reduce", 1)]
+    rows_of = [PACK_ROWS[kind] for kind, layer in kinds]
+    cut_of = [PACK_CUTS[kind] for kind, layer in kinds]
     x_rows = [0] + cut_of
     y_rows = [0] + [rows - cut for rows, cut in zip(rows_of, cut_of)]
     count = len(kinds)
@@ -1381,16 +1572,18 @@
     came = []
     own = own_packs(kinds[:1], matrices, vectors)
     new = send_round(0, own[0], None, None)
-    own += own_packs(kinds[1:], matrices, vectors)
     own_other = both(own)
+    own += own_packs(kinds[1:2], matrices, vectors)
     grad, low_mine, low_theirs = start_grad(place, slot_flags, cotangent.reshape(tokens, width))
-    own, own_other, new, grad, low_mine, low_theirs = seal(
-        (own, own_other, new, grad, low_mine, low_theirs)
+    own, own_other, new, grad, low_mine, low_theirs, matrices, vectors = seal(
+        (own, own_other, new, grad, low_mine, low_theirs, matrices, vectors)
     )
 
     got, new = new, send_round(1, own[1], *new)
     came.append(got + both(got))
     low = (low_mine, swap_core(low_theirs))
+    own += own_packs(kinds[2:], matrices, vectors)
+    own_other += both(own[1:])
     own, own_other, came, new, low, grad = seal((own, own_other, came, new, low, grad))
 
     got, new = new, send_round(2, own[2], *new)
@@ -1416,7 +1609,7 @@
         (own, came, new, second_0, active_0, slope_0, hidden_1, others_a0)
     )
 
-    got, new = new, send_round(4, None, *new)
+    got, new = new, send_round(4, own[4], *new)
     came.append(got + both(got))
     pack_a1 = pack_of(2, (own[2], own_other[2]), came)
     small_1, expand_rows_1 = gathered_vectors(place, pack_a1)
@@ -1426,25 +1619,29 @@
         (came, new, small_1, expand_rows_1, middle_1, normed_1, qkv_1, mixed_1, second_other_0)
     )
 
+    got, new = new, send_round(5, None, *new)
+    came.append(got + both(got))
+    pack_e1 = pack_of(3, (own[3], own_other[3]), came)
+    second_1, active_1, slope_1 = expand_forward(
+        place, middle_1, small_1, expand_rows_1, pack_e1, 0
+    )
+    others_a1 = both((normed_1, mixed_1))
+    second_1, active_1, slope_1, others_a1, came, new = seal(
+        (second_1, active_1, slope_1, others_a1, came, new)
+    )
     came.append(new + both(new))
-    pack_f1 = pack_of(3, (own[3], own_other[3]), came)
-    second_1, active_1, slope_1 = expand_forward(
-        place, middle_1, small_1, expand_rows_1, pack_f1, 0
-    )
-    others_a1 = both((normed_1, mixed_1))
-    active_other_0 = swap_core(active_0)
-    second_1, active_1, slope_1, others_a1, active_other_0, came = seal(
-        (second_1, active_1, slope_1, others_a1, active_other_0, came)
-    )
-    pack_f1 = pack_of(3, (own[3], own_other[3]), came)
+    second_1, active_1, came = seal((second_1, active_1, came))
+    pack_e1 = pack_of(3, (own[3], own_other[3]), came)
+    pack_r1 = pack_of(4, (own[4], own_other[4]), came)
 
     grad, pre_mine, pre_theirs, attn_mine, attn_theirs, ff_sums = ff_backward(
-        place, grad, slope_1, middle_1, small_1, pack_f1
+        place, grad, slope_1, middle_1, small_1, (pack_e1, 0), (pack_r1, 0)
     )
     others_f1 = both((second_1, active_1))
-    grad, pre_mine, pre_theirs, attn_mine, attn_theirs, ff_sums, others_f1 = seal(
-        (grad, pre_mine, pre_theirs, attn_mine, attn_theirs, ff_sums, others_f1)
-    )
+    made = (grad, pre_mine, pre_theirs, attn_mine, attn_theirs, ff_sums)
+    made, others_f1, pack_r1_arrays = seal((made, others_f1, pack_r1[0]))
+    grad, pre_mine, pre_theirs, attn_mine, attn_theirs, ff_sums = made
+    pack_r1 = (pack_r1_arrays, pack_r1[1])
 
     travel_r1 = owner_terms(reduce=(low, (active_1, others_f1[1])))
     pre_other, attn_other = both((pre_theirs, attn_theirs))
@@ -1455,15 +1652,16 @@
         expand=((pre_mine, pre_other), (second_1, others_f1[0])),
         merge=((attn_mine, attn_other), (mixed_1, others_a1[1])),
     )
-    state_r1, travel_em1, grad = seal((state_r1, travel_em1, grad))
+    state_r1, travel_em1, grad, active_0 = seal((state_r1, travel_em1, grad, active_0))
 
     state_r1 = second_steps(state_r1)
     state_em1 = first_steps(travel_em1)
     grad, qkv_mine, qkv_theirs, vec_mine, vec_theirs, low_mine, low_theirs = attn_backward(
-        place, grad, hidden_1, qkv_1, small_1, ff_sums, pack_a1, False
-    )
+        place, grad, hidden_1, qkv_1, mixed_1, small_1, ff_sums, pack_a1, False
+    )
+    active_other_0 = swap_core(active_0)
     made = (grad, qkv_mine, qkv_theirs, vec_mine, vec_theirs, low_mine, low_theirs)
-    state_r1, state_em1, made = seal((state_r1, state_em1, made))
+    state_r1, state_em1, made, active_other_0 = seal((state_r1, state_em1, made, active_other_0))
     grad, qkv_mine, qkv_theirs, vec_mine, vec_theirs, low_mine, low_theirs = made
 
     sum_r1 = to_middle(ends(state_r1))
@@ -1480,7 +1678,7 @@
     sum_em1 = to_middle(ends(state_em1))
     sum_r1 = across_middle(sum_r1)
     grad, pre_mine, pre_theirs, attn_mine, attn_theirs, ff_sums = ff_backward(
-        place, grad, slope_0, middle_0, small_0, pack_f0
+        place, grad, slope_0, middle_0, small_0, (pack_f0, 0), (pack_f0, 384)
     )
     made = (grad, pre_mine, pre_theirs, attn_mine, attn_theirs, ff_sums)
     state_hr, sum_em1, sum_r1, made = seal((state_hr, sum_em1, sum_r1, made))
@@ -1499,7 +1697,7 @@
     sum_hr = to_middle(ends(state_hr))
     final_r1, final_em1 = to_ends(sum_r1), to_ends(sum_em1)
     images_grad, qkv_mine, qkv_theirs, vec_mine, vec_theirs = attn_backward(
-        place, grad, hidden, qkv_0, small_0, ff_sums, pack_a0, True
+        place, grad, hidden, qkv_0, mixed_0, small_0, ff_sums, pack_a0, True
     )
     made = (images_grad, qkv_mine, qkv_theirs, vec_mine, vec_theirs)
     state_em0, sum_hr, final_r1, final_em1, made = seal(
@@ -1513,80 +1711,48 @@
     travel_h0 = owner_terms(
         heads=((qkv_mine, qkv_other), (normed_0, others_a0[0])), small_terms=(vec_mine, vec_other)
     )
-    state_em0, sum_hr, travel_h0 = seal((state_em0, sum_hr, travel_h0))
+    state_em0, travel_h0, middle_1, active_1 = seal((state_em0, travel_h0, middle_1, active_1))
 
     state_h0 = first_steps(travel_h0)
     sum_em0 = to_middle(ends(state_em0))
+    outputs = reduce_forward(
+        place, slot_flags, middle_1, active_1, small_1, pack_r1, 0, True
+    ).reshape(images.shape)
+    state_h0, outputs, sum_hr = seal((state_h0, outputs, sum_hr))
+
+    state_h0 = second_steps(state_h0)
     final_hr = to_ends(sum_hr)
-    middle_last, active_last, travel_h0 = seal((middle_1, active_1, travel_h0))
-    outputs = reduce_forward(
-        place, slot_flags, middle_last, active_last, small_1, pack_f1, 384, True
-    ).reshape(images.shape)
-    state_h0, outputs = seal((state_h0, outputs))
-
-    state_h0 = second_steps(state_h0)
+    state_h0, sum_em0 = seal((state_h0, sum_em0))
+    sum_h0 = to_middle(ends(state_h0))
     sum_em0 = across_middle(sum_em0)
-    state_h0 = seal(state_h0)
-    sum_h0 = to_middle(ends(state_h0))
-    sum_h0, sum_em0 = seal((sum_h0, sum_em0))
+    sum_h0, final_hr, sum_em0 = seal((sum_h0, final_hr, sum_em0))
     sum_h0 = across_middle(sum_h0)
     final_em0 = to_ends(sum_em0)
     final_h0 = to_ends(sum_h0)
-    rep_at = lax.axis_index("rep")
-    at_end = (rep_at == 0) | (rep_at == lax.axis_size("rep") - 1)
-    final_r1, final_em1, final_hr, final_em0, final_h0 = (
-        jnp.where(at_end, outward, total)
-        for total, outward in (final_r1, final_em1, final_hr, final_em0, final_h0)
-    )
+
     images_grad = images_grad.reshape(images.shape)
-
     grad_scale = (
         micro_count * images.shape[1] * lax.axis_size("fsdp") * lax.axis_size("rep") * seq_len
     ) ** (-0.5)
-
-    def halves(low_half, high_half):
-        return jnp.concatenate([low_half, high_half], axis=1).astype(f32) * grad_scale
-
-    def as_reduce(rows):
-        return rows.reshape(4, 96, width).transpose(1, 0, 2).reshape(96, 4 * width)
-
-    def layer_grads(reduce_sum, em_sum, heads_sum, vectors):
-        vectors = vectors.astype(f32) * grad_scale
-        short = vectors[:, :96]
-        return (
-            heads_sum.reshape(3, 96, width),
-            short[SM_HB0 : SM_HB1 + 1],
-            em_sum[384:480],
-            short[SM_MB],
-            short[SM_G1],
-            short[SM_S1],
-            short[SM_G2],
-            short[SM_S2],
-            em_sum[:384],
-            vectors[8],
-            as_reduce(reduce_sum),
-            short[SM_RB],
-        )
-
-    hr_low, hr_high = final_hr[:688], final_hr[688:]
-    hr_sum = halves(hr_low[:672], hr_high)
-    h0_low, h0_high = final_h0[:304], final_h0[304:]
-    finals = [
-        layer_grads(
-            hr_sum[:384],
-            halves(final_em0[:480], final_em0[480:]),
-            halves(h0_low[:288], h0_high),
-            h0_low[288:],
-        ),
-        layer_grads(
-            halves(final_r1[:384], final_r1[384:]),
-            halves(final_em1[:480], final_em1[480:]),
-            hr_sum[384:],
-            hr_low[672:],
-        ),
-    ]
-    stacked = tuple(jnp.stack(member) for member in zip(*finals))
-    return (outputs, images_grad) + stacked
+    rep_at = lax.axis_index("rep")
+    at_end = ((rep_at == 0) | (rep_at == lax.axis_size("rep") - 1)).astype(jnp.int32)[None]
+    heads_grad, merge_grad, expand_grad, reduce_grad, vectors_1 = finish_most(
+        at_end, final_r1, final_em1, final_hr, grad_scale
+    )
+    merge_grad, expand_grad = finish_expand(at_end, final_em0, merge_grad, expand_grad, grad_scale)
+    heads_grad, *vector_grads = finish_heads(at_end, final_h0, vectors_1, heads_grad, grad_scale)
+    return (
+        outputs,
+        images_grad,
+        heads_grad,
+        vector_grads[0],
+        merge_grad,
+        *vector_grads[1:6],
+        expand_grad,
+        vector_grads[7],
+        reduce_grad,
+        vector_grads[6],
+    )
 
 
 def solution(mesh):

time: 468 us -> 441 us (0.942)
  other arithmetic: 16.5 us -> 0 us
  local copies, waits for them, and re-layouts: 36.1 us -> 21.6 us
  Pallas kernels: 205 us -> 217 us
  waiting for transfers between devices: 126 us -> 116 us
    another operation x9 -> x0, other arithmetic: 9.88 us -> none  [shards(): stacked = tuple((jnp.stack(member) for member in zip(*finals)))]
    ppermute x32 -> x35, waiting for transfers between devices: 19.9 us -> 11.7 us  [swap_core(): return lax.ppermute(value, 'fsdp', [(at, at ^ 1) for at in range(8)])]
    pallas_call x5, Pallas kernels: 40.1 us -> 48.1 us  [owner_terms(): pl.pallas_call(kernel, grid=(4,), in_specs=in_specs, out_specs=[pl.BlockS...]
    ppermute x5, starting transfers between devices: 29.1 us -> 22.4 us  [to_middle(): return (part, lax.ppermute(part, 'rep', [(0, 1), (3, 2)]))]
    unnamed x161 -> x143, local copies, waits for them, and re-layouts: 27.6 us -> 21.6 us
    ppermute x5, waiting for transfers between devices: 24.4 us -> 29.7 us  [to_ends(): return (total, lax.ppermute(total, 'rep', [(1, 0), (2, 3)]))]
    pallas_call x14 -> x19, Pallas kernels: 127 us -> 131 us  [the longest x2 36.4 us: attn_backward(): pl.pallas_call(kernel, in_specs=[in_smem()] + [in_any()] * 4 + [in_vmem]...]
    ppermute x15 -> x16, waiting for transfers between devices: 57.3 us -> 53.4 us  [swap_x(): return lax.ppermute(value, 'fsdp', [(at, at ^ 2) for at in range(8)])]
  transfers between devices with their start and end apart: 77 -> 82, of which waited for: 24 -> 28; matrix products, arithmetic and copies ran while one was open for 5% -> 0% of each run, Pallas kernels for 43% -> 48%
where the time goes in v3:
time: 441 us; the launch traced here: 433 us
  Pallas kernels  217 us (49%)
  waiting for transfers between devices  116 us (26%)
  starting transfers between devices  76.4 us (17%)
  local copies, waits for them, and re-layouts  21.6 us (5%)
    ppermute x16, waiting for transfers between devices, swap_x(): return lax.ppermute(value, 'fsdp', [(at, at ^ 2) for at in range(8)])  53.4 us
    pallas_call x5, Pallas kernels, owner_terms(): pl.pallas_call(kernel, grid=(4,), in_specs=in_specs, out_specs=[pl.BlockS...  48.1 us
    pallas_call x2, Pallas kernels, attn_backward(): pl.pallas_call(kernel, in_specs=[in_smem()] + [in_any()] * 4 + [in_vmem]...  36.4 us
    pallas_call x2, Pallas kernels, ff_backward(): pl.pallas_call(kernel, in_specs=[in_smem()] + [in_any()] * 3 + [in_vmem]...  32.3 us
    ppermute x5, waiting for transfers between devices, to_ends(): return (total, lax.ppermute(total, 'rep', [(1, 0), (2, 3)]))  29.7 us
    pallas_call x2, Pallas kernels, attn_forward(): pl.pallas_call(kernel, grid=(tokens // ROWS,), in_specs=[in_smem(), rows_...  22.9 us
    ppermute x5, starting transfers between devices, to_middle(): return (part, lax.ppermute(part, 'rep', [(0, 1), (3, 2)]))  22.4 us
    pallas_call x2, Pallas kernels, expand_forward(): pl.pallas_call(kernel, grid=(FF_PARTS,), in_specs=[in_smem(), fixed(middl...  22.1 us
  transfers between devices with their start and end apart: 82, of which 28 were waited for; matrix products, arithmetic and copies ran while one was open for 0% of the time, Pallas kernels for 48%

profile of v3, /device:TPU:0, one launch (start us, length us, event | category | flops | bytes accessed | tf_op | source)
XLA Modules:
  0.0 432.6 jit_solution(13176915155764224053)
XLA Ops:
  2.9 3.0 collective-permute-start.2
  8.0 2.8 own_packs.4.refs_1_.refs_3_.rest_0_.rest_10_
  13.1 6.8 %collective-permute-done.2.refs_0_.refs_4_.rest_2_ = bf16[400,768]{1,0:T(8,128)(2,1)S(1)} collective-permute-done((bf16[400,768]{1,0:T(8,128)(2,1)}, bf16[400,768]{1,0:T(8,128)(2,1)S(1)}, u32[]{:S(2)}, u32[]{:S(2)}) %collective-permute-start.2) | collective-permute-done | bytes 614432 | tf_op jit(solution)/shard_map/ppermute | solution.py:388
  21.4 3.8 own_packs.5
  35.5 25.7 %collective-permute-done.9.refs_2_.rest_3_.rest_1_.rest_11_ = bf16[960,768]{1,0:T(8,128)(2,1)} collective-permute-done((bf16[960,768]{1,0:T(8,128)(2,1)S(1)}, bf16[960,768]{1,0:T(8,128)(2,1)}, u32[]{:S(2)}, u32[]{:S(2)}) %collective-permute-start.9) | collective-permute-done | bytes 1474592 | tf_op jit(solution)/shard_map/ppermute | solution.py:384
  61.8 2.8 join_rows.6
  69.5 11.4 %attn_forward.2 = (f32[512,768]{1,0:T(8,128)}, bf16[512,768]{1,0:T(8,128)(2,1)}, bf16[512,2304]{1,0:T(8,128)(2,1)}, bf16[512,768]{1,0:T(8,128)(2,1)}) custom-call(s32[1]{0:T(128)} %bitcast.place_ref, bf16[512,768]{1,0:T(8,128)(2,1)} %bitcast.9, f32[8,768]{1,0:T(8,128)} %get-tuple-element.434.small_ref, bf16[400,768]{1,0:T(8,128)(2,1)} %own_packs.3.refs_0_.rest_0_, ...), custom_call_target="tpu_custom_call" | custom-call | flops 11000000 | bytes 1024 | tf_op jit(solution)/shard_map/attn_forward/pallas_call | solution.py:747
  80.9 12.5 %collective-permute-done.14.refs_2_.rest_3_.rest_1_.rest_13_ = bf16[784,768]{1,0:T(8,128)(2,1)S(1)} collective-permute-done((bf16[784,768]{1,0:T(8,128)(2,1)}, bf16[784,768]{1,0:T(8,128)(2,1)S(1)}, u32[]{:S(2)}, u32[]{:S(2)}) %collective-permute-start.14) | collective-permute-done | bytes 1204256 | tf_op jit(solution)/shard_map/ppermute | solution.py:384
  100.4 11.1 %expand_forward.2 = (bf16[512,768]{1,0:T(8,128)(2,1)}, bf16[512,3072]{1,0:T(8,128)(2,1)}, bf16[512,3072]{1,0:T(8,128)(2,1)}) custom-call(s32[1]{0:T(128)} %bitcast.place_ref, f32[512,768]{1,0:T(8,128)} %get-tuple-element.433.middle_ref.middle_in, f32[8,768]{1,0:T(8,128)} %get-tuple-element.434.small_ref, f32[4,1,768]{2,1,0:T(1,128)} %get-tuple-element.435.bias_ref, ...), custom_call_target="tpu_custom_call" | custom-call | flops 11000000 | bytes 1024 | tf_op jit(solution)/shard_map/expand_forward/pallas_call | solution.py:797
  111.4 8.3 %reduce_forward.2.hidden_ref.hidden_in = f32[512,768]{1,0:T(8,128)} custom-call(s32[1]{0:T(128)} %bitcast.place_ref, s32[2,1]{1,0:T(2,128)} %copy.32.live_ref, f32[512,768]{1,0:T(8,128)} %get-tuple-element.433.middle_ref.middle_in, bf16[512,3072]{1,0:T(8,128)(2,1)} %get-tuple-element.560.active_ref.refs_2_, f32[8,768]{1,0:T(8,128)} %get-tuple-element.434.small_ref, ...), custom_call_target="tpu_custom_call" | custom-call | flops 11000000 | bytes 1024 | tf_op jit(solution)/shard_map/reduce_forward/pallas_call | solution.py:869
  127.1 11.5 %attn_forward.3 = (f32[512,768]{1,0:T(8,128)}, bf16[512,768]{1,0:T(8,128)(2,1)}, bf16[512,2304]{1,0:T(8,128)(2,1)}, bf16[512,768]{1,0:T(8,128)(2,1)}) custom-call(s32[1]{0:T(128)} %bitcast.place_ref, f32[512,768]{1,0:T(8,128)} %reduce_forward.2.hidden_ref.hidden_in, f32[8,768]{1,0:T(8,128)} %get-tuple-element.462.small_ref, ...), custom_call_target="tpu_custom_call" | custom-call | flops 11000000 | bytes 1024 | tf_op jit(solution)/shard_map/attn_forward/pallas_call | solution.py:747
  138.6 6.5 %collective-permute-done.24.rest_3_.refs_1_.rest_11_.rest_1_ = bf16[576,768]{1,0:T(8,128)(2,1)S(1)} collective-permute-done((bf16[576,768]{1,0:T(8,128)(2,1)}, bf16[576,768]{1,0:T(8,128)(2,1)S(1)}, u32[]{:S(2)}, u32[]{:S(2)}) %collective-permute-start.24) | collective-permute-done | bytes 884768 | tf_op jit(solution)/shard_map/ppermute | solution.py:384
  152.6 11.0 %expand_forward.3 = (bf16[512,768]{1,0:T(8,128)(2,1)}, bf16[512,3072]{1,0:T(8,128)(2,1)}, bf16[512,3072]{1,0:T(8,128)(2,1)}) custom-call(s32[1]{0:T(128)} %bitcast.place_ref, f32[512,768]{1,0:T(8,128)} %get-tuple-element.666.middle_ref.middle_in, f32[8,768]{1,0:T(8,128)} %get-tuple-element.462.small_ref, f32[4,1,768]{2,1,0:T(1,128)} %get-tuple-element.463.bias_ref, ...), custom_call_target="tpu_custom_call" | custom-call | flops 11000000 | bytes 1024 | tf_op jit(solution)/shard_map/expand_forward/pallas_call | solution.py:797
  166.5 16.2 %ff_backward.2 = (f32[512,768]{1,0:T(8,128)}, bf16[4,384,512]{2,1,0:T(8,128)(2,1)}, bf16[4,384,512]{2,1,0:T(8,128)(2,1)}, bf16[4,96,512]{2,1,0:T(8,128)(2,1)}, b...) custom-call(s32[1]{0:T(128)} %bitcast.place_ref, bf16[512,768]{1,0:T(8,128)(2,1)} %get-tuple-element.492.grad_in, ...), custom_call_target="tpu_custom_call" | custom-call | flops 11000000 | bytes 1024 | tf_op jit(solution)/shard_map/ff_backward/pallas_call | solution.py:1030
  184.6 6.8 %owner_terms.5 = (bf16[2,384,384]{2,1,0:T(8,128)(2,1)}, bf16[2,384,384]{2,1,0:T(8,128)(2,1)}, bf16[2,384,384]{2,1,0:T(8,128)(2,1)}, bf16[2,384,384]{2,1,0:T(8,128)(2,1)}) custom-call(bf16[4,96,512]{2,1,0:T(8,128)(2,1)} %get-tuple-element.399.refs_0_, bf16[4,96,512]{2,1,0:T(8,128)(2,1)} %copy-done.62, ...), custom_call_target="tpu_custom_call" | custom-call | flops 11000000 | bytes 1024 | tf_op jit(solution)/shard_map/owner_terms/pallas_call | solution.py:1348
  194.1 16.9 %owner_terms.6 = (bf16[2,480,384]{2,1,0:T(8,128)(2,1)}, bf16[2,480,384]{2,1,0:T(8,128)(2,1)}, bf16[2,480,384]{2,1,0:T(8,128)(2,1)}, bf16[2,480,384]{2,1,0:T(8,128)(2,1)}) custom-call(bf16[4,384,512]{2,1,0:T(8,128)(2,1)} %get-tuple-element.526.refs_0_, bf16[4,384,512]{2,1,0:T(8,128)(2,1)} %copy-done.52, bf16[512,768]{1,0:T(8,128)(2,1)} %get-tuple-element.513.refs_2_, ...), custom_call_target="tpu_custom_call" | custom-call | flops 11000000 | bytes 1024 | tf_op jit(solution)/shard_map/owner_terms/pallas_call | solution.py:1348
  215.6 18.9 %attn_backward.2 = (f32[512,768]{1,0:T(8,128)}, bf16[3,4,96,512]{3,2,1,0:T(8,128)(2,1)}, bf16[3,4,96,512]{3,2,1,0:T(8,128)(2,1)}, f32[4,16,384]{2,1,0:T(8,128)},...) custom-call(s32[1]{0:T(128)} %bitcast.place_ref, ...), custom_call_target="tpu_custom_call" | custom-call | flops 11000000 | bytes 1024 | tf_op jit(solution)/shard_map/attn_backward/pallas_call | solution.py:1230
  237.0 3.9 collective-permute-start.46
  244.9 10.3 %owner_terms.7 = (bf16[2,688,384]{2,1,0:T(8,128)(2,1)}, bf16[2,672,384]{2,1,0:T(8,128)(2,1)}, bf16[2,688,384]{2,1,0:T(8,128)(2,1)}, bf16[2,672,384]{2,1,0:T(8,128)(2,1)}) custom-call(bf16[4,96,512]{2,1,0:T(8,128)(2,1)} %get-tuple-element.573.refs_0_, bf16[4,96,512]{2,1,0:T(8,128)(2,1)} %copy-done.61, ...), custom_call_target="tpu_custom_call" | custom-call | flops 11000000 | bytes 1024 | tf_op jit(solution)/shard_map/owner_terms/pallas_call | solution.py:1348
  263.2 16.2 %ff_backward.3 = (f32[512,768]{1,0:T(8,128)}, bf16[4,384,512]{2,1,0:T(8,128)(2,1)}, bf16[4,384,512]{2,1,0:T(8,128)(2,1)}, bf16[4,96,512]{2,1,0:T(8,128)(2,1)}, b...) custom-call(s32[1]{0:T(128)} %bitcast.place_ref, f32[512,768]{1,0:T(8,128)} %get-tuple-element.596.grad_in, ...), custom_call_target="tpu_custom_call" | custom-call | flops 11000000 | bytes 1024 | tf_op jit(solution)/shard_map/ff_backward/pallas_call | solution.py:1030
  290.0 8.5 %owner_terms.8 = (bf16[2,480,384]{2,1,0:T(8,128)(2,1)}, bf16[2,480,384]{2,1,0:T(8,128)(2,1)}, bf16[2,480,384]{2,1,0:T(8,128)(2,1)}, bf16[2,480,384]{2,1,0:T(8,128)(2,1)}) custom-call(bf16[4,384,512]{2,1,0:T(8,128)(2,1)} %get-tuple-element.614.refs_0_, bf16[4,384,512]{2,1,0:T(8,128)(2,1)} %collective-permute-done.59.refs_1_, ...), custom_call_target="tpu_custom_call" | custom-call | flops 11000000 | bytes 1024 | tf_op jit(solution)/shard_map/owner_terms/pallas_call | solution.py:1348
  301.5 5.8 %collective-permute-start.63 = (bf16[1360,384]{1,0:T(8,128)(2,1)S(1)}, bf16[1360,384]{1,0:T(8,128)(2,1)S(1)}, u32[]{:S(2)}, u32[]{:S(2)}) collective-permute-start(bf16[1360,384]{1,0:T(8,128)(2,1)S(1)} %ends.7.refs_0_), channel_id=1, source_target_pairs={{0,1},{3,2},{4,5},{7,6},{8,9},{11,10},{12,13},{15,14},{16,17},{19,... | collective-permute-start | bytes 3133448 | tf_op jit(solution)/shard_map/ppermute | solution.py:657
  312.0 17.5 %attn_backward.3 = (bf16[512,768]{1,0:T(8,128)(2,1)}, bf16[3,4,96,512]{3,2,1,0:T(8,128)(2,1)}, bf16[3,4,96,512]{3,2,1,0:T(8,128)(2,1)}, f32[4,16,384]{2,1,0:T(8,128)}, f32[4,16,384]{2,1,0:T(8,128)}) custom-call(s32[1]{0:T(128)} %bitcast.place_ref, f32[512,768]{1,0:T(8,128)} %get-tuple-element.637.grad_in, bf16[512,768]{1,0:T(8,128)(2,1)} %bitcast.10, ...), custom_call_target="tpu_custom_call" | custom-call | flops 11000000 | bytes 1024 | tf_op jit(solution)/shard_map/attn_backward/pallas_call | solution.py:1230
  329.5 10.3 %collective-permute-done.64.refs_1_ = bf16[768,384]{1,0:T(8,128)(2,1)S(1)} collective-permute-done((bf16[768,384]{1,0:T(8,128)(2,1)S(1)}, bf16[768,384]{1,0:T(8,128)(2,1)S(1)}, u32[]{:S(2)}, u32[]{:S(2)}) %collective-permute-start.64) | collective-permute-done | bytes 589856 | tf_op jit(solution)/shard_map/ppermute | solution.py:674
  348.2 5.6 %owner_terms.9 = (bf16[2,304,384]{2,1,0:T(8,128)(2,1)}, bf16[2,288,384]{2,1,0:T(8,128)(2,1)}, bf16[2,304,384]{2,1,0:T(8,128)(2,1)}, bf16[2,288,384]{2,1,0:T(8,128)(2,1)}) custom-call(bf16[3,4,96,512]{3,2,1,0:T(8,128)(2,1)} %get-tuple-element.653.refs_0_, bf16[3,4,96,512]{3,2,1,0:T(8,128)(2,1)} %collective-permute-done.68.refs_1_, ...), custom_call_target="tpu_custom_call" | custom-call | flops 11000000 | bytes 1024 | tf_op jit(solution)/shard_map/owner_terms/pallas_call | solution.py:1348
  358.5 4.0 collective-permute-start.75
  362.5 8.1 %reduce_forward.3 = bf16[512,768]{1,0:T(8,128)(2,1)} custom-call(s32[1]{0:T(128)} %bitcast.place_ref, s32[2,1]{1,0:T(2,128)} %copy.32.live_ref, f32[512,768]{1,0:T(8,128)} %get-tuple-element.666.middle_ref.middle_in, bf16[512,3072]{1,0:T(8,128)(2,1)} %get-tuple-element.667.refs_2_.active_ref, f32[8,768]{1,0:T(8,128)} %get-tuple-element.462.small_ref, ...), custom_call_target="tpu_custom_call" | custom-call | flops 11000000 | bytes 1024 | tf_op jit(solution)/shard_map/reduce_forward/pallas_call | solution.py:869
  379.3 4.8 %collective-permute-done.74.refs_1_ = bf16[288,384]{1,0:T(8,128)(2,1)S(1)} collective-permute-done((bf16[288,384]{1,0:T(8,128)(2,1)S(1)}, bf16[288,384]{1,0:T(8,128)(2,1)S(1)}, u32[]{:S(2)}, u32[]{:S(2)}) %collective-permute-start.74) | collective-permute-done | bytes 221216 | tf_op jit(solution)/shard_map/ppermute | solution.py:384
  385.1 6.3 %collective-permute-start.76 = (bf16[592,384]{1,0:T(8,128)(2,1)S(1)}, bf16[592,384]{1,0:T(8,128)(2,1)S(1)}, u32[]{:S(2)}, u32[]{:S(2)}) collective-permute-start(bf16[592,384]{1,0:T(8,128)(2,1)S(1)} %ends.9.refs_0_), channel_id=1, source_target_pairs={{0,1},{3,2},{4,5},{7,6},{8,9},{11,10},{12,13},{15,14},{16,17},{19,... | collective-permute-start | bytes 1363976 | tf_op jit(solution)/shard_map/ppermute | solution.py:657
  391.4 6.1 %collective-permute-done.76.refs_1_ = bf16[592,384]{1,0:T(8,128)(2,1)S(1)} collective-permute-done((bf16[592,384]{1,0:T(8,128)(2,1)S(1)}, bf16[592,384]{1,0:T(8,128)(2,1)S(1)}, u32[]{:S(2)}, u32[]{:S(2)}) %collective-permute-start.76) | collective-permute-done | bytes 454688 | tf_op jit(solution)/shard_map/ppermute | solution.py:657
  409.3 15.4 %collective-permute-done.81.outward = bf16[960,384]{1,0:T(8,128)(2,1)} collective-permute-done((bf16[960,384]{1,0:T(8,128)(2,1)S(1)}, bf16[960,384]{1,0:T(8,128)(2,1)}, u32[]{:S(2)}, u32[]{:S(2)}) %collective-permute-start.81) | collective-permute-done | bytes 737312 | tf_op jit(solution)/shard_map/ppermute | solution.py:674
  429.6 2.8 finish_heads.1
  (324 shorter events, 129.2 us)
Async XLA Ops:
  26.4 34.9 %collective-permute-start.10 = (bf16[976,768]{1,0:T(8,128)(2,1)S(1)}, bf16[976,768]{1,0:T(8,128)(2,1)S(1)}, u32[]{:S(2)}, u32[]{:S(2)}) collective-permute-start(bf16[976,768]{1,0:T(8,128)(2,1)S(1)} %get-tuple-element.395), channel_id=1, source_target_pairs={{0,16},{4,20},{8,24},{12,28},{16,0},{20,4},{24,8},{28,12},{1,17},{... | collective-permute-start | bytes 4497416 | tf_op jit(solution)/shard_map/ppermute | solution.py:388
  27.0 34.1 %collective-permute-start.9 = (bf16[960,768]{1,0:T(8,128)(2,1)S(1)}, bf16[960,768]{1,0:T(8,128)(2,1)}, u32[]{:S(2)}, u32[]{:S(2)}) collective-permute-start(bf16[960,768]{1,0:T(8,128)(2,1)S(1)} %get-tuple-element.394), channel_id=1, source_target_pairs={{0,8},{4,12},{8,0},{12,4},{16,24},{20,28},{24,16},{28,20},{1,9},{5... | collective-permute-start | bytes 4423688 | tf_op jit(solution)/shard_map/ppermute | solution.py:384
  64.6 28.8 %collective-permute-start.14 = (bf16[784,768]{1,0:T(8,128)(2,1)}, bf16[784,768]{1,0:T(8,128)(2,1)S(1)}, u32[]{:S(2)}, u32[]{:S(2)}) collective-permute-start(bf16[784,768]{1,0:T(8,128)(2,1)} %get-tuple-element.412), channel_id=1, source_target_pairs={{0,8},{4,12},{8,0},{12,4},{16,24},{20,28},{24,16},{28,20},{1,9},{5... | collective-permute-start | bytes 3612680 | tf_op jit(solution)/shard_map/ppermute | solution.py:384
  66.2 28.4 %collective-permute-start.15 = (bf16[784,768]{1,0:T(8,128)(2,1)}, bf16[784,768]{1,0:T(8,128)(2,1)S(1)}, u32[]{:S(2)}, u32[]{:S(2)}) collective-permute-start(bf16[784,768]{1,0:T(8,128)(2,1)} %get-tuple-element.413), channel_id=1, source_target_pairs={{0,16},{4,20},{8,24},{12,28},{16,0},{20,4},{24,8},{28,12},{1,17},{... | collective-permute-start | bytes 3612680 | tf_op jit(solution)/shard_map/ppermute | solution.py:388
  96.5 23.4 %collective-permute-start.19 = (bf16[592,768]{1,0:T(8,128)(2,1)S(1)}, bf16[592,768]{1,0:T(8,128)(2,1)S(1)}, u32[]{:S(2)}, u32[]{:S(2)}) collective-permute-start(bf16[592,768]{1,0:T(8,128)(2,1)S(1)} %get-tuple-element.432), channel_id=1, source_target_pairs={{0,16},{4,20},{8,24},{12,28},{16,0},{20,4},{24,8},{28,12},{1,17},{... | collective-permute-start | bytes 2727944 | tf_op jit(solution)/shard_map/ppermute | solution.py:388
  98.0 21.9 %collective-permute-start.18 = (bf16[576,768]{1,0:T(8,128)(2,1)}, bf16[576,768]{1,0:T(8,128)(2,1)}, u32[]{:S(2)}, u32[]{:S(2)}) collective-permute-start(bf16[576,768]{1,0:T(8,128)(2,1)} %get-tuple-element.431), channel_id=1, source_target_pairs={{0,8},{4,12},{8,0},{12,4},{16,24},{20,28},{24,16},{28,20},{1,9},{5... | collective-permute-start | bytes 2654216 | tf_op jit(solution)/shard_map/ppermute | solution.py:384
  98.5 21.3 %collective-permute-start.20 = (bf16[512,768]{1,0:T(8,128)(2,1)}, bf16[512,768]{1,0:T(8,128)(2,1)}, u32[]{:S(2)}, u32[]{:S(2)}) collective-permute-start(bf16[512,768]{1,0:T(8,128)(2,1)} %get-tuple-element.440.refs_2_), channel_id=1, source_target_pairs={{0,4},{4,0},{8,12},{12,8},{16,20},{20,16},{24,28},{28,24},{1,5},{5... | collective-permute-start | bytes 2359304 | tf_op jit(solution)/shard_map/ppermute | solution.py:380
  100.2 19.6 %collective-permute-start.21 = (bf16[512,768]{1,0:T(8,128)(2,1)}, bf16[512,768]{1,0:T(8,128)(2,1)S(1)}, u32[]{:S(2)}, u32[]{:S(2)}) collective-permute-start(bf16[512,768]{1,0:T(8,128)(2,1)} %get-tuple-element.441.refs_6_.mixed_in), channel_id=1, source_target_pairs={{0,4},{4,0},{8,12},{12,8},{16,20},{20,16},{24,28},{28,24},{1,5},{5... | collective-permute-start | bytes 2359304 | tf_op jit(solution)/shard_map/ppermute | solution.py:380
  122.9 22.2 %collective-permute-start.24 = (bf16[576,768]{1,0:T(8,128)(2,1)}, bf16[576,768]{1,0:T(8,128)(2,1)S(1)}, u32[]{:S(2)}, u32[]{:S(2)}) collective-permute-start(bf16[576,768]{1,0:T(8,128)(2,1)} %get-tuple-element.449), channel_id=1, source_target_pairs={{0,8},{4,12},{8,0},{12,4},{16,24},{20,28},{24,16},{28,20},{1,9},{5... | collective-permute-start | bytes 2654216 | tf_op jit(solution)/shard_map/ppermute | solution.py:384
  124.1 21.6 %collective-permute-start.25 = (bf16[576,768]{1,0:T(8,128)(2,1)}, bf16[576,768]{1,0:T(8,128)(2,1)S(1)}, u32[]{:S(2)}, u32[]{:S(2)}) collective-permute-start(bf16[576,768]{1,0:T(8,128)(2,1)} %get-tuple-element.450), channel_id=1, source_target_pairs={{0,16},{4,20},{8,24},{12,28},{16,0},{20,4},{24,8},{28,12},{1,17},{... | collective-permute-start | bytes 2654216 | tf_op jit(solution)/shard_map/ppermute | solution.py:388
  191.5 19.5 %collective-permute-start.39 = (bf16[2,384,384]{2,1,0:T(8,128)(2,1)}, bf16[2,384,384]{2,1,0:T(8,128)(2,1)S(1)}, u32[]{:S(2)}, u32[]{:S(2)}) collective-permute-start(bf16[2,384,384]{2,1,0:T(8,128)(2,1)} %get-tuple-element.522), channel_id=1, source_target_pairs={{0,8},{4,12},{8,0},{12,4},{16,24},{20,28},{24,16},{28,20},{1,9},{5... | collective-permute-start | bytes 1769480 | tf_op jit(solution)/shard_map/ppermute | solution.py:384
  192.7 18.3 %collective-permute-start.40 = (bf16[2,384,384]{2,1,0:T(8,128)(2,1)}, bf16[2,384,384]{2,1,0:T(8,128)(2,1)S(1)}, u32[]{:S(2)}, u32[]{:S(2)}) collective-permute-start(bf16[2,384,384]{2,1,0:T(8,128)(2,1)} %get-tuple-element.523), channel_id=1, source_target_pairs={{0,16},{4,20},{8,24},{12,28},{16,0},{20,4},{24,8},{28,12},{1,17},{... | collective-permute-start | bytes 1769480 | tf_op jit(solution)/shard_map/ppermute | solution.py:388
  211.0 25.8 %collective-permute-start.45 = (bf16[512,3072]{1,0:T(8,128)(2,1)}, bf16[512,3072]{1,0:T(8,128)(2,1)}, u32[]{:S(2)}, u32[]{:S(2)}) collective-permute-start(bf16[512,3072]{1,0:T(8,128)(2,1)} %get-tuple-element.560.active_ref.refs_2_), channel_id=1, source_target_pairs={{0,4},{4,0},{8,12},{12,8},{16,20},{20,16},{24,28},{28,24},{1,5},{5... | collective-permute-start | bytes 9437192 | tf_op jit(solution)/shard_map/ppermute | solution.py:380
  211.1 25.7 %collective-permute-start.43 = (bf16[2,480,384]{2,1,0:T(8,128)(2,1)}, bf16[2,480,384]{2,1,0:T(8,128)(2,1)S(1)}, u32[]{:S(2)}, u32[]{:S(2)}) collective-permute-start(bf16[2,480,384]{2,1,0:T(8,128)(2,1)} %get-tuple-element.546), channel_id=1, source_target_pairs={{0,8},{4,12},{8,0},{12,4},{16,24},{20,28},{24,16},{28,20},{1,9},{5... | collective-permute-start | bytes 2211848 | tf_op jit(solution)/shard_map/ppermute | solution.py:384
  211.7 25.1 %collective-permute-start.44 = (bf16[2,480,384]{2,1,0:T(8,128)(2,1)}, bf16[2,480,384]{2,1,0:T(8,128)(2,1)S(1)}, u32[]{:S(2)}, u32[]{:S(2)}) collective-permute-start(bf16[2,480,384]{2,1,0:T(8,128)(2,1)} %get-tuple-element.547), channel_id=1, source_target_pairs={{0,16},{4,20},{8,24},{12,28},{16,0},{20,4},{24,8},{28,12},{1,17},{... | collective-permute-start | bytes 2211848 | tf_op jit(solution)/shard_map/ppermute | solution.py:388
  213.0 23.8 %collective-permute-start.41 = (bf16[384,384]{1,0:T(8,128)(2,1)S(1)}, bf16[384,384]{1,0:T(8,128)(2,1)S(1)}, u32[]{:S(2)}, u32[]{:S(2)}) collective-permute-start(bf16[384,384]{1,0:T(8,128)(2,1)S(1)} %get-tuple-element.542), channel_id=1, source_target_pairs={{0,16},{4,20},{8,24},{12,28},{16,0},{20,4},{24,8},{28,12},{1,17},{... | collective-permute-start | bytes 884744 | tf_op jit(solution)/shard_map/ppermute | solution.py:388
  214.1 22.7 %collective-permute-start.42 = (bf16[384,384]{1,0:T(8,128)(2,1)S(1)}, bf16[384,384]{1,0:T(8,128)(2,1)S(1)}, u32[]{:S(2)}, u32[]{:S(2)}) collective-permute-start(bf16[384,384]{1,0:T(8,128)(2,1)S(1)} %get-tuple-element.543), channel_id=1, source_target_pairs={{0,8},{4,12},{8,0},{12,4},{16,24},{20,28},{24,16},{28,20},{1,9},{5... | collective-permute-start | bytes 884744 | tf_op jit(solution)/shard_map/ppermute | solution.py:384
  237.0 18.9 %collective-permute-start.46 = (bf16[768,384]{1,0:T(8,128)(2,1)S(1)}, bf16[768,384]{1,0:T(8,128)(2,1)S(1)}, u32[]{:S(2)}, u32[]{:S(2)}) collective-permute-start(bf16[768,384]{1,0:T(8,128)(2,1)S(1)} %ends.5.refs_0_), channel_id=1, source_target_pairs={{0,1},{3,2},{4,5},{7,6},{8,9},{11,10},{12,13},{15,14},{16,17},{19,... | collective-permute-start | bytes 1769480 | tf_op jit(solution)/shard_map/ppermute | solution.py:657
  256.7 25.5 %collective-permute-start.52 = (bf16[2,688,384]{2,1,0:T(8,128)(2,1)}, bf16[2,688,384]{2,1,0:T(8,128)(2,1)S(1)}, u32[]{:S(2)}, u32[]{:S(2)}) collective-permute-start(bf16[2,688,384]{2,1,0:T(8,128)(2,1)} %get-tuple-element.586), channel_id=1, source_target_pairs={{0,8},{4,12},{8,0},{12,4},{16,24},{20,28},{24,16},{28,20},{1,9},{5... | collective-permute-start | bytes 3170312 | tf_op jit(solution)/shard_map/ppermute | solution.py:384
  257.6 24.7 %collective-permute-start.53 = (bf16[2,672,384]{2,1,0:T(8,128)(2,1)}, bf16[2,672,384]{2,1,0:T(8,128)(2,1)S(1)}, u32[]{:S(2)}, u32[]{:S(2)}) collective-permute-start(bf16[2,672,384]{2,1,0:T(8,128)(2,1)} %get-tuple-element.587), channel_id=1, source_target_pairs={{0,16},{4,20},{8,24},{12,28},{16,0},{20,4},{24,8},{28,12},{1,17},{... | collective-permute-start | bytes 3096584 | tf_op jit(solution)/shard_map/ppermute | solution.py:388
  259.8 20.4 %collective-permute-start.54 = (bf16[960,384]{1,0:T(8,128)(2,1)S(1)}, bf16[960,384]{1,0:T(8,128)(2,1)S(1)}, u32[]{:S(2)}, u32[]{:S(2)}) collective-permute-start(bf16[960,384]{1,0:T(8,128)(2,1)S(1)} %ends.6.refs_0_), channel_id=1, source_target_pairs={{0,1},{3,2},{4,5},{7,6},{8,9},{11,10},{12,13},{15,14},{16,17},{19,... | collective-permute-start | bytes 2211848 | tf_op jit(solution)/shard_map/ppermute | solution.py:657
  282.4 17.9 %collective-permute-start.58 = (bf16[960,384]{1,0:T(8,128)(2,1)S(1)}, bf16[960,384]{1,0:T(8,128)(2,1)S(1)}, u32[]{:S(2)}, u32[]{:S(2)}) collective-permute-start(bf16[960,384]{1,0:T(8,128)(2,1)S(1)} %plus.11.refs_0_), channel_id=1, source_target_pairs={{1,2},{2,1},{5,6},{6,5},{9,10},{10,9},{13,14},{14,13},{17,18},{18,... | collective-permute-start | bytes 2211848 | tf_op jit(solution)/shard_map/ppermute | solution.py:669
  301.5 40.0 %collective-permute-start.63 = (bf16[1360,384]{1,0:T(8,128)(2,1)S(1)}, bf16[1360,384]{1,0:T(8,128)(2,1)S(1)}, u32[]{:S(2)}, u32[]{:S(2)}) collective-permute-start(bf16[1360,384]{1,0:T(8,128)(2,1)S(1)} %ends.7.refs_0_), channel_id=1, source_target_pairs={{0,1},{3,2},{4,5},{7,6},{8,9},{11,10},{12,13},{15,14},{16,17},{19,... | collective-permute-start | bytes 3133448 | tf_op jit(solution)/shard_map/ppermute | solution.py:657
  307.5 33.2 %collective-permute-start.65 = (bf16[960,384]{1,0:T(8,128)(2,1)S(1)}, bf16[960,384]{1,0:T(8,128)(2,1)S(1)}, u32[]{:S(2)}, u32[]{:S(2)}) collective-permute-start(bf16[960,384]{1,0:T(8,128)(2,1)S(1)} %plus.13.refs_2_), channel_id=1, source_target_pairs={{1,0},{2,3},{5,4},{6,7},{9,8},{10,11},{13,12},{14,15},{17,16},{18,... | collective-permute-start | bytes 2211848 | tf_op jit(solution)/shard_map/ppermute | solution.py:674
  308.8 32.8 %collective-permute-start.61 = (bf16[2,480,384]{2,1,0:T(8,128)(2,1)}, bf16[2,480,384]{2,1,0:T(8,128)(2,1)}, u32[]{:S(2)}, u32[]{:S(2)}) collective-permute-start(bf16[2,480,384]{2,1,0:T(8,128)(2,1)} %get-tuple-element.625), channel_id=1, source_target_pairs={{0,8},{4,12},{8,0},{12,4},{16,24},{20,28},{24,16},{28,20},{1,9},{5... | collective-permute-start | bytes 2211848 | tf_op jit(solution)/shard_map/ppermute | solution.py:384
  309.7 31.9 %collective-permute-start.62 = (bf16[2,480,384]{2,1,0:T(8,128)(2,1)}, bf16[2,480,384]{2,1,0:T(8,128)(2,1)}, u32[]{:S(2)}, u32[]{:S(2)}) collective-permute-start(bf16[2,480,384]{2,1,0:T(8,128)(2,1)} %get-tuple-element.626), channel_id=1, source_target_pairs={{0,16},{4,20},{8,24},{12,28},{16,0},{20,4},{24,8},{28,12},{1,17},{... | collective-permute-start | bytes 2211848 | tf_op jit(solution)/shard_map/ppermute | solution.py:388
  310.5 29.4 %collective-permute-start.64 = (bf16[768,384]{1,0:T(8,128)(2,1)S(1)}, bf16[768,384]{1,0:T(8,128)(2,1)S(1)}, u32[]{:S(2)}, u32[]{:S(2)}) collective-permute-start(bf16[768,384]{1,0:T(8,128)(2,1)S(1)} %plus.12.refs_0_), channel_id=1, source_target_pairs={{1,0},{2,3},{5,4},{6,7},{9,8},{10,11},{13,12},{14,15},{17,16},{18,... | collective-permute-start | bytes 1769480 | tf_op jit(solution)/shard_map/ppermute | solution.py:674
  341.9 28.7 %collective-permute-start.72 = (bf16[1360,384]{1,0:T(8,128)(2,1)S(1)}, bf16[1360,384]{1,0:T(8,128)(2,1)S(1)}, u32[]{:S(2)}, u32[]{:S(2)}) collective-permute-start(bf16[1360,384]{1,0:T(8,128)(2,1)S(1)} %plus.14.refs_0_), channel_id=1, source_target_pairs={{1,2},{2,1},{5,6},{6,5},{9,10},{10,9},{13,14},{14,13},{17,18},{18,... | collective-permute-start | bytes 3133448 | tf_op jit(solution)/shard_map/ppermute | solution.py:669
  358.5 25.6 %collective-permute-start.75 = (bf16[960,384]{1,0:T(8,128)(2,1)S(1)}, bf16[960,384]{1,0:T(8,128)(2,1)S(1)}, u32[]{:S(2)}, u32[]{:S(2)}) collective-permute-start(bf16[960,384]{1,0:T(8,128)(2,1)S(1)} %ends.8.refs_0_), channel_id=1, source_target_pairs={{0,1},{3,2},{4,5},{7,6},{8,9},{11,10},{12,13},{15,14},{16,17},{19,... | collective-permute-start | bytes 2211848 | tf_op jit(solution)/shard_map/ppermute | solution.py:657
  373.8 25.1 %collective-permute-start.77 = (bf16[1360,384]{1,0:T(8,128)(2,1)S(1)}, bf16[1360,384]{1,0:T(8,128)(2,1)S(1)}, u32[]{:S(2)}, u32[]{:S(2)}) collective-permute-start(bf16[1360,384]{1,0:T(8,128)(2,1)S(1)} %plus.15.refs_4_), channel_id=1, source_target_pairs={{1,0},{2,3},{5,4},{6,7},{9,8},{10,11},{13,12},{14,15},{17,16},{18,... | collective-permute-start | bytes 3133448 | tf_op jit(solution)/shard_map/ppermute | solution.py:674
  400.0 24.8 %collective-permute-start.81 = (bf16[960,384]{1,0:T(8,128)(2,1)S(1)}, bf16[960,384]{1,0:T(8,128)(2,1)}, u32[]{:S(2)}, u32[]{:S(2)}) collective-permute-start(bf16[960,384]{1,0:T(8,128)(2,1)S(1)} %plus.19.total), channel_id=1, source_target_pairs={{1,0},{2,3},{5,4},{6,7},{9,8},{10,11},{13,12},{14,15},{17,16},{18,... | collective-permute-start | bytes 2211848 | tf_op jit(solution)/shard_map/ppermute | solution.py:674
  402.2 27.4 %collective-permute-start.80 = (bf16[592,384]{1,0:T(8,128)(2,1)}, bf16[592,384]{1,0:T(8,128)(2,1)}, u32[]{:S(2)}, u32[]{:S(2)}) collective-permute-start(bf16[592,384]{1,0:T(8,128)(2,1)} %plus.18.total), channel_id=1, source_target_pairs={{1,0},{2,3},{5,4},{6,7},{9,8},{10,11},{13,12},{14,15},{17,16},{18,... | collective-permute-start | bytes 1363976 | tf_op jit(solution)/shard_map/ppermute | solution.py:674
  (121 other events, 852.2 us)
